TPU v7x, 128 devices: a whole 4x4x4 slice. The times are simulated.
128 devices in a mesh: round: 2 (over core), head: 2 (over x_hi), seq: 32 (over y, x_lo, z).
Axes of the slice: x: 4 (x_hi: 2, x_lo: 2; x = x_hi * 2 + x_lo), y: 4, z: 4, core: 2. Of those that a mesh axis runs over, the one named last changes fastest.
Arguments:
- tokens: bfloat16 [32768, 1024], P(('round', 'head', 'seq')), may hold values from -48 to 48
- w_qk: bfloat16 [1024, 1024], replicated, may hold values from -0.375 to 0.375
- w_v: bfloat16 [1024, 1024], replicated, may hold values from -0.1875 to 0.1875
- w_out: bfloat16 [1024, 1024], replicated, may hold values from -0.375 to 0.375
- positions: int32 [2, 32768], P(None, ('round', 'head', 'seq')), may hold values from 0 to 32767, as said below
- buckets: int32 [2, 32768], P('round', 'seq'), may hold values from 0 to 1022, as said below
Outputs:
- layer_out: bfloat16 [32768, 1024], P(('round', 'head', 'seq'))
Inputs may be any that keep to these rules, and one draw needn't show every extreme that they name: Each row is a permutation: every sorted position appears once. Of the 256 tokens of one device, at most 14 have positions of one round in one range of 1024 sorted positions starting at a multiple of 1024. `buckets`: along each row the bucket numbers never fall, except that the last run of positions carries bucket 0 again: the bucket of the first positions continues around the end of the row.
All inputs are finite; a program needn't handle non-finite values.
Results may differ from a plain program's by a relative error of at most 0.022.
Values may be sent and summed in bfloat16 or wider, within the bound.
No kernel may reach another device: no remote copies, remote signals or barrier semaphores. Data moves between devices by JAX's collectives and lax.ppermute only.
A program may use at most 64 MiB of HBM per device.

v0:
```python
import jax
import jax.numpy as jnp
from jax import lax
from jax.sharding import PartitionSpec as P

DH = 128
BLOCK = 1024


SELF_PENALTY = -100000.0
BUCKET_PENALTY = -1000000000.0
EPSILON = 1e-06


def from_behind(block, axis, distance):
    devices = range(lax.axis_size(axis))
    route = [((i - distance) % len(devices), i) for i in devices]
    return lax.ppermute(block, axis, route)


def key_scaling(rows):
    feature_len = rows.shape[-1]
    squares = jnp.mean(jnp.square(rows.astype(jnp.float32)), axis=-1)
    return lax.rsqrt(squares + EPSILON) * feature_len ** (-0.5)


def attend(queries, key_rows, values, scaling, query_bucket, key_bucket):
    block_len = queries.shape[0]
    products = lax.dot_general(
        queries, key_rows, (((1,), (1,)), ((), ())), preferred_element_type=jnp.float32
    )
    scores = products * scaling[None, :]
    row_index = jnp.arange(block_len, dtype=jnp.int32)[:, None]
    col_index = jnp.arange(2 * block_len, dtype=jnp.int32)[None, :]
    matching = query_bucket[:, None] == key_bucket[None, :]
    scores = jnp.where(
        col_index == row_index + block_len,
        SELF_PENALTY,
        jnp.where(matching, scores, BUCKET_PENALTY),
    )
    maximum = jnp.max(scores, axis=1, keepdims=True)
    powers = jnp.exp(scores - maximum)
    totals = jnp.sum(powers, axis=1, keepdims=True)
    weights = (powers / totals).astype(jnp.bfloat16)
    result = jnp.dot(weights, values, preferred_element_type=jnp.float32).astype(jnp.bfloat16)
    return (result, maximum[:, 0] + jnp.log(totals[:, 0]))


def shards(tokens, w_qk, w_v, w_out, positions, buckets):
    tok_dev, model_width = tokens.shape
    rounds = positions.shape[0]
    head_count = w_qk.shape[1] // DH
    head_groups = lax.axis_size("head")
    head_dev = head_count // head_groups
    owners = lax.axis_size("seq")
    all_devices = lax.axis_size("round") * head_groups * owners
    owner_len = buckets.shape[1]
    share_len = tok_dev // owners
    capacity = share_len + share_len // 2 + share_len // 4
    features = 2 * DH
    row_width = head_dev * features
    joined_weight = jnp.concatenate(
        [w_qk.reshape(model_width, head_count, DH), w_v.reshape(model_width, head_count, DH)],
        axis=2,
    ).reshape(model_width, head_count * features)
    projected = (
        jnp.dot(tokens, joined_weight, preferred_element_type=jnp.float32)
        .astype(jnp.bfloat16)
        .reshape(tok_dev, head_groups, row_width)
    )
    destination = positions // owner_len
    within = positions % owner_len
    owner_ids = jnp.arange(owners, dtype=jnp.int32)
    onehot = (destination[:, :, None] == owner_ids[None, None, :]).astype(jnp.int32)
    slot_index = jnp.sum(jnp.cumsum(onehot, axis=1) * onehot, axis=2) - 1
    round_ids = jnp.broadcast_to(jnp.arange(rounds, dtype=jnp.int32)[:, None], destination.shape)
    token_ids = jnp.broadcast_to(jnp.arange(tok_dev, dtype=jnp.int32)[None, :], destination.shape)
    slot_token = (
        jnp.full((rounds, owners, capacity), tok_dev, jnp.int32)
        .at[round_ids, destination, slot_index]
        .set(token_ids)
    )
    slot_place = (
        jnp.full((rounds, owners, capacity), owner_len, jnp.int32)
        .at[round_ids, destination, slot_index]
        .set(within)
    )
    padded = jnp.concatenate(
        [projected, jnp.zeros((1, head_groups, row_width), jnp.bfloat16)], axis=0
    )
    group_ids = jnp.arange(head_groups, dtype=jnp.int32)
    outgoing = padded[slot_token[:, None, :, :], group_ids[None, :, None, None]]
    out_place = jnp.broadcast_to(slot_place[:, None], (rounds, head_groups, owners, capacity))
    arrived, arrived_place = (
        lax.all_to_all(
            outgoing.reshape(all_devices, capacity, row_width),
            ("round", "head", "seq"),
            split_axis=0,
            concat_axis=0,
            tiled=True,
        ),
        lax.all_to_all(
            out_place.reshape(all_devices, capacity),
            ("round", "head", "seq"),
            split_axis=0,
            concat_axis=0,
            tiled=True,
        ),
    )
    arrived = arrived.reshape(-1, row_width)
    arrived_place = arrived_place.reshape(-1)
    ordered = (
        jnp.zeros((owner_len, row_width), jnp.bfloat16).at[arrived_place].set(arrived, mode="drop")
    )
    own_bucket = buckets[0]
    before, before_bucket = from_behind((ordered, own_bucket), "seq", 1)
    head_rows = jnp.transpose(ordered.reshape(owner_len, head_dev, features), (1, 0, 2))
    head_before = jnp.transpose(before.reshape(BLOCK, head_dev, features), (1, 0, 2))
    block_count = owner_len // BLOCK

    def one_head(pair):
        rows, prior = pair
        own_scale = key_scaling(rows[:, :DH])
        before_scale = key_scaling(prior[:, :DH])
        rows_joined = jnp.concatenate([prior, rows], axis=0)
        scale_joined = jnp.concatenate([before_scale, own_scale], axis=0)
        bucket_joined = jnp.concatenate([before_bucket, own_bucket], axis=0)

        def block_step(block_index):
            return attend(
                rows[:, :DH],
                rows_joined[:, :DH],
                rows_joined[:, DH:],
                scale_joined,
                own_bucket,
                bucket_joined,
            )

        block_out, block_sum = lax.map(block_step, jnp.arange(block_count, dtype=jnp.int32))
        return (block_out.reshape(owner_len, DH), block_sum.reshape(owner_len))

    results, sums = lax.map(one_head, (head_rows, head_before))
    flat_out = jnp.transpose(results, (1, 0, 2)).reshape(owner_len, head_dev * DH)
    flat_sum = jnp.transpose(sums, (1, 0))
    padded_out = jnp.concatenate([flat_out, jnp.zeros((1, head_dev * DH), jnp.bfloat16)], axis=0)
    padded_sum = jnp.concatenate([flat_sum, jnp.zeros((1, head_dev), jnp.float32)], axis=0)
    back_rows = padded_out[arrived_place].reshape(all_devices, capacity, head_dev * DH)
    back_sums = padded_sum[arrived_place].reshape(all_devices, capacity, head_dev)
    returned, returned_sum = (
        lax.all_to_all(
            back_rows, ("round", "head", "seq"), split_axis=0, concat_axis=0, tiled=True
        ),
        lax.all_to_all(
            back_sums.astype(jnp.bfloat16),
            ("round", "head", "seq"),
            split_axis=0,
            concat_axis=0,
            tiled=True,
        ).astype(back_sums.dtype),
    )
    returned = returned.reshape(rounds, head_groups, owners, capacity, head_dev, DH)
    returned_sum = returned_sum.reshape(rounds, head_groups, owners, capacity, head_dev)
    round_select = jnp.arange(rounds, dtype=jnp.int32)[:, None, None]
    group_select = group_ids[None, :, None]
    per_round = returned[
        round_select, group_select, destination[:, None, :], slot_index[:, None, :]
    ]
    per_sum = returned_sum[
        round_select, group_select, destination[:, None, :], slot_index[:, None, :]
    ]
    largest = jnp.max(per_sum, axis=0, keepdims=True)
    shares = jnp.exp(per_sum - largest)
    combined = (
        jnp.sum(shares[..., None] * per_round.astype(jnp.float32), axis=0)
        / jnp.sum(shares, axis=0)[..., None]
    ).astype(jnp.bfloat16)
    out_weight = w_out.reshape(head_groups, head_dev, DH, model_width)
    return jnp.einsum(
        "gtjf,gjfd->td", combined, out_weight, preferred_element_type=jnp.float32
    ).astype(jnp.bfloat16)


def solution(mesh):
    in_specs = (
        P(("round", "head", "seq"), None),
        P(),
        P(),
        P(),
        P(None, ("round", "head", "seq")),
        P("round", "seq"),
    )
    out_specs = P(("round", "head", "seq"), None)
    return jax.shard_map(shards, mesh=mesh, in_specs=in_specs, out_specs=out_specs, check_vma=False)
```

profile of v0, /device:TPU:1, one launch (start us, length us, event | category | flops | bytes accessed | tf_op | source)
XLA Modules:
  0.0 407.0 jit_solution(9329618217813699931)
XLA Ops:
  3.1 29.9 %scatter_fusion = s32[2,32,14]{1,0,2:T(2,128)S(1)} fusion(s32[2,32,14]{1,0,2:T(2,128)S(1)} %broadcast_in_dim.73, s32[512]{0:T(512)S(1)} %bitcast.108, s32[512]{0:T(512)S(1)} %bitcast.130), kind=kCustom, calls=%fused_computation.5 | custom fusion | bytes 12288 | tf_op jit(solution)/shard_map/scatter | solution.py:86
  33.7 11.5 %all-to-all-start = ((s32[128,1,14]{2,1,0:T(1,128)}), s32[128,1,14]{2,1,0:T(1,128)S(1)}, u32[]{:S(2)}, u32[]{:S(2)}) async-start(s32[128,1,14]{2,1,0:T(1,128)} %bitcast.10), calls=%async_computation | async-start | bytes 131072 | tf_op jit(solution)/shard_map/all_to_all | solution.py:102
  45.2 29.9 %scatter_fusion.1 = s32[2,32,14]{1,0,2:T(2,128)S(1)} fusion(s32[2,32,14]{1,0,2:T(2,128)S(1)} %broadcast_in_dim.77, s32[512]{0:T(512)S(1)} %bitcast.109, s32[512]{0:T(512)S(1)} %bitcast.129), kind=kCustom, calls=%fused_computation.6 | custom fusion | bytes 12288 | tf_op jit(solution)/shard_map/scatter | solution.py:81
  85.9 18.4 %gather_fusion = bf16[1792,1024]{1,0:T(8,128)(2,1)} fusion(bf16[257,2,1024]{2,1,0:T(2,128)(2,1)S(1)} %concatenate.41, s32[1792]{0:T(1024)S(1)} %reshape.236), kind=kCustom, calls=%fused_computation | custom fusion | bytes 7354368 | tf_op jit(solution)/shard_map/gather | solution.py:92
  104.3 6.4 %reshape.224 = bf16[128,14,1024]{2,1,0:T(8,128)(2,1)} reshape(bf16[1792,1024]{1,0:T(8,128)(2,1)} %gather_fusion) | data formatting | bytes 7340032 | tf_op jit(solution)/shard_map/reshape | solution.py:96
  110.6 10.2 %all-to-all-start.1 = ((bf16[128,14,1024]{2,1,0:T(8,128)(2,1)}), bf16[128,14,1024]{2,1,0:T(8,128)(2,1)}, u32[]{:S(2)}, u32[]{:S(2)}) async-start(bf16[128,14,1024]{2,1,0:T(8,128)(2,1)} %reshape.224), calls=%async_computation.1 | async-start | bytes 8388608 | tf_op jit(solution)/shard_map/all_to_all | solution.py:95
  122.4 52.5 %all-to-all-done.1 = bf16[128,14,1024]{2,1,0:T(8,128)(2,1)} async-done(((bf16[128,14,1024]{2,1,0:T(8,128)(2,1)}), bf16[128,14,1024]{2,1,0:T(8,128)(2,1)}, u32[]{:S(2)}, u32[]{:S(2)}) %all-to-all-start.1) | async-done | bytes 3670048 | tf_op jit(solution)/shard_map/all_to_all | solution.py:95
  175.0 6.4 %reshape.286 = bf16[1792,1024]{1,0:T(8,128)(2,1)} reshape(bf16[128,14,1024]{2,1,0:T(8,128)(2,1)} %all-to-all-done.1) | data formatting | bytes 7340032 | tf_op jit(solution)/shard_map/reshape | solution.py:110
  181.4 12.9 %scatter_custom_fusion.2 = bf16[1024,1024]{1,0:T(8,128)(2,1)} fusion(s32[1792]{0:T(1024)S(1)} %get-tuple-element.152, bf16[1792,1024]{1,0:T(8,128)(2,1)} %reshape.286, bf16[]{:T(256)} %constant.135.clone.1), kind=kCustom, calls=%fused_computation.41 | custom fusion | bytes 2097664 | tf_op jit(solution)/shard_map/scatter | solution.py:113
  196.8 48.8 %collective-permute-done = s32[1024]{0:T(1024)S(1)} collective-permute-done((s32[1024]{0:T(1024)S(1)}, s32[1024]{0:T(1024)S(1)}, u32[]{:S(2)}, u32[]{:S(2)}) %collective-permute-start) | collective-permute-done | bytes 4128 | tf_op jit(solution)/shard_map/ppermute | solution.py:18
  245.6 3.9 copy.58
  249.6 3.9 copy.59
  253.5 64.4 %while.14 = (s32[]{:T(128)}, bf16[4,1024,128]{2,1,0:T(8,128)(2,1)}, bf16[4,1024]{1,0:T(4,128)(2,1)S(1)}, s32[1,1024]{1,0:T(1,128)S(1)}, s32[2048]{0:T(1024)S(1)}...) while((s32[]{:T(128)}, bf16[4,1024,128]{2,1,0:T(8,128)(2,1)}, ...), condition=%wide.region_11.12_spmd, body=%wide.region_6.11_spmd.sunk | while | flops 1099831296 | bytes 68268704 | solution.py:142
  257.4 3.3 fusion.38
  264.0 5.6 %fusion.40 = bf16[4,1024,128]{2,1,0:T(8,128)(2,1)} fusion(bf16[4,1024,128]{2,1,0:T(8,128)(2,1)} %get-tuple-element.235, s32[]{:T(128)} %get-tuple-element.234, f32[1024,2048]{1,0:T(8,128)} %copy-done.1, f32[1024]{0:T(1024)S(1)} %fusion.39, f32[1024]{0:T(1024)S(1)} %get-tuple-element.224, bf16[1024,256]{1,0:T(8,128)(2,1)S(1)} %bitcast.112, ...), kind=kOutput, calls=%fused_computation.16.clone.1 | convolution fusion | flops 544342016 | bytes 9708032 | tf_op jit(solution)/shard_map/while/body/eval_jaxpr/while/body/eval_jaxpr/dot_general | solution.py:45
  273.5 3.3 fusion.38
  280.1 5.6 %fusion.40 = bf16[4,1024,128]{2,1,0:T(8,128)(2,1)} fusion(bf16[4,1024,128]{2,1,0:T(8,128)(2,1)} %get-tuple-element.235, s32[]{:T(128)} %get-tuple-element.234, f32[1024,2048]{1,0:T(8,128)} %copy-done.1, f32[1024]{0:T(1024)S(1)} %fusion.39, f32[1024]{0:T(1024)S(1)} %get-tuple-element.224, bf16[1024,256]{1,0:T(8,128)(2,1)S(1)} %bitcast.112, ...), kind=kOutput, calls=%fused_computation.16.clone.1 | convolution fusion | flops 544342016 | bytes 9708032 | tf_op jit(solution)/shard_map/while/body/eval_jaxpr/while/body/eval_jaxpr/dot_general | solution.py:45
  289.6 3.3 fusion.38
  296.2 5.6 %fusion.40 = bf16[4,1024,128]{2,1,0:T(8,128)(2,1)} fusion(bf16[4,1024,128]{2,1,0:T(8,128)(2,1)} %get-tuple-element.235, s32[]{:T(128)} %get-tuple-element.234, f32[1024,2048]{1,0:T(8,128)} %copy-done.1, f32[1024]{0:T(1024)S(1)} %fusion.39, f32[1024]{0:T(1024)S(1)} %get-tuple-element.224, bf16[1024,256]{1,0:T(8,128)(2,1)S(1)} %bitcast.112, ...), kind=kOutput, calls=%fused_computation.16.clone.1 | convolution fusion | flops 544342016 | bytes 9708032 | tf_op jit(solution)/shard_map/while/body/eval_jaxpr/while/body/eval_jaxpr/dot_general | solution.py:45
  305.7 3.3 fusion.38
  312.3 5.6 %fusion.40 = bf16[4,1024,128]{2,1,0:T(8,128)(2,1)} fusion(bf16[4,1024,128]{2,1,0:T(8,128)(2,1)} %get-tuple-element.235, s32[]{:T(128)} %get-tuple-element.234, f32[1024,2048]{1,0:T(8,128)} %copy-done.1, f32[1024]{0:T(1024)S(1)} %fusion.39, f32[1024]{0:T(1024)S(1)} %get-tuple-element.224, bf16[1024,256]{1,0:T(8,128)(2,1)S(1)} %bitcast.112, ...), kind=kOutput, calls=%fused_computation.16.clone.1 | convolution fusion | flops 544342016 | bytes 9708032 | tf_op jit(solution)/shard_map/while/body/eval_jaxpr/while/body/eval_jaxpr/dot_general | solution.py:45
  318.2 3.7 gather_fusion.1
  323.2 5.5 %all-to-all-start.2 = ((bf16[128,14,4]{1,2,0:T(4,128)(2,1)}), bf16[128,14,4]{1,2,0:T(4,128)(2,1)S(1)}, u32[]{:S(2)}, u32[]{:S(2)}) async-start(bf16[128,14,4]{1,2,0:T(4,128)(2,1)} %copy.64), calls=%async_computation.2 | async-start | bytes 262144 | tf_op jit(solution)/shard_map/all_to_all | solution.py:153
  330.1 6.1 %gather_fusion.3 = bf16[1792,512]{1,0:T(8,128)(2,1)} fusion(bf16[1025,512]{1,0:T(8,128)(2,1)S(1)} %concatenate.45, s32[2048]{0:T(1024)S(1)} %pad_clamp_fusion), kind=kCustom, calls=%fused_computation.3 | custom fusion | bytes 3677184 | tf_op jit(solution)/shard_map/gather | solution.py:147
  336.2 3.8 reshape.231
  340.1 10.2 %all-to-all-start.3 = ((bf16[128,14,512]{2,1,0:T(8,128)(2,1)}), bf16[128,14,512]{2,1,0:T(8,128)(2,1)}, u32[]{:S(2)}, u32[]{:S(2)}) async-start(bf16[128,14,512]{2,1,0:T(8,128)(2,1)} %reshape.231), calls=%async_computation.3 | async-start | bytes 4194304 | tf_op jit(solution)/shard_map/all_to_all | solution.py:150
  351.1 10.0 %gather_fusion.2 = f32[1024,4]{1,0:T(8,128)S(1)} fusion(f32[2,2,32,14,4]{4,2,3,1,0:T(8,128)S(1)} %copy.66, s32[1024]{0:T(1024)S(1)} %bitcast.106), kind=kCustom, calls=%fused_computation.2 | custom fusion | bytes 49152 | tf_op jit(solution)/shard_map/gather | solution.py:168
  361.3 18.5 %all-to-all-done.3 = bf16[128,14,512]{2,1,0:T(8,128)(2,1)} async-done(((bf16[128,14,512]{2,1,0:T(8,128)(2,1)}), bf16[128,14,512]{2,1,0:T(8,128)(2,1)}, u32[]{:S(2)}, u32[]{:S(2)}) %all-to-all-start.3) | async-done | bytes 1835040 | tf_op jit(solution)/shard_map/all_to_all | solution.py:150
  379.9 4.4 %reshape.293 = bf16[2,2,32,14,4,128]{5,4,3,2,1,0:T(4,128)(2,1)} reshape(bf16[128,14,512]{2,1,0:T(8,128)(2,1)} %all-to-all-done.3) | data formatting | bytes 3670016 | tf_op jit(solution)/shard_map/reshape | solution.py:161
  384.2 3.8 copy.71
  388.0 12.6 %gather_fusion.4 = bf16[1024,4,128]{2,1,0:T(4,128)(2,1)} fusion(bf16[2,2,32,14,4,128]{5,4,2,1,0,3:T(4,128)(2,1)} %copy.71, s32[1024]{0:T(1024)S(1)} %bitcast.107), kind=kCustom, calls=%fused_computation.4 | custom fusion | bytes 2113536 | tf_op jit(solution)/shard_map/gather | solution.py:165
  400.6 4.2 %fusion.11 = f32[2,256,4,128]{3,2,1,0:T(4,128)S(1)} fusion(bf16[2,2,256,4,128]{4,3,2,1,0:T(4,128)(2,1)} %bitcast.123, f32[2,2,256,4]{3,2,1,0:T(8,128)S(1)} %subtract_exponential_fusion.1), kind=kLoop, calls=%fused_computation.37 | loop fusion | flops 1310720 | bytes 2113536 | tf_op jit(solution)/shard_map/reduce_sum | solution.py:174
  (137 shorter events, 53.1 us)
Async XLA Ops:
  0.0 405.5 %copy-start = (bf16[1024,1024]{1,0:T(8,128)(2,1)S(1)}, bf16[1024,1024]{1,0:T(8,128)(2,1)}, u32[]{:S(2)}) copy-start(bf16[1024,1024]{1,0:T(8,128)(2,1)} %param.11) | copy-start | bytes 6291460
  3.0 72.1 %copy-start.4 = (s32[2,256]{1,0:T(2,128)}, s32[2,256]{1,0:T(2,128)S(1)}, u32[]{:S(2)}) copy-start(s32[2,256]{1,0:T(2,128)S(1)} %fusion.17) | copy-start | bytes 6148
  33.7 77.0 %all-to-all-start = ((s32[128,1,14]{2,1,0:T(1,128)}), s32[128,1,14]{2,1,0:T(1,128)S(1)}, u32[]{:S(2)}, u32[]{:S(2)}) async-start(s32[128,1,14]{2,1,0:T(1,128)} %bitcast.10), calls=%async_computation | async-start | bytes 131072 | tf_op jit(solution)/shard_map/all_to_all | solution.py:102
  75.2 2.4 copy-start.3
  78.7 1.5 copy-start.8
  110.6 64.3 %all-to-all-start.1 = ((bf16[128,14,1024]{2,1,0:T(8,128)(2,1)}), bf16[128,14,1024]{2,1,0:T(8,128)(2,1)}, u32[]{:S(2)}, u32[]{:S(2)}) async-start(bf16[128,14,1024]{2,1,0:T(8,128)(2,1)} %reshape.224), calls=%async_computation.1 | async-start | bytes 8388608 | tf_op jit(solution)/shard_map/all_to_all | solution.py:95
  122.4 74.4 %copy-start.7 = (s32[1,1024]{1,0:T(1,128)S(1)}, s32[1,1024]{1,0:T(1,128)}, u32[]{:S(2)}) copy-start(s32[1,1024]{1,0:T(1,128)} %param.13) | copy-start | bytes 12292
  194.3 55.3 %collective-permute-start.1 = (bf16[1024,1024]{1,0:T(8,128)(2,1)}, bf16[1024,1024]{1,0:T(8,128)(2,1)}, u32[]{:S(2)}, u32[]{:S(2)}) collective-permute-start(bf16[1024,1024]{1,0:T(8,128)(2,1)} %scatter_custom_fusion.2), channel_id=1, source_target_pairs={{31,0},{0,1},{1,2},{2,3},{3,4},{4,5},{5,6},{6,7},{7,8},{8,9},{9,10... | collective-permute-start | bytes 6291464 | tf_op jit(solution)/shard_map/ppermute | solution.py:18
  196.8 48.8 %collective-permute-start = (s32[1024]{0:T(1024)S(1)}, s32[1024]{0:T(1024)S(1)}, u32[]{:S(2)}, u32[]{:S(2)}) collective-permute-start(s32[1024]{0:T(1024)S(1)} %bitcast.131), channel_id=1, source_target_pairs={{31,0},{0,1},{1,2},{2,3},{3,4},{4,5},{5,6},{6,7},{7,8},{8,9},{9,10... | collective-permute-start | bytes 12296 | tf_op jit(solution)/shard_map/ppermute | solution.py:18
  260.8 3.2 copy-start.1
  260.8 3.3 copy-start.2
  276.9 3.2 copy-start.1
  276.9 3.3 copy-start.2
  292.9 3.2 copy-start.1
  293.0 3.3 copy-start.2
  309.1 3.2 copy-start.1
  309.1 3.3 copy-start.2
  323.2 16.9 %all-to-all-start.2 = ((bf16[128,14,4]{1,2,0:T(4,128)(2,1)}), bf16[128,14,4]{1,2,0:T(4,128)(2,1)S(1)}, u32[]{:S(2)}, u32[]{:S(2)}) async-start(bf16[128,14,4]{1,2,0:T(4,128)(2,1)} %copy.64), calls=%async_computation.2 | async-start | bytes 262144 | tf_op jit(solution)/shard_map/all_to_all | solution.py:153
  336.2 14.1 %copy-start.5 = (s32[2,256]{1,0:T(2,128)S(1)}, s32[2,256]{1,0:T(2,128)}, u32[]{:S(2)}) copy-start(s32[2,256]{1,0:T(2,128)} %copy-done.4) | copy-start | bytes 6148
  336.2 14.1 %copy-start.6 = (s32[2,256]{1,0:T(2,128)S(1)}, s32[2,256]{1,0:T(2,128)}, u32[]{:S(2)}) copy-start(s32[2,256]{1,0:T(2,128)} %get-tuple-element.167) | copy-start | bytes 6148
  340.1 39.8 %all-to-all-start.3 = ((bf16[128,14,512]{2,1,0:T(8,128)(2,1)}), bf16[128,14,512]{2,1,0:T(8,128)(2,1)}, u32[]{:S(2)}, u32[]{:S(2)}) async-start(bf16[128,14,512]{2,1,0:T(8,128)(2,1)} %reshape.231), calls=%async_computation.3 | async-start | bytes 4194304 | tf_op jit(solution)/shard_map/all_to_all | solution.py:150
where the time goes:
time: 409 us; the launch traced here: 407 us
  local copies, waits for them, and re-layouts  188 us (46%)
  waiting for transfers between devices  120 us (29%)
  starting transfers between devices  40 us (10%)
  matrix products  38.5 us (9%)
  other arithmetic  19.8 us (5%)
    all_to_all x1, waiting for transfers between devices, shards(): lax.all_to_all(outgoing.reshape(all_devices, capacity, row_width), ('roun...  52.5 us
    ppermute x2, waiting for transfers between devices, from_behind(): return lax.ppermute(block, axis, route)  48.8 us
    scatter x2, local copies, waits for them, and re-layouts, shards(): slot_place = jnp.full((rounds, owners, capacity), owner_len, jnp.int32).a...  30 us
    scatter x1, local copies, waits for them, and re-layouts, shards(): slot_token = jnp.full((rounds, owners, capacity), tok_dev, jnp.int32).at[...  29.9 us
    dot_general x4, matrix products, attend(): jnp.dot(weights, values, preferred_element_type=jnp.float32)  22.3 us
    all_to_all x1, waiting for transfers between devices, shards(): lax.all_to_all(back_rows, ('round', 'head', 'seq'), split_axis=0, concat_...  18.5 us
    gather x1, local copies, waits for them, and re-layouts, shards(): outgoing = padded[slot_token[:, None, :, :], group_ids[None, :, None, None]]  18.4 us
    scatter x2, local copies, waits for them, and re-layouts, shards(): jnp.zeros((owner_len, row_width), jnp.bfloat16).at[arrived_place]  16.8 us
  transfers between devices with their start and end apart: 6, of which 3 were waited for; matrix products, arithmetic and copies ran while one was open for 23% of the time, Pallas kernels for 0%

commit v1 on v0

v1 whole, which is shorter than its diff:
```python
import functools

import jax
import jax.numpy as jnp
from jax import lax
from jax.experimental import pallas as pl
from jax.experimental.pallas import tpu as pltpu
from jax.sharding import PartitionSpec as P

DH = 128
BLOCK = 1024
TILE = 128
SLOTS = 16
META = 14
SHIFT = 1024

SELF_PENALTY = -100000.0
BUCKET_PENALTY = -1000000000.0
EPSILON = 1e-06
LOWEST = -3.0e38

BF = jnp.bfloat16
F32 = jnp.float32
I32 = jnp.int32
NT = (((1,), (1,)), ((), ()))


def iota(shape, dim):
    return lax.broadcasted_iota(I32, shape, dim)


def mask(cond):
    return jnp.where(cond, 1.0, 0.0).astype(BF)


def mm(a, b):
    return jnp.dot(a, b, preferred_element_type=F32)


def mm_nt(a, b):
    return lax.dot_general(a, b, NT, preferred_element_type=F32)


def full(shape):
    return pl.BlockSpec(shape, lambda *_: (0,) * len(shape))


def slots_of(pos, owners):
    count = pos.shape[1]
    dest = pos >> 10
    hot = iota((owners, count), 0) == dest
    earlier = mask(iota((count, count), 0) < iota((count, count), 1))
    before = mm(mask(hot), earlier)
    rank = jnp.sum(jnp.where(hot, before, 0.0), axis=0, keepdims=True).astype(I32)
    return dest, hot, rank


def pack_kernel(tok_ref, pos_ref, out_ref, *, owners):
    count = tok_ref.shape[0]
    width = out_ref.shape[1]
    rows = owners * SLOTS
    tokens = tok_ref[...]
    for r in range(2):
        pos = pos_ref[r : r + 1, :]
        dest, hot, rank = slots_of(pos, owners)
        within = pos & (BLOCK - 1)
        slot = dest * SLOTS + rank
        body = mm(mask(iota((rows, count), 0) == slot), tokens)
        value = iota((128, count), 0)
        code = jnp.where((value & 1) == 0, (within >> 5) + 1, within & 31)
        code = jnp.where((value >> 1) == rank, code, 0).astype(F32).astype(BF)
        places = mm_nt(mask(hot), code).astype(BF)
        at_meta = mask(iota((rows, owners), 0) == iota((rows, owners), 1) * SLOTS + META)
        extra = mm(at_meta, places)
        for a in range(2):
            at = (a * 2 + r) * rows
            out_ref[at : at + rows, 0:128] = (
                body[:, a * width : a * width + 128] + extra
            ).astype(BF)
            out_ref[at : at + rows, 128:width] = body[
                :, a * width + 128 : (a + 1) * width
            ].astype(BF)


def meta_of(x_ref):
    rows = x_ref.shape[0]
    count = rows // SLOTS
    pick = mask(iota((count, rows), 1) == iota((count, rows), 0) * SLOTS + META)
    return mm(pick, x_ref[:, 0:128]).astype(BF)


def place_rows(meta):
    count = meta.shape[0]
    v, lane = iota((128, 128), 0), iota((128, 128), 1)
    j = lane & (SLOTS - 1)
    weight = jnp.where(v == 2 * j, 32.0, jnp.where(v == 2 * j + 1, 1.0, 0.0)).astype(BF)
    codes = mm(meta, weight)
    own = (iota((count, 128), 0) & 7) == (iota((count, 128), 1) >> 4)
    codes = jnp.where(own, codes, 0.0)
    return jnp.sum(codes.reshape(count // 8, 8, 128), axis=1)


def place_columns(meta, first, rows):
    count = meta.shape[0]
    slot = iota((rows, count), 0) + first
    source = mask((slot >> 4) == iota((rows, count), 1))
    values = mm(source, meta)
    lane = iota((rows, 128), 1)
    keep = (lane >> 1) == (iota((rows, 128), 0) & (SLOTS - 1))
    values = jnp.where(keep, values, 0.0).astype(BF)
    weight = jnp.where((iota((128, 128), 0) & 1) == 0, 32.0, 1.0).astype(BF)
    return mm(values, weight)


def sort_kernel(x_ref, low_ref, high_ref, meta_ref, code_ref):
    meta = meta_of(x_ref)
    meta_ref[...] = meta
    codes = place_rows(meta)
    code_ref[...] = codes
    chunks = codes.shape[0]
    half = low_ref.shape[0]
    step = 256

    def rows_at(start, out_ref, at):
        position = (iota((step, 128), 0) + start + 32).astype(F32)
        picks = [
            mask(position == jnp.broadcast_to(code_ref[q : q + 1, :], (step, 128)))
            for q in range(chunks)
        ]
        out_ref[pl.ds(at, step), :] = mm(jnp.concatenate(picks, axis=1), x_ref[...]).astype(BF)

    for t in range(half // step):
        rows_at(half + t * step, high_ref, t * step)
    for t in range(half // step):
        rows_at(t * step, low_ref, t * step)


def project(mine, other, wm, wo):
    return (mm(mine, wm) + mm(other, wo)).astype(BF)


def key_scales(keys):
    sq = jnp.square(keys.astype(F32))
    top = sq.astype(BF)
    rest = (sq - top.astype(F32)).astype(BF)
    ones = jnp.ones((8, DH), BF)
    total = mm_nt(ones, top) + mm_nt(ones, rest)
    return lax.rsqrt(total * (1.0 / DH) + EPSILON) * DH ** (-0.5)


def lse_lanes(tile, lse, head):
    top = lse.astype(BF).astype(F32)
    rest = lse - top
    lane = iota(tile.shape, 1) & 7
    return jnp.where(lane == 2 * head, top, jnp.where(lane == 2 * head + 1, rest, tile))


def masked(products, scale, query_label, key_label, self_at):
    cols = products.shape[1]
    match = jnp.concatenate(
        [query_label == key_label[:, c : c + TILE] for c in range(0, cols, TILE)], axis=1
    )
    scores = jnp.where(match, products * scale, BUCKET_PENALTY)
    diagonal = iota(products.shape, 1) - iota(products.shape, 0) == self_at
    return jnp.where(diagonal, SELF_PENALTY, scores)


def own_kernel(
    info_ref, lm_ref, hm_ref, lo_ref, ho_ref, wqm_ref, wqo_ref, wvm_ref, wvo_ref,
    row_ref, col_ref, q_ref, v_ref, scale_ref, out_ref, lse_ref,
):
    half = lm_ref.shape[0]
    heads = q_ref.shape[1] // DH
    for m_ref, o_ref, at in ((hm_ref, ho_ref, half), (lm_ref, lo_ref, 0)):
        mine, other = m_ref[...], o_ref[...]
        q_ref[at : at + half, :] = project(mine, other, wqm_ref[...], wqo_ref[...])
        v_ref[at : at + half, :] = project(mine, other, wvm_ref[...], wvo_ref[...])
    for h in range(heads):
        scale_ref[h * 8 : h * 8 + 8, :] = key_scales(q_ref[:, h * DH : (h + 1) * DH])
    tiles = BLOCK // TILE
    band = 3 * TILE

    @pl.loop(0, tiles)
    def _(i):
        at = pl.multiple_of(i * TILE, TILE)
        start = pl.multiple_of(jnp.clip(i - 1, 0, tiles - 3) * TILE, TILE)

        @pl.when(info_ref[2 + i] == 0)
        def _():
            query_label = col_ref[pl.ds(at, TILE), :]
            key_label = row_ref[0:1, pl.ds(start, band)]
            lse_tile = jnp.zeros((TILE, 128), F32)
            for h in range(heads):
                cols = slice(h * DH, (h + 1) * DH)
                products = mm_nt(q_ref[pl.ds(at, TILE), cols], q_ref[pl.ds(start, band), cols])
                scale = scale_ref[h * 8 : h * 8 + 1, pl.ds(start, band)]
                scores = masked(products, scale, query_label, key_label, at - start)
                top = jnp.max(scores, axis=1, keepdims=True)
                powers = jnp.exp(scores - top)
                total = jnp.sum(powers, axis=1, keepdims=True)
                result = mm(powers.astype(BF), v_ref[pl.ds(start, band), cols])
                out_ref[pl.ds(at, TILE), cols] = (result / total).astype(BF)
                lse_tile = lse_lanes(lse_tile, top + jnp.log(total), h)
            lse_ref[pl.ds(at, TILE), :] = lse_tile.astype(BF)

        @pl.when(info_ref[2 + i] != 0)
        def _():
            out_ref[pl.ds(at, TILE), :] = jnp.zeros((TILE, heads * DH), BF)
            lse_ref[pl.ds(at, TILE), :] = jnp.zeros((TILE, 128), BF)


def rest_kernel(
    info_ref, xm_ref, xo_ref, wqm_ref, wqo_ref, wvm_ref, wvo_ref, row_ref, col_ref,
    q_ref, v_ref, scale_ref, own_ref, own_lse_ref, meta_ref, send_ref,
    out_ref, lse_ref, pk_ref, pv_ref, ps_ref, m_ref, l_ref, acc_ref,
):
    halo = xm_ref.shape[0]
    heads = q_ref.shape[1] // DH
    tiles = BLOCK // TILE
    skipped = (BLOCK - halo) // TILE
    flags = 2 + tiles
    used = flags + tiles * 2 * tiles
    out_ref[...] = own_ref[...]
    lse_ref[...] = own_lse_ref[...]

    @pl.loop(0, halo // TILE)
    def _(t):
        @pl.when(info_ref[used + skipped + t] != 0)
        def _():
            at = pl.multiple_of(t * TILE, TILE)
            mine, other = xm_ref[pl.ds(at, TILE), :], xo_ref[pl.ds(at, TILE), :]
            keys = project(mine, other, wqm_ref[...], wqo_ref[...])
            pk_ref[pl.ds(at, TILE), :] = keys
            pv_ref[pl.ds(at, TILE), :] = project(mine, other, wvm_ref[...], wvo_ref[...])
            for h in range(heads):
                ps_ref[h * 8 : h * 8 + 8, pl.ds(at, TILE)] = key_scales(
                    keys[:, h * DH : (h + 1) * DH]
                )

    @pl.loop(0, tiles)
    def _(i):
        @pl.when(info_ref[2 + i] != 0)
        def _():
            at = pl.multiple_of(i * TILE, TILE)
            query_label = col_ref[pl.ds(at, TILE), :]
            m_ref[...] = jnp.full(m_ref.shape, LOWEST, F32)
            l_ref[...] = jnp.zeros(l_ref.shape, F32)
            acc_ref[...] = jnp.zeros(acc_ref.shape, F32)

            def add(keys_ref, values_ref, scales_ref, key_at, label_at, self_at):
                key_label = row_ref[0:1, pl.ds(label_at, TILE)]
                for h in range(heads):
                    cols = slice(h * DH, (h + 1) * DH)
                    products = mm_nt(
                        q_ref[pl.ds(at, TILE), cols], keys_ref[pl.ds(key_at, TILE), cols]
                    )
                    scale = scales_ref[h * 8 : h * 8 + 1, pl.ds(key_at, TILE)]
                    scores = masked(products, scale, query_label, key_label, self_at)
                    old = m_ref[:, cols]
                    top = jnp.maximum(old, jnp.max(scores, axis=1, keepdims=True))
                    powers = jnp.exp(scores - top)
                    shrink = jnp.exp(old - top)
                    m_ref[:, cols] = top
                    l_ref[:, cols] = l_ref[:, cols] * shrink + jnp.sum(
                        powers, axis=1, keepdims=True
                    )
                    acc_ref[:, cols] = acc_ref[:, cols] * shrink + mm(
                        powers.astype(BF), values_ref[pl.ds(key_at, TILE), cols]
                    )

            @pl.loop(0, halo // TILE)
            def _(t):
                @pl.when(info_ref[flags + i * 2 * tiles + skipped + t] != 0)
                def _():
                    add(
                        pk_ref, pv_ref, ps_ref, pl.multiple_of(t * TILE, TILE),
                        pl.multiple_of((skipped + t) * TILE, TILE), -4 * BLOCK,
                    )

            @pl.loop(0, tiles)
            def _(t):
                @pl.when(info_ref[flags + i * 2 * tiles + tiles + t] != 0)
                def _():
                    key_at = pl.multiple_of(t * TILE, TILE)
                    add(
                        q_ref, v_ref, scale_ref, key_at,
                        pl.multiple_of(BLOCK + t * TILE, TILE), at - key_at,
                    )

            lse_tile = jnp.zeros((TILE, 128), F32)
            for h in range(heads):
                cols = slice(h * DH, (h + 1) * DH)
                total = l_ref[:, cols]
                out_ref[pl.ds(at, TILE), cols] = (acc_ref[:, cols] / total).astype(BF)
                lse_tile = lse_lanes(lse_tile, m_ref[:, cols] + jnp.log(total), h)
            lse_ref[pl.ds(at, TILE), :] = lse_tile.astype(BF)

    step = 256

    @pl.loop(0, send_ref.shape[0] // step)
    def _(t):
        at = pl.multiple_of(t * step, step)
        codes = place_columns(meta_ref[...], at, step)
        lane = (iota((step, 128), 1) + 32).astype(F32)
        pick = jnp.concatenate(
            [mask(codes == lane + float(c)) for c in range(0, BLOCK, 128)], axis=1
        )
        body = mm(pick, out_ref[...])
        sums = mm(pick, lse_ref[...])
        row = iota((step, 128), 0) & (SLOTS - 1)
        sums = jnp.where(row == (iota((step, 128), 1) >> 3), sums, 0.0)
        sums = jnp.sum(sums.reshape(step // SLOTS, SLOTS, 128), axis=1, keepdims=True)
        sums = jnp.broadcast_to(sums, (step // SLOTS, SLOTS, 128)).reshape(step, 128)
        extra = jnp.where(row == META, sums, 0.0)
        send_ref[pl.ds(at, step), 0:128] = (body[:, 0:128] + extra).astype(BF)
        send_ref[pl.ds(at, step), 128:] = body[:, 128:].astype(BF)


def final_kernel(x_ref, pos_ref, w_ref, out_ref, *, owners):
    count = out_ref.shape[0]
    width = x_ref.shape[1]
    rows = owners * SLOTS
    heads = width // DH
    lane = iota((count, 128), 1)
    picks, meta_picks, ranks = [], [], []
    for r in range(2):
        dest, _, rank = slots_of(pos_ref[r : r + 1, :], owners)
        slot = (dest * SLOTS + rank).astype(F32)
        slot = jnp.transpose(jnp.broadcast_to(slot, (128, count))).astype(I32)
        place = slot & (SLOTS - 1)
        at_meta = slot - place + META
        picks.append(
            jnp.concatenate([mask(slot == lane + c) for c in range(0, rows, 128)], axis=1)
        )
        meta_picks.append(
            jnp.concatenate([mask(at_meta == lane + c) for c in range(0, rows, 128)], axis=1)
        )
        ranks.append(place)
    v = iota((128, width), 0) & 7
    select = mask((v >> 1) == (iota((128, width), 1) >> 7))
    total = None
    for a in range(2):
        values, sums = [], []
        for r in range(2):
            at = (a * 2 + r) * rows
            values.append(mm(picks[r], x_ref[at : at + rows, :]))
            own = mm(meta_picks[r], x_ref[at : at + rows, 0:128])
            own = jnp.where((lane >> 3) == ranks[r], own, 0.0).astype(BF)
            sums.append(mm(own, select))
        largest = jnp.maximum(sums[0], sums[1])
        first, second = jnp.exp(sums[0] - largest), jnp.exp(sums[1] - largest)
        combined = ((first * values[0] + second * values[1]) / (first + second)).astype(BF)
        part = mm(combined, w_ref[a * width : (a + 1) * width, :])
        total = part if total is None else total + part
    out_ref[...] = total.astype(BF)


def window_plan(own, prior):
    first = prior[0]
    own = jnp.where(own < first, own + SHIFT, own).reshape(-1, TILE)
    prior = jnp.where(prior < first, prior + SHIFT, prior).reshape(-1, TILE)
    keys = jnp.concatenate([prior, own], axis=0)
    low, high = jnp.min(keys, axis=1), jnp.max(keys, axis=1)
    tiles = own.shape[0]
    own_low, own_high = low[tiles:], high[tiles:]
    meets = (low[None, :] <= own_high[:, None]) & (high[None, :] >= own_low[:, None])
    tile = jnp.arange(tiles, dtype=I32)[:, None]
    key = jnp.arange(-tiles, tiles, dtype=I32)[None, :]
    start = jnp.clip(tile - 1, 0, tiles - 3)
    outside = jnp.any(meets & ((key < start) | (key > start + 2)), axis=1)
    return outside, meets


def shards(tokens, w_qk, w_v, w_out, positions, buckets):
    tok_dev, model_width = tokens.shape
    owners = lax.axis_size("seq")
    everyone = ("round", "head", "seq")
    total = 2 * 2 * owners
    width = model_width // 2
    heads = width // DH
    rows = total * SLOTS
    half = BLOCK // 2
    tiles = BLOCK // TILE
    core = lax.axis_index("round")
    my_round = lax.axis_index("head")
    block = lax.axis_index("seq")
    call = functools.partial(pl.pallas_call)
    params = pltpu.CompilerParams(vmem_limit_bytes=48 * 1024 * 1024)

    def shape(*dims, dtype=BF):
        return jax.ShapeDtypeStruct(dims, dtype)

    def swap(x):
        return lax.ppermute(x, "round", [(0, 1), (1, 0)])

    def onward(x):
        return lax.ppermute(x, "seq", [(i, (i + 1) % owners) for i in range(owners)])

    def exchange(x):
        x = x.reshape(total, SLOTS, width)
        x = lax.all_to_all(x, everyone, split_axis=0, concat_axis=0, tiled=True)
        return x.reshape(rows, width)

    packed = call(
        functools.partial(pack_kernel, owners=owners),
        out_shape=shape(rows, width),
        compiler_params=params,
        name="pack",
    )(tokens, positions)
    labels = lax.all_gather(buckets[0], ("round", "seq")).reshape(2, owners, BLOCK)
    arrived = exchange(packed)

    low, high, meta, _ = call(
        sort_kernel,
        out_shape=[
            shape(half, width),
            shape(half, width),
            shape(total, 128),
            shape(total // 8, 128, dtype=F32),
        ],
        compiler_params=params,
        name="sort_rows",
    )(arrived)
    halo_high = onward(high)
    low_other, high_other = swap(low), swap(high)

    before = jnp.roll(labels, 1, axis=1)
    first = before[:, :, :1]
    moved = jnp.where(labels < first, labels + SHIFT, labels)
    moved_before = jnp.where(before < first, before + SHIFT, before)
    wide = jnp.any(
        jnp.max(moved_before[:, :, :half], axis=2) >= jnp.min(moved, axis=2)
    )
    own_label = labels[my_round, block]
    prior_label = before[my_round, block]
    outside, meets = window_plan(own_label, prior_label)
    needed = jnp.any(meets[:, :tiles] & outside[:, None], axis=0)
    info = jnp.concatenate(
        [
            jnp.stack([core, 1 - core]).astype(I32),
            outside.astype(I32),
            meets.astype(I32).reshape(-1),
            needed.astype(I32),
        ]
    )
    label_row = jnp.concatenate([prior_label, own_label])[None, :]
    label_col = jnp.broadcast_to(own_label[:, None], (BLOCK, TILE))

    def weight(flip):
        return pl.BlockSpec((width, width), lambda i, s: (s[flip], s[0]))

    weights = [weight(0), weight(1), weight(0), weight(1)]
    weight_args = (w_qk, w_qk, w_v, w_v)
    halves = full((half, width))
    wide_rows = full((BLOCK, width))
    queries, values, scales, own_out, own_lse = call(
        own_kernel,
        out_shape=[
            shape(BLOCK, width),
            shape(BLOCK, width),
            shape(heads * 8, BLOCK, dtype=F32),
            shape(BLOCK, width),
            shape(BLOCK, 128),
        ],
        grid_spec=pltpu.PrefetchScalarGridSpec(
            num_scalar_prefetch=1,
            grid=(1,),
            in_specs=[halves] * 4 + weights + [full((1, BLOCK)), full((BLOCK, TILE))],
            out_specs=[
                wide_rows,
                wide_rows,
                full((heads * 8, BLOCK)),
                wide_rows,
                full((BLOCK, 128)),
            ],
        ),
        compiler_params=params,
        name="own_block",
    )(info, low, high, low_other, high_other, *weight_args, label_row[:, BLOCK:], label_col)

    def finish(halo_mine, halo_other):
        halo = halo_mine.shape[0]
        return call(
            rest_kernel,
            out_shape=shape(rows, width),
            grid_spec=pltpu.PrefetchScalarGridSpec(
                num_scalar_prefetch=1,
                grid=(1,),
                in_specs=[full((halo, width))] * 2
                + weights
                + [
                    full((1, 2 * BLOCK)),
                    full((BLOCK, TILE)),
                    wide_rows,
                    wide_rows,
                    full((heads * 8, BLOCK)),
                    wide_rows,
                    full((BLOCK, 128)),
                    full((total, 128)),
                ],
                out_specs=full((rows, width)),
                scratch_shapes=[
                    pltpu.VMEM((BLOCK, width), BF),
                    pltpu.VMEM((BLOCK, 128), BF),
                    pltpu.VMEM((halo, width), BF),
                    pltpu.VMEM((halo, width), BF),
                    pltpu.VMEM((heads * 8, halo), F32),
                    pltpu.VMEM((TILE, width), F32),
                    pltpu.VMEM((TILE, width), F32),
                    pltpu.VMEM((TILE, width), F32),
                ],
            ),
            compiler_params=params,
            name="prior_block",
        )(
            info, halo_mine, halo_other, *weight_args, label_row, label_col,
            queries, values, scales, own_out, own_lse, meta,
        )

    halo_high_other = swap(halo_high)

    def whole_window():
        halo_low = onward(low)
        return finish(
            jnp.concatenate([halo_low, halo_high], axis=0),
            jnp.concatenate([swap(halo_low), halo_high_other], axis=0),
        )

    back = lax.cond(wide, whole_window, lambda: finish(halo_high, halo_high_other))
    returned = exchange(back)
    return call(
        functools.partial(final_kernel, owners=owners),
        out_shape=shape(tok_dev, model_width),
        compiler_params=params,
        name="combine",
    )(returned, positions, w_out)


def solution(mesh):
    in_specs = (
        P(("round", "head", "seq"), None),
        P(),
        P(),
        P(),
        P(None, ("round", "head", "seq")),
        P("round", "seq"),
    )
    out_specs = P(("round", "head", "seq"), None)
    return jax.shard_map(shards, mesh=mesh, in_specs=in_specs, out_specs=out_specs, check_vma=False)
```

time: 409 us -> 285 us (0.70)
  blocking collectives: 0 us -> 196 us
  local copies, waits for them, and re-layouts: 188 us -> 4.41 us
  waiting for transfers between devices: 120 us -> 14.7 us
  Pallas kernels: 0 us -> 52.8 us
  matrix products: 38.5 us -> 0 us
  starting transfers between devices: 40 us -> 12.9 us
  other arithmetic: 19.8 us -> 3.11 us
    all_gather x0 -> x1, blocking collectives: none -> 161 us  [shards(): lax.all_gather(buckets[0], ('round', 'seq')).reshape(2, owners, BLOCK)]
    scatter x5 -> x0, local copies, waits for them, and re-layouts: 76.7 us -> none  [the longest x2 30 us: shards(): slot_place = jnp.full((rounds, owners, capacity), owner_len, jnp.int32).a...]
    all_to_all x4 -> x1, waiting for transfers between devices: 71.1 us -> 0.01 us  [exchange(): x = lax.all_to_all(x, everyone, split_axis=0, concat_axis=0, tiled=True)]
    pallas_call x0 -> x5, Pallas kernels: none -> 52.8 us  [the longest x1 33.1 us: finish(): call(rest_kernel, out_shape=shape(rows, width), grid_spec=pltpu.PrefetchS...]
    gather x5 -> x0, local copies, waits for them, and re-layouts: 50.9 us -> none  [the longest x1 18.4 us: shards(): outgoing = padded[slot_token[:, None, :, :], group_ids[None, :, None, None]]]
    dot_general x10 -> x0, matrix products: 38.5 us -> none  [the longest x4 22.3 us: attend(): jnp.dot(weights, values, preferred_element_type=jnp.float32)]
    all_to_all x0 -> x1, blocking collectives: none -> 34.1 us  [exchange(): x = lax.all_to_all(x, everyone, split_axis=0, concat_axis=0, tiled=True)]
    ppermute x2 -> x4, waiting for transfers between devices: 48.8 us -> 14.7 us  [the longest x1 14.7 us: onward(): lax.ppermute(x, 'seq', [(i, (i + 1) % owners) for i in range(owners)])]
  transfers between devices with their start and end apart: 6 -> 5, of which waited for: 3 -> 1; matrix products, arithmetic and copies ran while one was open for 23% -> 2% of each run, Pallas kernels for 0% -> 4%
where the time goes in v1:
time: 285 us; the launch traced here: 284 us
  blocking collectives  196 us (69%)
  Pallas kernels  52.8 us (19%)
  waiting for transfers between devices  14.7 us (5%)
  starting transfers between devices  12.9 us (5%)
  local copies, waits for them, and re-layouts  4.41 us (2%)
  other arithmetic  3.11 us (1%)
    all_gather x1, blocking collectives, shards(): lax.all_gather(buckets[0], ('round', 'seq')).reshape(2, owners, BLOCK)  161 us
    all_to_all x1, blocking collectives, exchange(): x = lax.all_to_all(x, everyone, split_axis=0, concat_axis=0, tiled=True)  34.1 us
    pallas_call x1, Pallas kernels, finish(): call(rest_kernel, out_shape=shape(rows, width), grid_spec=pltpu.PrefetchS...  33.1 us
    ppermute x1, waiting for transfers between devices, onward(): lax.ppermute(x, 'seq', [(i, (i + 1) % owners) for i in range(owners)])  14.7 us
    all_to_all x1, starting transfers between devices, exchange(): x = lax.all_to_all(x, everyone, split_axis=0, concat_axis=0, tiled=True)  11.5 us
    pallas_call x1, Pallas kernels, shards(): call(own_kernel, out_shape=[shape(BLOCK, width), shape(BLOCK, width), sha...  11.5 us
  transfers between devices with their start and end apart: 5, of which 1 were waited for; matrix products, arithmetic and copies ran while one was open for 2% of the time, Pallas kernels for 4%

profile of v1, /device:TPU:1, one launch (start us, length us, event | category | flops | bytes accessed | tf_op | source)
XLA Modules:
  0.0 284.3 jit_solution(1787811716039927702)
XLA Ops:
  0.0 1.0 copy-done.2
  1.0 0.7 copy-done.3
  1.7 1.2 pack.1
  3.0 1.3 copy-done
  4.3 11.5 %all-to-all-start = ((bf16[128,16,512]{2,1,0:T(8,128)(2,1)}), bf16[128,16,512]{2,1,0:T(8,128)(2,1)S(1)}, u32[]{:S(2)}, u32[]{:S(2)}) async-start(bf16[128,16,512]{2,1,0:T(8,128)(2,1)} %bitcast.18), calls=%async_computation | async-start | bytes 4194304 | tf_op jit(solution)/shard_map/all_to_all | solution.py:401
  15.8 161.4 %all-gather = s32[64,1,1024]{2,1,0:T(1,128)S(1)} all-gather(s32[1,1,1024]{2,1,0:T(1,128)S(1)} %bitcast.33), channel_id=1, replica_groups=mesh['round'=2,'head'=2,'seq'=32] {'round','seq'}, dimensions={0}, use_global_device_ids=true | all-gather | bytes 266240 | tf_op jit(solution)/shard_map/all_gather | solution.py:410
  177.3 0.1 fusion.4
  177.4 0.1 lt.57
  177.5 0.6 slice.45
  178.1 0.2 fusion
  178.3 0.1 reduce_min.21
  178.4 0.2 fusion.2
  178.6 0.7 compare_select_fusion.3
  179.3 3.5 %sort_rows.1 = (bf16[512,512]{1,0:T(8,128)(2,1)}, bf16[512,512]{1,0:T(8,128)(2,1)S(1)}, bf16[128,128]{1,0:T(8,128)(2,1)S(1)}, f32[16,128]{1,0:T(8,128)}) custom-call(bf16[2048,512]{1,0:T(8,128)(2,1)S(1)} %bitcast.17), custom_call_target="tpu_custom_call" | custom-call | tf_op jit(solution)/shard_map/sort_rows/pallas_call | solution.py:413
  182.8 0.7 compare_reduce_fusion
  184.2 0.7 compare_select_fusion.2
  184.9 0.1 fusion.6
  185.2 0.1 fusion.8
  185.3 0.1 reshape.63
  185.3 0.3 collective-permute-start.5
  185.7 0.2 collective-permute-start.4
  185.9 14.7 %collective-permute-done.2 = bf16[512,512]{1,0:T(8,128)(2,1)S(1)} collective-permute-done((bf16[512,512]{1,0:T(8,128)(2,1)S(1)}, bf16[512,512]{1,0:T(8,128)(2,1)S(1)}, u32[]{:S(2)}, u32[]{:S(2)}) %collective-permute-start.2) | collective-permute-done | bytes 524320 | tf_op jit(solution)/shard_map/ppermute | solution.py:397
  200.5 0.9 collective-permute-start.3
  201.4 0.2 and_reduce_fusion.1
  201.6 0.1 and_reduce_fusion
  201.7 0.1 concatenate.21.info_ref
  201.8 0.2 broadcast_in_dim.5.col_ref
  202.0 11.5 %own_block.1 = (bf16[1024,512]{1,0:T(8,128)(2,1)S(1)}, bf16[1024,512]{1,0:T(8,128)(2,1)S(1)}, f32[32,1024]{1,0:T(8,128)S(1)}, bf16[1024,512]{1,0:T(8,128)(2,1)S(1)}, bf16[1024,128]{1,0:T(8,128)(2,1)S(1)}) custom-call(s32[146]{0:T(256)S(1)} %concatenate.21.info_ref, bf16[512,512]{1,0:T(8,128)(2,1)} %get-tuple-element.98.lm_ref, ...), custom_call_target="tpu_custom_call" | custom-call | tf_op jit(solution)/shard_map/own_block/pallas_call | solution.py:456
  213.6 33.1 %conditional.1 = (bf16[2048,512]{1,0:T(8,128)(2,1)}) conditional(s32[]{:T(128)} %convert_element_type.16, (s32[146]{0:T(256)S(1)}, bf16[512,512]{1,0:T(8,128)(2,1)S(1)}, bf16[512,512]{1,0:T(8,128)(2,1)}, bf16[1024,1024]{1,0:T(8,128)(2,1)S(1)}, bf16[1024,1024]{1,0:T(8,128)(2,1)S(1)}, /*index=5*/s32[1,2048]{1,0:T(1,128)S(1)}, ...), branch_computations={%region_7.8_spmd, %region_8.9_spmd} | conditional | flops 4194304 | bytes 41943240 | solution.py:529
  213.6 33.1 %prior_block.2 = bf16[2048,512]{1,0:T(8,128)(2,1)} custom-call(s32[146]{0:T(256)S(1)} %get-tuple-element.62.info_ref, bf16[512,512]{1,0:T(8,128)(2,1)S(1)} %get-tuple-element.63.xm_ref, bf16[512,512]{1,0:T(8,128)(2,1)} %get-tuple-element.64.xo_ref, bf16[1024,1024]{1,0:T(8,128)(2,1)S(1)} %get-tuple-element.65.wqm_ref.wqo_ref, ...), custom_call_target="tpu_custom_call" | custom-call | tf_op jit(solution)/shard_map/cond/branch_0_fun/prior_block/pallas_call | solution.py:483
  246.7 34.1 %all_to_all.10 = bf16[128,16,512]{2,1,0:T(8,128)(2,1)S(1)} all-to-all(bf16[128,16,512]{2,1,0:T(8,128)(2,1)} %bitcast.11), channel_id=1, replica_groups=mesh['round'=2,'head'=2,'seq'=32] {'round','head','seq'}, dimensions={0} | all-to-all | bytes 4194304 | tf_op jit(solution)/shard_map/all_to_all | solution.py:401
  280.8 3.5 %combine.1 = bf16[256,1024]{1,0:T(8,128)(2,1)} custom-call(bf16[2048,512]{1,0:T(8,128)(2,1)S(1)} %bitcast.19, s32[2,256]{1,0:T(2,128)S(1)} %copy-done.4, bf16[1024,1024]{1,0:T(8,128)(2,1)S(1)} %copy-done.1), custom_call_target="tpu_custom_call" | custom-call | tf_op jit(solution)/shard_map/combine/pallas_call | solution.py:531
  (31 shorter events, 0.3 us)
Async XLA Ops:
  0.0 1.0 copy-start.2
  1.0 0.7 copy-start.3
  2.9 1.4 copy-start
  4.3 11.5 %copy-start.12 = (s32[1,1024]{1,0:T(1,128)S(1)}, s32[1,1024]{1,0:T(1,128)}, u32[]{:S(2)}) copy-start(s32[1,1024]{1,0:T(1,128)} %param.13) | copy-start | bytes 12292
  4.3 175.0 %all-to-all-start = ((bf16[128,16,512]{2,1,0:T(8,128)(2,1)}), bf16[128,16,512]{2,1,0:T(8,128)(2,1)S(1)}, u32[]{:S(2)}, u32[]{:S(2)}) async-start(bf16[128,16,512]{2,1,0:T(8,128)(2,1)} %bitcast.18), calls=%async_computation | async-start | bytes 4194304 | tf_op jit(solution)/shard_map/all_to_all | solution.py:401
  182.8 17.7 %collective-permute-start.2 = (bf16[512,512]{1,0:T(8,128)(2,1)S(1)}, bf16[512,512]{1,0:T(8,128)(2,1)S(1)}, u32[]{:S(2)}, u32[]{:S(2)}) collective-permute-start(bf16[512,512]{1,0:T(8,128)(2,1)S(1)} %get-tuple-element.97.hm_ref), channel_id=1, source_target_pairs={{0,1},{1,2},{2,3},{3,4},{4,5},{5,6},{6,7},{7,8},{8,9},{9,10},{10,1... | collective-permute-start | bytes 1572872 | tf_op jit(solution)/shard_map/ppermute | solution.py:397
  185.3 16.5 %collective-permute-start.5 = (bf16[512,512]{1,0:T(8,128)(2,1)S(1)}, bf16[512,512]{1,0:T(8,128)(2,1)S(1)}, u32[]{:S(2)}, u32[]{:S(2)}) collective-permute-start(bf16[512,512]{1,0:T(8,128)(2,1)S(1)} %get-tuple-element.97.hm_ref), channel_id=1, source_target_pairs={{0,64},{64,0},{1,65},{65,1},{2,66},{66,2},{3,67},{67,3},{4,68},{68... | collective-permute-start | bytes 1572872 | tf_op jit(solution)/shard_map/ppermute | solution.py:394
  185.7 16.1 %collective-permute-start.4 = (bf16[512,512]{1,0:T(8,128)(2,1)}, bf16[512,512]{1,0:T(8,128)(2,1)S(1)}, u32[]{:S(2)}, u32[]{:S(2)}) collective-permute-start(bf16[512,512]{1,0:T(8,128)(2,1)} %get-tuple-element.98.lm_ref), channel_id=1, source_target_pairs={{0,64},{64,0},{1,65},{65,1},{2,66},{66,2},{3,67},{67,3},{4,68},{68... | collective-permute-start | bytes 1572872 | tf_op jit(solution)/shard_map/ppermute | solution.py:394
  200.5 13.0 %collective-permute-start.3 = (bf16[512,512]{1,0:T(8,128)(2,1)S(1)}, bf16[512,512]{1,0:T(8,128)(2,1)}, u32[]{:S(2)}, u32[]{:S(2)}) collective-permute-start(bf16[512,512]{1,0:T(8,128)(2,1)S(1)} %collective-permute-done.2), channel_id=1, source_target_pairs={{0,64},{64,0},{1,65},{65,1},{2,66},{66,2},{3,67},{67,3},{4,68},{68... | collective-permute-start | bytes 1572872 | tf_op jit(solution)/shard_map/ppermute | solution.py:394
  202.0 11.5 %copy-start.5 = (bf16[1024,1024]{1,0:T(8,128)(2,1)S(1)}, bf16[1024,1024]{1,0:T(8,128)(2,1)}, u32[]{:S(2)}) copy-start(bf16[1024,1024]{1,0:T(8,128)(2,1)} %wqo_ref.1) | copy-start | bytes 6291460
  202.0 11.5 %copy-start.8 = (bf16[1024,1024]{1,0:T(8,128)(2,1)S(1)}, bf16[1024,1024]{1,0:T(8,128)(2,1)}, u32[]{:S(2)}) copy-start(bf16[1024,1024]{1,0:T(8,128)(2,1)} %wvo_ref.1) | copy-start | bytes 6291460
  202.0 11.5 %copy-start.11 = (bf16[512,512]{1,0:T(8,128)(2,1)S(1)}, bf16[512,512]{1,0:T(8,128)(2,1)}, u32[]{:S(2)}) copy-start(bf16[512,512]{1,0:T(8,128)(2,1)} %get-tuple-element.98.lm_ref) | copy-start | bytes 1572868
  246.7 34.1 %copy-start.1 = (bf16[1024,1024]{1,0:T(8,128)(2,1)S(1)}, bf16[1024,1024]{1,0:T(8,128)(2,1)}, u32[]{:S(2)}) copy-start(bf16[1024,1024]{1,0:T(8,128)(2,1)} %w_ref.1) | copy-start | bytes 6291460
  246.7 34.1 %copy-start.4 = (s32[2,256]{1,0:T(2,128)S(1)}, s32[2,256]{1,0:T(2,128)}, u32[]{:S(2)}) copy-start(s32[2,256]{1,0:T(2,128)} %pos_ref.3) | copy-start | bytes 6148

commit v2 on v1

v2 whole, which is shorter than its diff:
```python
import functools

import jax
import jax.numpy as jnp
from jax import lax
from jax.experimental import pallas as pl
from jax.experimental.pallas import tpu as pltpu
from jax.sharding import PartitionSpec as P

DH = 128
BLOCK = 1024
TILE = 128
SLOTS = 16
META = 14
SHIFT = 1024

SELF_PENALTY = -100000.0
BUCKET_PENALTY = -1000000000.0
EPSILON = 1e-06
LOWEST = -3.0e38

BF = jnp.bfloat16
F32 = jnp.float32
I32 = jnp.int32
NT = (((1,), (1,)), ((), ()))


def iota(shape, dim):
    return lax.broadcasted_iota(I32, shape, dim)


def mask(cond):
    return jnp.where(cond, 1.0, 0.0).astype(BF)


def mm(a, b):
    return jnp.dot(a, b, preferred_element_type=F32)


def mm_nt(a, b):
    return lax.dot_general(a, b, NT, preferred_element_type=F32)


def full(shape):
    return pl.BlockSpec(shape, lambda *_: (0,) * len(shape))


def slots_of(pos, owners):
    count = pos.shape[1]
    dest = pos >> 10
    hot = iota((owners, count), 0) == dest
    earlier = mask(iota((count, count), 0) < iota((count, count), 1))
    before = mm(mask(hot), earlier)
    rank = jnp.sum(jnp.where(hot, before, 0.0), axis=0, keepdims=True).astype(I32)
    return dest, hot, rank


def pack_kernel(tok_ref, pos_ref, label_ref, out_ref, *, owners):
    count = tok_ref.shape[0]
    width = out_ref.shape[1]
    rows = owners * SLOTS
    tokens = tok_ref[...]
    half = BLOCK // 2
    first, last = label_ref[0:1, 0:1], label_ref[0:1, BLOCK - 1 : BLOCK]
    middle = label_ref[0:1, half - 1 : half]
    marked = jnp.where(last == 0, jnp.minimum(first, middle), jnp.abs(middle - last))
    wide = jnp.where(jnp.broadcast_to(marked, (owners, 128)) == 0, 1.0, 0.0)
    for r in range(2):
        pos = pos_ref[r : r + 1, :]
        dest, hot, rank = slots_of(pos, owners)
        within = pos & (BLOCK - 1)
        slot = dest * SLOTS + rank
        body = mm(mask(iota((rows, count), 0) == slot), tokens)
        value = iota((128, count), 0)
        code = jnp.where((value & 1) == 0, (within >> 5) + 1, within & 31)
        code = jnp.where((value >> 1) == rank, code, 0).astype(F32).astype(BF)
        places = mm_nt(mask(hot), code)
        places = jnp.where(iota((owners, 128), 1) == 2 * SLOTS, wide, places).astype(BF)
        at_meta = mask(iota((rows, owners), 0) == iota((rows, owners), 1) * SLOTS + META)
        extra = mm(at_meta, places)
        for a in range(2):
            at = (a * 2 + r) * rows
            out_ref[at : at + rows, 0:128] = (
                body[:, a * width : a * width + 128] + extra
            ).astype(BF)
            out_ref[at : at + rows, 128:width] = body[
                :, a * width + 128 : (a + 1) * width
            ].astype(BF)


def meta_of(x_ref):
    rows = x_ref.shape[0]
    count = rows // SLOTS
    pick = mask(iota((count, rows), 1) == iota((count, rows), 0) * SLOTS + META)
    return mm(pick, x_ref[:, 0:128]).astype(BF)


def place_rows(meta):
    count = meta.shape[0]
    v, lane = iota((128, 128), 0), iota((128, 128), 1)
    j = lane & (SLOTS - 1)
    weight = jnp.where(v == 2 * j, 32.0, jnp.where(v == 2 * j + 1, 1.0, 0.0)).astype(BF)
    codes = mm(meta, weight)
    own = (iota((count, 128), 0) & 7) == (iota((count, 128), 1) >> 4)
    codes = jnp.where(own, codes, 0.0)
    return jnp.sum(codes.reshape(count // 8, 8, 128), axis=1)


def place_columns(meta, first, rows):
    count = meta.shape[0]
    slot = iota((rows, count), 0) + first
    source = mask((slot >> 4) == iota((rows, count), 1))
    values = mm(source, meta)
    lane = iota((rows, 128), 1)
    keep = (lane >> 1) == (iota((rows, 128), 0) & (SLOTS - 1))
    values = jnp.where(keep, values, 0.0).astype(BF)
    weight = jnp.where((iota((128, 128), 0) & 1) == 0, 32.0, 1.0).astype(BF)
    return mm(values, weight)


def sorted_rows(x_ref, code_ref, out_ref, first):
    step = 256
    chunks = code_ref.shape[0]
    for start in range(0, out_ref.shape[0], step):
        position = (iota((step, 128), 0) + (first + start + 32)).astype(F32)
        picks = [
            mask(position == jnp.broadcast_to(code_ref[q : q + 1, :], (step, 128)))
            for q in range(chunks)
        ]
        picks = jnp.concatenate(picks, axis=1)
        out_ref[start : start + step, :] = mm(picks, x_ref[...]).astype(BF)


def sort_high_kernel(x_ref, high_ref, meta_ref, code_ref, wide_ref):
    meta = meta_of(x_ref)
    meta_ref[...] = meta
    flags = jnp.where(iota(meta.shape, 1) == 2 * SLOTS, meta.astype(F32), 0.0)
    wide_ref[...] = jnp.max(jnp.max(flags, axis=1, keepdims=True), axis=0, keepdims=True)
    code_ref[...] = place_rows(meta)
    sorted_rows(x_ref, code_ref, high_ref, high_ref.shape[0])


def sort_low_kernel(x_ref, code_ref, low_ref):
    sorted_rows(x_ref, code_ref, low_ref, 0)


def project(mine, other, wm, wo):
    return (mm(mine, wm) + mm(other, wo)).astype(BF)


def project_t(mine, other, wm_t, wo_t):
    return (mm_nt(wm_t, mine) + mm_nt(wo_t, other)).astype(BF)


def key_scales(keys):
    sq = jnp.square(keys.astype(F32))
    top = sq.astype(BF)
    rest = (sq - top.astype(F32)).astype(BF)
    total = mm(jnp.concatenate([top, rest], axis=1), jnp.ones((2 * DH, 128), BF))
    return lax.rsqrt(total * (1.0 / DH) + EPSILON) * DH ** (-0.5)


def score_tile(keys, queries, scale, key_label, query_label, diagonal):
    scores = jnp.where(key_label == query_label, mm_nt(keys, queries) * scale, BUCKET_PENALTY)
    if diagonal is None:
        return scores
    cut = scores[diagonal : diagonal + TILE]
    cut = jnp.where(iota((TILE, TILE), 0) == iota((TILE, TILE), 1), SELF_PENALTY, cut)
    parts = [scores[:diagonal]] * (diagonal > 0) + [cut]
    parts += [scores[diagonal + TILE :]] * (diagonal + TILE < scores.shape[0])
    return jnp.concatenate(parts, axis=0) if len(parts) > 1 else cut


def soft(scores, values_t):
    top = jnp.max(scores, axis=0, keepdims=True)
    powers = jnp.exp(scores - top)
    total = jnp.sum(powers, axis=0, keepdims=True)
    return mm(values_t, powers.astype(BF)), top, total


def own_kernel(
    info_ref, lm_ref, hm_ref, lo_ref, ho_ref, wqm_ref, wqo_ref, wvm_ref, wvo_ref,
    row_ref, col_ref, q_ref, out_ref, lse_ref, vt_ref, scale_ref, m_ref, l_ref, acc_ref,
):
    half = lm_ref.shape[0]
    heads = q_ref.shape[1] // DH
    wvm, wvo = jnp.transpose(wvm_ref[...]), jnp.transpose(wvo_ref[...])
    for m_part, o_part, at in ((hm_ref, ho_ref, half), (lm_ref, lo_ref, 0)):
        mine, other = m_part[...], o_part[...]
        keys = project(mine, other, wqm_ref[...], wqo_ref[...])
        q_ref[at : at + half, :] = keys
        for h in range(heads):
            cols = slice(h * DH, (h + 1) * DH)
            scale_ref[at : at + half, cols] = key_scales(keys[:, cols])
        vt_ref[:, at : at + half] = project_t(mine, other, wvm, wvo)
    tiles = BLOCK // TILE
    lse_row = iota((8, TILE), 0)

    def put(at, h, result, total, lse_tile, top):
        out_ref[h * DH : (h + 1) * DH, pl.ds(at, TILE)] = (result * (1.0 / total)).astype(BF)
        return jnp.where(lse_row == h, top + jnp.log(total), lse_tile)

    def band(at, start, size, diagonal):
        query_label = row_ref[0:1, pl.ds(at, TILE)]
        key_label = col_ref[pl.ds(start, size), :]
        lse_tile = jnp.zeros((8, TILE), F32)
        for h in range(heads):
            cols = slice(h * DH, (h + 1) * DH)
            scores = score_tile(
                q_ref[pl.ds(start, size), cols], q_ref[pl.ds(at, TILE), cols],
                scale_ref[pl.ds(start, size), cols], key_label, query_label, diagonal,
            )
            result, top, total = soft(scores, vt_ref[cols, pl.ds(start, size)])
            lse_tile = put(at, h, result, total, lse_tile, top)
        lse_ref[:, pl.ds(at, TILE)] = lse_tile

    @pl.when(info_ref[2] == 0)
    def _():
        band(0, 0, 2 * TILE, 0)

    @pl.loop(1, tiles - 1)
    def _(i):
        @pl.when(info_ref[2 + i] == 0)
        def _():
            at = pl.multiple_of(i * TILE, TILE)
            band(at, pl.multiple_of(at - TILE, TILE), 3 * TILE, TILE)

    @pl.when(info_ref[1 + tiles] == 0)
    def _():
        band(BLOCK - TILE, BLOCK - 2 * TILE, 2 * TILE, TILE)

    @pl.loop(0, tiles)
    def _(i):
        @pl.when(info_ref[2 + i] != 0)
        def _():
            at = pl.multiple_of(i * TILE, TILE)
            query_label = row_ref[0:1, pl.ds(at, TILE)]
            m_ref[...] = jnp.full(m_ref.shape, LOWEST, F32)
            l_ref[...] = jnp.zeros(l_ref.shape, F32)
            acc_ref[...] = jnp.zeros(acc_ref.shape, F32)

            @pl.loop(0, tiles)
            def _(t):
                @pl.when(info_ref[2 + tiles + i * tiles + t] != 0)
                def _():
                    start = pl.multiple_of(t * TILE, TILE)
                    key_label = col_ref[pl.ds(start, TILE), :]
                    apart = iota((TILE, TILE), 0) - iota((TILE, TILE), 1)
                    for h in range(heads):
                        cols = slice(h * DH, (h + 1) * DH)
                        scores = score_tile(
                            q_ref[pl.ds(start, TILE), cols], q_ref[pl.ds(at, TILE), cols],
                            scale_ref[pl.ds(start, TILE), cols], key_label, query_label, None,
                        )
                        scores = jnp.where(apart == at - start, SELF_PENALTY, scores)
                        old = m_ref[h : h + 1, :]
                        top = jnp.maximum(old, jnp.max(scores, axis=0, keepdims=True))
                        powers = jnp.exp(scores - top)
                        shrink = jnp.exp(old - top)
                        m_ref[h : h + 1, :] = top
                        l_ref[h : h + 1, :] = l_ref[h : h + 1, :] * shrink + jnp.sum(
                            powers, axis=0, keepdims=True
                        )
                        acc_ref[cols, :] = acc_ref[cols, :] * shrink + mm(
                            vt_ref[cols, pl.ds(start, TILE)], powers.astype(BF)
                        )

            lse_tile = jnp.zeros((8, TILE), F32)
            for h in range(heads):
                lse_tile = put(
                    at, h, acc_ref[h * DH : (h + 1) * DH, :], l_ref[h : h + 1, :], lse_tile,
                    m_ref[h : h + 1, :],
                )
            lse_ref[:, pl.ds(at, TILE)] = lse_tile


def rest_kernel(
    info_ref, xm_ref, xo_ref, wqm_ref, wqo_ref, wvm_ref, wvo_ref, row_ref, col_ref,
    q_ref, own_ref, own_lse_ref, meta_ref, send_ref,
    out_ref, lse_ref, sums_ref, wvm_t_ref, wvo_t_ref, pk_ref, pv_ref, ps_ref,
):
    halo = xm_ref.shape[0]
    heads = q_ref.shape[1] // DH
    tiles = BLOCK // TILE
    skipped = (BLOCK - halo) // TILE
    meets = 2 + tiles + tiles * tiles
    used = meets + tiles
    out_ref[...] = own_ref[...]
    lse_ref[...] = own_lse_ref[...]
    wvm_t_ref[...] = jnp.transpose(wvm_ref[...])
    wvo_t_ref[...] = jnp.transpose(wvo_ref[...])

    @pl.loop(0, halo // TILE)
    def _(t):
        at = pl.multiple_of(t * TILE, TILE)

        @pl.when(info_ref[used + skipped + t] != 0)
        def _():
            mine, other = xm_ref[pl.ds(at, TILE), :], xo_ref[pl.ds(at, TILE), :]
            keys = project(mine, other, wqm_ref[...], wqo_ref[...])
            pk_ref[pl.ds(at, TILE), :] = keys
            pv_ref[:, pl.ds(at, TILE)] = project_t(mine, other, wvm_t_ref[...], wvo_t_ref[...])
            for h in range(heads):
                cols = slice(h * DH, (h + 1) * DH)
                ps_ref[pl.ds(at, TILE), cols] = key_scales(keys[:, cols])

        @pl.when(info_ref[used + skipped + t] == 0)
        def _():
            pk_ref[pl.ds(at, TILE), :] = jnp.zeros((TILE, heads * DH), BF)
            pv_ref[:, pl.ds(at, TILE)] = jnp.zeros((heads * DH, TILE), BF)
            ps_ref[pl.ds(at, TILE), :] = jnp.zeros((TILE, heads * DH), F32)

    lse_row = iota((8, TILE), 0)

    @pl.loop(0, tiles)
    def _(i):
        @pl.when(info_ref[meets + i] != 0)
        def _():
            at = pl.multiple_of(i * TILE, TILE)
            query_label = row_ref[0:1, pl.ds(at, TILE)]
            lse_tile = lse_ref[:, pl.ds(at, TILE)]
            for h in range(heads):
                cols = slice(h * DH, (h + 1) * DH)
                scores = score_tile(
                    pk_ref[:, cols], q_ref[pl.ds(at, TILE), cols], ps_ref[:, cols],
                    col_ref[BLOCK - halo :, :], query_label, None,
                )
                result, top, total = soft(scores, pv_ref[cols, :])
                there = top + jnp.log(total)
                here = lse_tile[h : h + 1, :]
                largest = jnp.maximum(here, there)
                kept, added = jnp.exp(here - largest), jnp.exp(there - largest)
                merged = kept * out_ref[cols, pl.ds(at, TILE)].astype(F32) + result * (
                    added / total
                )
                out_ref[cols, pl.ds(at, TILE)] = (merged * (1.0 / (kept + added))).astype(BF)
                lse_tile = jnp.where(lse_row == h, largest + jnp.log(kept + added), lse_tile)
            lse_ref[:, pl.ds(at, TILE)] = lse_tile

    row8 = iota((8, BLOCK), 0)
    sums = jnp.zeros((8, BLOCK), F32)
    for h in range(heads):
        lse = lse_ref[h : h + 1, :]
        top = lse.astype(BF).astype(F32)
        sums = jnp.where(row8 == 2 * h, top, jnp.where(row8 == 2 * h + 1, lse - top, sums))
    sums_ref[...] = jnp.concatenate([sums] * SLOTS, axis=0).astype(BF)

    step = 256

    @pl.loop(0, send_ref.shape[0] // step)
    def _(t):
        at = pl.multiple_of(t * step, step)
        codes = place_columns(meta_ref[...], at, step)
        lane = (iota((step, 128), 1) + 32).astype(F32)
        pick = jnp.concatenate(
            [mask(codes == lane + float(c)) for c in range(0, BLOCK, 128)], axis=1
        )
        body = mm_nt(pick, out_ref[...])
        sums = mm_nt(pick, sums_ref[...])
        row = iota((step, 128), 0) & (SLOTS - 1)
        sums = jnp.where(row == (iota((step, 128), 1) >> 3), sums, 0.0)
        sums = jnp.sum(sums.reshape(step // SLOTS, SLOTS, 128), axis=1, keepdims=True)
        sums = jnp.broadcast_to(sums, (step // SLOTS, SLOTS, 128)).reshape(step, 128)
        extra = jnp.where(row == META, sums, 0.0)
        send_ref[pl.ds(at, step), 0:128] = (body[:, 0:128] + extra).astype(BF)
        send_ref[pl.ds(at, step), 128:] = body[:, 128:].astype(BF)


def final_kernel(x_ref, pos_ref, w_ref, out_ref, *, owners):
    count = out_ref.shape[0]
    width = x_ref.shape[1]
    rows = owners * SLOTS
    heads = width // DH
    lane = iota((count, 128), 1)
    picks, meta_picks, ranks = [], [], []
    for r in range(2):
        dest, _, rank = slots_of(pos_ref[r : r + 1, :], owners)
        slot = (dest * SLOTS + rank).astype(F32)
        slot = jnp.transpose(jnp.broadcast_to(slot, (128, count))).astype(I32)
        place = slot & (SLOTS - 1)
        at_meta = slot - place + META
        picks.append(
            jnp.concatenate([mask(slot == lane + c) for c in range(0, rows, 128)], axis=1)
        )
        meta_picks.append(
            jnp.concatenate([mask(at_meta == lane + c) for c in range(0, rows, 128)], axis=1)
        )
        ranks.append(place)
    v = iota((128, width), 0) & 7
    select = mask((v >> 1) == (iota((128, width), 1) >> 7))
    total = None
    for a in range(2):
        values, sums = [], []
        for r in range(2):
            at = (a * 2 + r) * rows
            values.append(mm(picks[r], x_ref[at : at + rows, :]))
            own = mm(meta_picks[r], x_ref[at : at + rows, 0:128])
            own = jnp.where((lane >> 3) == ranks[r], own, 0.0).astype(BF)
            sums.append(mm(own, select))
        largest = jnp.maximum(sums[0], sums[1])
        first, second = jnp.exp(sums[0] - largest), jnp.exp(sums[1] - largest)
        combined = ((first * values[0] + second * values[1]) / (first + second)).astype(BF)
        part = mm(combined, w_ref[a * width : (a + 1) * width, :])
        total = part if total is None else total + part
    out_ref[...] = total.astype(BF)


def window_plan(own, prior):
    first = prior[0]
    own = jnp.where(own < first, own + SHIFT, own).reshape(-1, TILE)
    prior = jnp.where(prior < first, prior + SHIFT, prior).reshape(-1, TILE)
    low, high = jnp.min(own, axis=1), jnp.max(own, axis=1)
    prior_low, prior_high = jnp.min(prior, axis=1), jnp.max(prior, axis=1)

    def meets(key_low, key_high):
        return (key_low[None, :] <= high[:, None]) & (key_high[None, :] >= low[:, None])

    own_meets, prior_meets = meets(low, high), meets(prior_low, prior_high)
    tile = jnp.arange(own.shape[0], dtype=I32)
    beyond = jnp.any(own_meets & (jnp.abs(tile[:, None] - tile[None, :]) > 1), axis=1)
    flags = [beyond, own_meets.reshape(-1), jnp.any(prior_meets, 1), jnp.any(prior_meets, 0)]
    return jnp.concatenate(flags).astype(I32)


def shards(tokens, w_qk, w_v, w_out, positions, buckets):
    tok_dev, model_width = tokens.shape
    owners = lax.axis_size("seq")
    everyone = ("round", "head", "seq")
    total = 2 * 2 * owners
    width = model_width // 2
    heads = width // DH
    rows = total * SLOTS
    half = BLOCK // 2
    core = lax.axis_index("round").astype(I32)
    params = pltpu.CompilerParams(vmem_limit_bytes=48 * 1024 * 1024)

    def shape(*dims, dtype=BF):
        return jax.ShapeDtypeStruct(dims, dtype)

    def cost(flops, moved):
        return pl.CostEstimate(flops=flops, bytes_accessed=moved, transcendentals=0)

    def swap(x):
        return lax.ppermute(x, "round", [(0, 1), (1, 0)])

    def onward(x):
        return lax.ppermute(x, "seq", [(i, (i + 1) % owners) for i in range(owners)])

    def to_round(x, ahead):
        route = []
        for r in range(2):
            for g in range(2):
                for i in range(owners):
                    at = (i + ahead) % owners
                    route.append(((r * 2 + g) * owners + i, (g * 2 + r) * owners + at))
        return lax.ppermute(x, everyone, route)

    def exchange(x):
        x = x.reshape(total, SLOTS, width)
        x = lax.all_to_all(x, everyone, split_axis=0, concat_axis=0, tiled=True)
        return x.reshape(rows, width)

    packed = pl.pallas_call(
        functools.partial(pack_kernel, owners=owners),
        out_shape=shape(rows, width),
        compiler_params=params,
        name="pack",
    )(tokens, positions, buckets)
    arrived = exchange(packed)
    own_label, prior_label = to_round(buckets[0], 0), to_round(buckets[0], 1)

    high, meta, codes, wide = pl.pallas_call(
        sort_high_kernel,
        out_shape=[
            shape(half, width),
            shape(total, 128),
            shape(total // 8, 128, dtype=F32),
            shape(1, 1, dtype=F32),
        ],
        compiler_params=params,
        name="sort_high",
    )(arrived)
    halo_high = onward(high)
    high_other = swap(high)
    low = pl.pallas_call(
        sort_low_kernel,
        out_shape=shape(half, width),
        compiler_params=params,
        cost_estimate=cost(2 * half * rows * width, 4 * 2**20),
        name="sort_low",
    )(arrived, codes)
    low_other = swap(low)

    plan = window_plan(own_label, prior_label)
    info = jnp.concatenate([jnp.stack([core, 1 - core]), plan])
    label_row = own_label[None, :]
    label_col = jnp.broadcast_to(own_label[:, None], (BLOCK, TILE))
    prior_col = jnp.broadcast_to(prior_label[:, None], (BLOCK, TILE))

    def weight(flip):
        return pl.BlockSpec((width, width), lambda i, s: (s[flip], s[0]))

    weights = [weight(0), weight(1), weight(0), weight(1)]
    weight_args = (w_qk, w_qk, w_v, w_v)
    halves = full((half, width))
    queries, own_out, own_lse = pl.pallas_call(
        own_kernel,
        out_shape=[shape(BLOCK, width), shape(width, BLOCK), shape(8, BLOCK, dtype=F32)],
        grid_spec=pltpu.PrefetchScalarGridSpec(
            num_scalar_prefetch=1,
            grid=(1,),
            in_specs=[halves] * 4 + weights + [full((1, BLOCK)), full((BLOCK, TILE))],
            out_specs=[full((BLOCK, width)), full((width, BLOCK)), full((8, BLOCK))],
            scratch_shapes=[
                pltpu.VMEM((width, BLOCK), BF),
                pltpu.VMEM((BLOCK, width), F32),
                pltpu.VMEM((8, TILE), F32),
                pltpu.VMEM((8, TILE), F32),
                pltpu.VMEM((width, TILE), F32),
            ],
        ),
        compiler_params=params,
        cost_estimate=cost(8 * BLOCK * width * width, 8 * 2**20),
        name="own_block",
    )(info, low, high, low_other, high_other, *weight_args, label_row, label_col)
    halo_high, own_lse = lax.optimization_barrier((halo_high, own_lse))

    def finish(halo_mine, halo_other):
        halo = halo_mine.shape[0]
        return pl.pallas_call(
            rest_kernel,
            out_shape=shape(rows, width),
            grid_spec=pltpu.PrefetchScalarGridSpec(
                num_scalar_prefetch=1,
                grid=(1,),
                in_specs=[full((halo, width))] * 2
                + weights
                + [
                    full((1, BLOCK)),
                    full((BLOCK, TILE)),
                    full((BLOCK, width)),
                    full((width, BLOCK)),
                    full((8, BLOCK)),
                    full((total, 128)),
                ],
                out_specs=full((rows, width)),
                scratch_shapes=[
                    pltpu.VMEM((width, BLOCK), BF),
                    pltpu.VMEM((8, BLOCK), F32),
                    pltpu.VMEM((128, BLOCK), BF),
                    pltpu.VMEM((width, width), BF),
                    pltpu.VMEM((width, width), BF),
                    pltpu.VMEM((halo, width), BF),
                    pltpu.VMEM((width, halo), BF),
                    pltpu.VMEM((halo, width), F32),
                ],
            ),
            compiler_params=params,
            name="prior_block",
        )(
            info, halo_mine, halo_other, *weight_args, label_row, prior_col,
            queries, own_out, own_lse, meta,
        )

    halo_high_other = swap(halo_high)

    def whole_window():
        halo_low = onward(low)
        return finish(
            jnp.concatenate([halo_low, halo_high], axis=0),
            jnp.concatenate([swap(halo_low), halo_high_other], axis=0),
        )

    back = lax.cond(
        wide[0, 0] > 0.0, whole_window, lambda: finish(halo_high, halo_high_other)
    )
    returned = exchange(back)
    return pl.pallas_call(
        functools.partial(final_kernel, owners=owners),
        out_shape=shape(tok_dev, model_width),
        compiler_params=params,
        name="combine",
    )(returned, positions, w_out)


def solution(mesh):
    in_specs = (
        P(("round", "head", "seq"), None),
        P(),
        P(),
        P(),
        P(None, ("round", "head", "seq")),
        P("round", "seq"),
    )
    out_specs = P(("round", "head", "seq"), None)
    return jax.shard_map(shards, mesh=mesh, in_specs=in_specs, out_specs=out_specs, check_vma=False)
```

time: 285 us -> 127 us (0.45)
  blocking collectives: 196 us -> 34.2 us
  Pallas kernels: 52.8 us -> 39 us
  waiting for transfers between devices: 14.7 us -> 26.7 us
  starting transfers between devices: 12.9 us -> 18.9 us
    all_gather x1 -> x0, blocking collectives: 161 us -> none  [shards(): lax.all_gather(buckets[0], ('round', 'seq')).reshape(2, owners, BLOCK)]
    ppermute x0 -> x2, waiting for transfers between devices: none -> 24.7 us  [to_round(): return lax.ppermute(x, everyone, route)]
    ppermute x1, waiting for transfers between devices: 14.7 us -> 0.01 us  [onward(): lax.ppermute(x, 'seq', [(i, (i + 1) % owners) for i in range(owners)])]
    pallas_call x5 -> x6, Pallas kernels: 52.8 us -> 39 us  [the longest x1 16.4 us: shards(): pl.pallas_call(own_kernel, out_shape=[shape(BLOCK, width), shape(width, B...]
    ppermute x0 -> x2, starting transfers between devices: none -> 6.44 us  [to_round(): return lax.ppermute(x, everyone, route)]
  transfers between devices with their start and end apart: 5 -> 7, of which waited for: 1 -> 3; matrix products, arithmetic and copies ran while one was open for 2% -> 2% of each run, Pallas kernels for 4% -> 16%
where the time goes in v2:
time: 127 us; the launch traced here: 126 us
  Pallas kernels  39 us (31%)
  blocking collectives  34.2 us (27%)
  waiting for transfers between devices  26.7 us (21%)
  starting transfers between devices  18.9 us (15%)
  local copies, waits for them, and re-layouts  4.7 us (4%)
  other arithmetic  1.76 us (1%)
    all_to_all x1, blocking collectives, exchange(): x = lax.all_to_all(x, everyone, split_axis=0, concat_axis=0, tiled=True)  34.2 us
    ppermute x2, waiting for transfers between devices, to_round(): return lax.ppermute(x, everyone, route)  24.7 us
    pallas_call x1, Pallas kernels, shards(): pl.pallas_call(own_kernel, out_shape=[shape(BLOCK, width), shape(width, B...  16.4 us
    pallas_call x1, Pallas kernels, finish(): pl.pallas_call(rest_kernel, out_shape=shape(rows, width), grid_spec=pltpu...  13.9 us
    all_to_all x1, starting transfers between devices, exchange(): x = lax.all_to_all(x, everyone, split_axis=0, concat_axis=0, tiled=True)  11.5 us
    ppermute x2, starting transfers between devices, to_round(): return lax.ppermute(x, everyone, route)  6.44 us
    unnamed x18, local copies, waits for them, and re-layouts  3.76 us
    pallas_call x1, Pallas kernels, shards(): pl.pallas_call(functools.partial(final_kernel, owners=owners), out_shape=...  3.5 us
  transfers between devices with their start and end apart: 7, of which 3 were waited for; matrix products, arithmetic and copies ran while one was open for 2% of the time, Pallas kernels for 16%

profile of v2, /device:TPU:1, one launch (start us, length us, event | category | flops | bytes accessed | tf_op | source)
XLA Modules:
  0.0 126.3 jit_solution(1089901417477931127)
XLA Ops:
  0.0 1.0 copy-done.2
  1.0 0.7 copy-done.3
  1.7 0.7 copy-done.5
  2.4 1.2 pack.1
  3.6 1.3 %copy-done = bf16[2048,512]{1,0:T(8,128)(2,1)} copy-done((bf16[2048,512]{1,0:T(8,128)(2,1)}, bf16[2048,512]{1,0:T(8,128)(2,1)S(1)}, u32[]{:S(2)}) %copy-start) | copy-done | bytes 2097176
  5.0 11.5 %all-to-all-start = ((bf16[128,16,512]{2,1,0:T(8,128)(2,1)}), bf16[128,16,512]{2,1,0:T(8,128)(2,1)S(1)}, u32[]{:S(2)}, u32[]{:S(2)}) async-start(bf16[128,16,512]{2,1,0:T(8,128)(2,1)} %bitcast.24), calls=%async_computation | async-start | bytes 4194304 | tf_op jit(solution)/shard_map/all_to_all | solution.py:460
  16.5 4.3 %collective-permute-start.3 = (s32[1024]{0:T(1024)S(1)}, s32[1024]{0:T(1024)S(1)}, u32[]{:S(2)}, u32[]{:S(2)}) collective-permute-start(s32[1024]{0:T(1024)S(1)} %bitcast.26), channel_id=1, source_target_pairs={{0,1},{1,2},{2,3},{3,4},{4,5},{5,6},{6,7},{7,8},{8,9},{9,10},{10,1... | collective-permute-start | bytes 12296 | tf_op jit(solution)/shard_map/ppermute | solution.py:456
  20.7 2.2 %collective-permute-start.2 = (s32[1024]{0:T(1024)S(1)}, s32[1024]{0:T(1024)S(1)}, u32[]{:S(2)}, u32[]{:S(2)}) collective-permute-start(s32[1024]{0:T(1024)S(1)} %bitcast.27), channel_id=1, source_target_pairs={{0,0},{1,1},{2,2},{3,3},{4,4},{5,5},{6,6},{7,7},{8,8},{9,9},{10,10... | collective-permute-start | bytes 12296 | tf_op jit(solution)/shard_map/ppermute | solution.py:456
  22.9 24.7 %collective-permute-done.3 = s32[1024]{0:T(1024)S(1)} collective-permute-done((s32[1024]{0:T(1024)S(1)}, s32[1024]{0:T(1024)S(1)}, u32[]{:S(2)}, u32[]{:S(2)}) %collective-permute-start.3) | collective-permute-done | bytes 4128 | tf_op jit(solution)/shard_map/ppermute | solution.py:456
  47.6 0.5 slice.3
  48.1 0.7 fusion.7
  48.8 2.0 %sort_high.1 = (bf16[512,512]{1,0:T(8,128)(2,1)S(1)}, bf16[128,128]{1,0:T(8,128)(2,1)S(1)}, f32[16,128]{1,0:T(8,128)S(1)}, f32[1,1]{1,0:T(1,128)}) custom-call(bf16[2048,512]{1,0:T(8,128)(2,1)S(1)} %bitcast.22), custom_call_target="tpu_custom_call" | custom-call | tf_op jit(solution)/shard_map/sort_high/pallas_call | solution.py:472
  50.8 2.0 %sort_low.1.lm_ref = bf16[512,512]{1,0:T(8,128)(2,1)} custom-call(bf16[2048,512]{1,0:T(8,128)(2,1)S(1)} %bitcast.23, f32[16,128]{1,0:T(8,128)S(1)} %get-tuple-element.88.code_ref), custom_call_target="tpu_custom_call" | custom-call | flops 1073741824 | bytes 4194304 | tf_op jit(solution)/shard_map/sort_low/pallas_call | solution.py:485
  52.8 0.5 collective-permute-start.6
  53.3 0.7 fusion.8
  54.0 0.1 collective-permute-start.4
  54.1 0.2 fusion.5
  54.3 0.1 and.16
  54.4 0.1 add_convert_fusion
  54.5 0.1 pad_add_fusion.info_ref
  54.6 1.1 collective-permute-done.5.lo_ref
  55.7 0.2 broadcast_in_dim.7.col_ref
  55.9 0.0 copy-start.7
  55.9 0.0 copy-start.10
  55.9 16.4 %own_block.1 = (bf16[1024,512]{1,0:T(8,128)(2,1)S(1)}, bf16[512,1024]{1,0:T(8,128)(2,1)S(1)}, f32[8,1024]{1,0:T(8,128)S(1)}) custom-call(s32[90]{0:T(128)S(1)} %pad_add_fusion.info_ref, bf16[512,512]{1,0:T(8,128)(2,1)} %sort_low.1.lm_ref, bf16[512,512]{1,0:T(8,128)(2,1)S(1)} %get-tuple-element.87.hm_ref, bf16[512,512]{1,0:T(8,128)(2,1)S(1)} %collective-permute-done.5.lo_ref, ...), custom_call_target="tpu_custom_call" | custom-call | flops 2147483648 | bytes 8388608 | tf_op jit(solution)/shard_map/own_block/pallas_call | solution.py:506
  72.3 0.4 collective-permute-start.7
  73.3 1.0 collective-permute-done.7
  74.3 0.2 broadcast_in_dim.8
  74.5 14.1 %conditional.1 = (bf16[2048,512]{1,0:T(8,128)(2,1)}) conditional(s32[]{:T(128)} %bitcast.2, (s32[90]{0:T(128)S(1)}, bf16[512,512]{1,0:T(8,128)(2,1)S(1)}, bf16[512,512]{1,0:T(8,128)(2,1)S(1)}, bf16[1024,1024]{1,0:T(8,128)(2,1)S(1)}, bf16[1024,1024]{1,0:T(8,128)(2,1)S(1)}, /*index=5*/s32[1,1024]{1,0:T(1,128)S(1)}, s32[1024,128]{1,0:T(8,128)S(1)}, ...), branch_computations={%region_7.8_spmd, %region_8.9_spmd} | conditional | flops 4194304 | bytes 41943240 | solution.py:574
  74.7 13.9 %prior_block.2 = bf16[2048,512]{1,0:T(8,128)(2,1)} custom-call(s32[90]{0:T(128)S(1)} %get-tuple-element.54.info_ref, bf16[512,512]{1,0:T(8,128)(2,1)S(1)} %get-tuple-element.55.xm_ref, bf16[512,512]{1,0:T(8,128)(2,1)S(1)} %get-tuple-element.56.xo_ref, bf16[1024,1024]{1,0:T(8,128)(2,1)S(1)} %get-tuple-element.57.wqm_ref.wqo_ref, ...), custom_call_target="tpu_custom_call" | custom-call | tf_op jit(solution)/shard_map/cond/branch_0_fun/prior_block/pallas_call | solution.py:530
  88.6 34.2 %all_to_all.10 = bf16[128,16,512]{2,1,0:T(8,128)(2,1)S(1)} all-to-all(bf16[128,16,512]{2,1,0:T(8,128)(2,1)} %bitcast.10), channel_id=1, replica_groups=mesh['round'=2,'head'=2,'seq'=32] {'round','head','seq'}, dimensions={0} | all-to-all | bytes 4194304 | tf_op jit(solution)/shard_map/all_to_all | solution.py:460
  122.8 3.5 %combine.1 = bf16[256,1024]{1,0:T(8,128)(2,1)} custom-call(bf16[2048,512]{1,0:T(8,128)(2,1)S(1)} %bitcast.25, s32[2,256]{1,0:T(2,128)S(1)} %copy-done.4, bf16[1024,1024]{1,0:T(8,128)(2,1)S(1)} %copy-done.1), custom_call_target="tpu_custom_call" | custom-call | tf_op jit(solution)/shard_map/combine/pallas_call | solution.py:578
  (17 shorter events, 0.0 us)
Async XLA Ops:
  0.0 1.0 copy-start.2
  1.0 0.7 copy-start.3
  1.7 0.7 copy-start.5
  3.6 1.3 %copy-start = (bf16[2048,512]{1,0:T(8,128)(2,1)}, bf16[2048,512]{1,0:T(8,128)(2,1)S(1)}, u32[]{:S(2)}) copy-start(bf16[2048,512]{1,0:T(8,128)(2,1)S(1)} %pack.1) | copy-start | bytes 6291460
  5.0 11.5 %copy-start.6 = (s32[1,1024]{1,0:T(1,128)S(1)}, s32[1,1024]{1,0:T(1,128)}, u32[]{:S(2)}) copy-start(s32[1,1024]{1,0:T(1,128)} %label_ref.1) | copy-start | bytes 12292
  5.0 43.8 %all-to-all-start = ((bf16[128,16,512]{2,1,0:T(8,128)(2,1)}), bf16[128,16,512]{2,1,0:T(8,128)(2,1)S(1)}, u32[]{:S(2)}, u32[]{:S(2)}) async-start(bf16[128,16,512]{2,1,0:T(8,128)(2,1)} %bitcast.24), calls=%async_computation | async-start | bytes 4194304 | tf_op jit(solution)/shard_map/all_to_all | solution.py:460
  16.5 31.1 %collective-permute-start.3 = (s32[1024]{0:T(1024)S(1)}, s32[1024]{0:T(1024)S(1)}, u32[]{:S(2)}, u32[]{:S(2)}) collective-permute-start(s32[1024]{0:T(1024)S(1)} %bitcast.26), channel_id=1, source_target_pairs={{0,1},{1,2},{2,3},{3,4},{4,5},{5,6},{6,7},{7,8},{8,9},{9,10},{10,1... | collective-permute-start | bytes 12296 | tf_op jit(solution)/shard_map/ppermute | solution.py:456
  20.7 32.6 %collective-permute-start.2 = (s32[1024]{0:T(1024)S(1)}, s32[1024]{0:T(1024)S(1)}, u32[]{:S(2)}, u32[]{:S(2)}) collective-permute-start(s32[1024]{0:T(1024)S(1)} %bitcast.27), channel_id=1, source_target_pairs={{0,0},{1,1},{2,2},{3,3},{4,4},{5,5},{6,6},{7,7},{8,8},{9,9},{10,10... | collective-permute-start | bytes 12296 | tf_op jit(solution)/shard_map/ppermute | solution.py:456
  52.8 2.8 %collective-permute-start.5 = (bf16[512,512]{1,0:T(8,128)(2,1)}, bf16[512,512]{1,0:T(8,128)(2,1)S(1)}, u32[]{:S(2)}, u32[]{:S(2)}) collective-permute-start(bf16[512,512]{1,0:T(8,128)(2,1)} %sort_low.1.lm_ref), channel_id=1, source_target_pairs={{0,64},{64,0},{1,65},{65,1},{2,66},{66,2},{3,67},{67,3},{4,68},{68... | collective-permute-start | bytes 1572872 | tf_op jit(solution)/shard_map/ppermute | solution.py:444
  52.8 2.8 %collective-permute-start.6 = (bf16[512,512]{1,0:T(8,128)(2,1)S(1)}, bf16[512,512]{1,0:T(8,128)(2,1)S(1)}, u32[]{:S(2)}, u32[]{:S(2)}) collective-permute-start(bf16[512,512]{1,0:T(8,128)(2,1)S(1)} %get-tuple-element.87.hm_ref), channel_id=1, source_target_pairs={{0,64},{64,0},{1,65},{65,1},{2,66},{66,2},{3,67},{67,3},{4,68},{68... | collective-permute-start | bytes 1572872 | tf_op jit(solution)/shard_map/ppermute | solution.py:444
  54.0 18.2 %collective-permute-start.4 = (bf16[512,512]{1,0:T(8,128)(2,1)S(1)}, bf16[512,512]{1,0:T(8,128)(2,1)S(1)}, u32[]{:S(2)}, u32[]{:S(2)}) collective-permute-start(bf16[512,512]{1,0:T(8,128)(2,1)S(1)} %get-tuple-element.87.hm_ref), channel_id=1, source_target_pairs={{0,1},{1,2},{2,3},{3,4},{4,5},{5,6},{6,7},{7,8},{8,9},{9,10},{10,1... | collective-permute-start | bytes 1572872 | tf_op jit(solution)/shard_map/ppermute | solution.py:447
  55.9 18.6 %copy-start.7 = (bf16[1024,1024]{1,0:T(8,128)(2,1)S(1)}, bf16[1024,1024]{1,0:T(8,128)(2,1)}, u32[]{:S(2)}) copy-start(bf16[1024,1024]{1,0:T(8,128)(2,1)} %wqo_ref.1) | copy-start | bytes 6291460
  55.9 18.6 %copy-start.10 = (bf16[1024,1024]{1,0:T(8,128)(2,1)S(1)}, bf16[1024,1024]{1,0:T(8,128)(2,1)}, u32[]{:S(2)}) copy-start(bf16[1024,1024]{1,0:T(8,128)(2,1)} %wvo_ref.1) | copy-start | bytes 6291460
  72.3 2.0 %collective-permute-start.7 = (bf16[512,512]{1,0:T(8,128)(2,1)S(1)}, bf16[512,512]{1,0:T(8,128)(2,1)S(1)}, u32[]{:S(2)}, u32[]{:S(2)}) collective-permute-start(bf16[512,512]{1,0:T(8,128)(2,1)S(1)} %collective-permute-done.4), channel_id=1, source_target_pairs={{0,64},{64,0},{1,65},{65,1},{2,66},{66,2},{3,67},{67,3},{4,68},{68... | collective-permute-start | bytes 1572872 | tf_op jit(solution)/shard_map/ppermute | solution.py:444
  88.6 34.2 %copy-start.1 = (bf16[1024,1024]{1,0:T(8,128)(2,1)S(1)}, bf16[1024,1024]{1,0:T(8,128)(2,1)}, u32[]{:S(2)}) copy-start(bf16[1024,1024]{1,0:T(8,128)(2,1)} %w_ref.1) | copy-start | bytes 6291460
  88.6 34.2 %copy-start.4 = (s32[2,256]{1,0:T(2,128)S(1)}, s32[2,256]{1,0:T(2,128)}, u32[]{:S(2)}) copy-start(s32[2,256]{1,0:T(2,128)} %pos_ref.3) | copy-start | bytes 6148

commit v3 on v2

v3 whole, which is shorter than its diff:
```python
import functools

import jax
import jax.numpy as jnp
from jax import lax
from jax.experimental import pallas as pl
from jax.experimental.pallas import tpu as pltpu
from jax.sharding import PartitionSpec as P

DH = 128
BLOCK = 1024
TILE = 128
SPAN = 256
SPANS = BLOCK // SPAN
SLOTS = 16
META = 14
LABELS = 15
SHIFT = 65536.0
STEP = 256

LOG2E = 1.4426950408889634
SELF_PENALTY = -100000.0 * LOG2E
BUCKET_PENALTY = -1000000000.0
EPSILON = 1e-06

BF = jnp.bfloat16
F32 = jnp.float32
I32 = jnp.int32
NT = (((1,), (1,)), ((), ()))


def iota(shape, dim):
    return lax.broadcasted_iota(I32, shape, dim)


def mask(cond):
    return jnp.where(cond, 1.0, 0.0).astype(BF)


def mm(a, b):
    return jnp.dot(a, b, preferred_element_type=F32)


def mm_nt(a, b):
    return lax.dot_general(a, b, NT, preferred_element_type=F32)


def head_cols(h, wide=1):
    return slice(h * DH * wide, (h + 1) * DH * wide)


def slots_of(pos, owners):
    count = pos.shape[1]
    dest = pos >> 10
    hot = iota((owners, count), 0) == dest
    earlier = mask(iota((count, count), 0) < iota((count, count), 1))
    before = mm(mask(hot), earlier)
    rank = jnp.sum(jnp.where(hot, before, 0.0), axis=0, keepdims=True).astype(I32)
    return hot, dest * SLOTS + rank


def pack_kernel(info_ref, tok_ref, pos_ref, label_ref, out_ref, buf_ref, sem_ref, *, owners):
    count = tok_ref.shape[0]
    width = out_ref.shape[1]
    rows = owners * SLOTS
    tokens = tok_ref[...]
    half = BLOCK // 2
    first, last = label_ref[0:1, 0:1], label_ref[0:1, BLOCK - 1 : BLOCK]
    middle = label_ref[0:1, half - 1 : half]
    marked = jnp.where(last == 0, jnp.minimum(first, middle), jnp.abs(middle - last))
    wide = jnp.where(jnp.broadcast_to(marked, (owners, 128)) == 0, 1.0, 0.0)
    label = label_ref[...]
    label = ((128 + (label & 127)) << (label >> 7)).astype(F32)
    label = jnp.where(info_ref[1] == 0, label[:, :half], label[:, half:])
    label = jnp.broadcast_to(label, (SLOTS, half))
    copies = []
    for r in range(2):
        pos = pos_ref[r : r + 1, :]
        hot, slot = slots_of(pos, owners)
        rank = slot & (SLOTS - 1)
        within = pos & (BLOCK - 1)
        pick = mask(iota((rows, count), 0) == slot)
        value = iota((128, count), 0)
        code = jnp.where((value & 1) == 0, (within >> 5) + 1, within & 31)
        code = jnp.where((value >> 1) == rank, code, 0).astype(F32).astype(BF)
        places = mm_nt(mask(hot), code)
        places = jnp.where(iota((owners, 128), 1) == 2 * SLOTS, wide, places).astype(BF)
        at_meta = mask(iota((rows, owners), 0) == iota((rows, owners), 1) * SLOTS + META)
        extra = mm(at_meta, places)
        for a in range(2):
            at = (a * 2 + r) * rows
            body = mm(pick, tokens[:, a * width : (a + 1) * width])
            buf_ref[at : at + rows, 0:128] = (body[:, 0:128] + extra).astype(BF)
            buf_ref[at : at + rows, 128:width] = body[:, 128:].astype(BF)

        @pl.when(info_ref[0] == r)
        def _():
            for a in range(2):
                for ahead in range(2):
                    block = (info_ref[2] + ahead) & (owners - 1)
                    at = pl.multiple_of((a * 2 + r) * rows + block * SLOTS, SLOTS)
                    old = buf_ref[pl.ds(at, SLOTS), :].astype(F32)
                    new = jnp.where(iota((SLOTS, half), 0) == LABELS, label, old)
                    buf_ref[pl.ds(at, SLOTS), :] = new.astype(BF)

        for a in range(2):
            piece = pl.ds((a * 2 + r) * rows, rows)
            copy = pltpu.make_async_copy(
                buf_ref.at[piece], out_ref.at[piece], sem_ref.at[a * 2 + r]
            )
            copy.start()
            copies.append(copy)
    for copy in copies:
        copy.wait()


def prepare_kernel(
    info_ref, wqm_ref, wqo_ref, wvm_ref, wvo_ref, wo_ref, pos_ref,
    wq_ref, wvt_ref, wout_ref, slot_ref, *, owners,
):
    width = wqm_ref.shape[0]
    wq_ref[0:width, :] = wqm_ref[...]
    wq_ref[width:, :] = wqo_ref[...]
    wvt_ref[:, 0:width] = jnp.transpose(wvm_ref[...])
    wvt_ref[:, width:] = jnp.transpose(wvo_ref[...])
    wout_ref[...] = wo_ref[...]
    count = pos_ref.shape[1]
    for r in range(2):
        slot = slots_of(pos_ref[r : r + 1, :], owners)[1].astype(F32)
        slot_ref[r * count : (r + 1) * count, :] = jnp.transpose(
            jnp.broadcast_to(slot, (128, count))
        )


def meta_of(x_ref):
    rows = x_ref.shape[0]
    count = rows // SLOTS
    pick = mask(iota((count, rows), 1) == iota((count, rows), 0) * SLOTS + META)
    return mm(pick, x_ref[:, 0:128]).astype(BF)


def place_rows(meta):
    count = meta.shape[0]
    v, lane = iota((128, 128), 0), iota((128, 128), 1)
    j = lane & (SLOTS - 1)
    weight = jnp.where(v == 2 * j, 32.0, jnp.where(v == 2 * j + 1, 1.0, 0.0)).astype(BF)
    codes = mm(meta, weight)
    own = (iota((count, 128), 0) & 7) == (iota((count, 128), 1) >> 4)
    codes = jnp.where(own, codes, 0.0)
    return jnp.sum(codes.reshape(count // 8, 8, 128), axis=1)


def place_columns(meta, first, rows):
    count = meta.shape[0]
    slot = iota((rows, count), 0) + first
    source = mask((slot >> 4) == iota((rows, count), 1))
    values = mm(source, meta)
    lane = iota((rows, 128), 1)
    keep = (lane >> 1) == (iota((rows, 128), 0) & (SLOTS - 1))
    values = jnp.where(keep, values, 0.0).astype(BF)
    weight = jnp.where((iota((128, 128), 0) & 1) == 0, 32.0, 1.0).astype(BF)
    return mm(values, weight)


def sorted_rows(x_ref, code_ref, out_ref, first):
    step = 256
    chunks = code_ref.shape[0]
    for start in range(0, out_ref.shape[0], step):
        position = (iota((step, 128), 0) + (first + start + 32)).astype(F32)
        picks = [
            mask(position == jnp.broadcast_to(code_ref[q : q + 1, :], (step, 128)))
            for q in range(chunks)
        ]
        picks = jnp.concatenate(picks, axis=1)
        out_ref[start : start + step, :] = mm(picks, x_ref[...]).astype(BF)


def sort_high_kernel(x_ref, high_ref, meta_ref, code_ref, wide_ref):
    meta = meta_of(x_ref)
    meta_ref[...] = meta
    flags = jnp.where(iota(meta.shape, 1) == 2 * SLOTS, meta.astype(F32), 0.0)
    wide_ref[...] = jnp.max(jnp.max(flags, axis=1, keepdims=True), axis=0, keepdims=True)
    code_ref[...] = place_rows(meta)
    sorted_rows(x_ref, code_ref, high_ref, high_ref.shape[0])


def sort_low_kernel(
    info_ref, x_ref, code_ref, low_ref, row_ref, col_ref, prior_col_ref, flag_ref, *, owners
):
    def labels(block):
        parts = []
        for half in range(2):
            source = (info_ref[1] * 2 + half) * owners + block
            rows = x_ref[pl.ds(pl.multiple_of(source * SLOTS, SLOTS), SLOTS), :].astype(F32)
            at_labels = iota(rows.shape, 0) == LABELS
            parts.append(jnp.sum(jnp.where(at_labels, rows, 0.0), axis=0, keepdims=True))
        return jnp.concatenate(parts, axis=1)

    own = labels(info_ref[2])
    prior = labels((info_ref[2] + owners - 1) & (owners - 1))
    row_ref[...] = own
    col_ref[...] = jnp.transpose(jnp.broadcast_to(own, (TILE, BLOCK)))
    prior_col_ref[...] = jnp.transpose(jnp.broadcast_to(prior, (TILE, BLOCK)))
    flag_ref[...] = jnp.broadcast_to(plan(own, prior), flag_ref.shape)
    sorted_rows(x_ref, code_ref, low_ref, 0)


def plan(own, prior):
    first = prior[:, 0:1]

    def ends(labels):
        labels = jnp.where(labels < first, labels + SHIFT, labels)
        tiles = jnp.concatenate([labels[:, t : t + TILE] for t in range(0, BLOCK, TILE)], axis=0)
        low = jnp.min(tiles, axis=1, keepdims=True)
        high = jnp.max(tiles, axis=1, keepdims=True)
        return jnp.broadcast_to(low, tiles.shape), jnp.broadcast_to(high, tiles.shape)

    low, high = ends(own)
    prior_low, prior_high = ends(prior)
    tile = iota(low.shape, 0)
    bits = jnp.zeros((1, TILE), F32)

    def add(bits, flag, found):
        found = jnp.max(jnp.where(found, 1.0, 0.0), axis=0, keepdims=True)
        return bits + float(2**flag) * found

    per, tiles = SPAN // TILE, BLOCK // TILE
    for i in range(SPANS):
        at = i * per
        span_low = jnp.min(low[at : at + per], axis=0, keepdims=True)
        span_high = jnp.max(high[at : at + per], axis=0, keepdims=True)
        meets = (low <= span_high) & (high >= span_low)
        bits = add(bits, i, meets & ((tile < at - 1) | (tile > at + per)))
        start = min(max(at - 2, 0), tiles - per - 4)
        bits = add(bits, 4 + i, meets & ((tile < start) | (tile >= start + per + 4)))
    some = jnp.zeros(low.shape, F32)
    for i in range(tiles):
        meets = (prior_low <= high[i : i + 1]) & (prior_high >= low[i : i + 1])
        some = jnp.maximum(some, jnp.where(meets, 1.0, 0.0))
        bits = add(bits, 8 + i, meets)
    bits = add(bits, 16, (some > 0.0) & (tile < tiles - 1))
    return add(bits, 17, (some > 0.0) & (tile < tiles - 3))


def flag_bits(flag_ref):
    return jnp.max(flag_ref[...]).astype(I32)


def project(mine, other, wq_ref, wvt_ref):
    width = mine.shape[1]
    queries = (mm(mine, wq_ref[0:width, :]) + mm(other, wq_ref[width:, :])).astype(BF)
    values = mm_nt(wvt_ref[:, 0:width], mine) + mm_nt(wvt_ref[:, width:], other)
    parts = []
    for h in range(queries.shape[1] // DH):
        rows = queries[:, head_cols(h)].astype(F32)
        sq = jnp.square(rows)
        top = sq.astype(BF)
        rest = (sq - top.astype(F32)).astype(BF)
        total = mm(jnp.concatenate([top, rest], axis=1), jnp.ones((2 * DH, 128), BF))
        keys = rows * (lax.rsqrt(total * (1.0 / DH) + EPSILON) * (LOG2E * DH ** (-0.5)))
        top = keys.astype(BF)
        parts += [top, (keys - top.astype(F32)).astype(BF)]
    return queries, parts, values.astype(BF)


def value_rows(h):
    return slice(h * (DH + 16), (h + 1) * (DH + 16))


def store_keys(at, parts, values, key_ref, vt_ref):
    rows = parts[0].shape[0]
    for h in range(len(parts) // 2):
        key_ref[at : at + rows, h * 2 * DH : h * 2 * DH + DH] = parts[2 * h]
        key_ref[at : at + rows, h * 2 * DH + DH : (h + 1) * 2 * DH] = parts[2 * h + 1]
        first = h * (DH + 16)
        vt_ref[first : first + DH, at : at + rows] = values[head_cols(h), :]
        vt_ref[first + DH : first + DH + 16, at : at + rows] = jnp.ones((16, rows), BF)


def attend(keys, queries, values, key_label, query_label, diagonal):
    count, span = keys.shape[0], queries.shape[0]
    scores = mm_nt(keys, jnp.concatenate([queries, queries], axis=1))
    match = jnp.concatenate([key_label] * (span // TILE), axis=1) == query_label
    scores = jnp.where(match, scores, BUCKET_PENALTY)
    if isinstance(diagonal, int):
        cut = scores[diagonal : diagonal + span]
        cut = jnp.where(iota((span, span), 0) == iota((span, span), 1), SELF_PENALTY, cut)
        parts = [scores[:diagonal]] * (diagonal > 0) + [cut]
        parts += [scores[diagonal + span :]] * (diagonal + span < count)
        scores = jnp.concatenate(parts, axis=0) if len(parts) > 1 else cut
    elif diagonal is not None:
        apart = iota((count, span), 0) - iota((count, span), 1)
        scores = jnp.where(apart == diagonal, SELF_PENALTY, scores)
    top = jnp.max(scores, axis=0, keepdims=True)
    result = mm(values, jnp.exp2(scores - top).astype(BF))
    return result[0:DH], top, result[DH : DH + 1]


def sums_of(lse, heads):
    row = iota(lse.shape, 0)
    sums = jnp.zeros(lse.shape, F32)
    for h in range(heads):
        part = lse[h : h + 1, :]
        top = part.astype(BF).astype(F32)
        sums = jnp.where(row == 2 * h, top, jnp.where(row == 2 * h + 1, part - top, sums))
    return jnp.concatenate([sums] * SLOTS, axis=0).astype(BF)


def packed_rows(pick, out, sums):
    body = mm_nt(pick, out)
    sums = mm_nt(pick, sums)
    row = iota((STEP, 128), 0) & (SLOTS - 1)
    sums = jnp.where(row == (iota((STEP, 128), 1) >> 3), sums, 0.0)
    sums = jnp.sum(sums.reshape(STEP // SLOTS, SLOTS, 128), axis=1, keepdims=True)
    sums = jnp.broadcast_to(sums, (STEP // SLOTS, SLOTS, 128)).reshape(STEP, 128)
    extra = jnp.where(row == META, sums, 0.0)
    return jnp.concatenate([body[:, 0:128] + extra, body[:, 128:]], axis=1)


def own_kernel(
    lm_ref, hm_ref, lo_ref, ho_ref, wq_ref, wvt_ref, row_ref, col_ref, flag_ref, meta_ref,
    q_ref, out_ref, lse_ref, place_ref, key_ref, vt_ref,
):
    half = lm_ref.shape[0]
    heads = q_ref.shape[1] // DH
    bits = flag_bits(flag_ref)
    for m_part, o_part, at in ((hm_ref, ho_ref, half), (lm_ref, lo_ref, 0)):
        queries, parts, values = project(m_part[...], o_part[...], wq_ref, wvt_ref)
        q_ref[at : at + half, :] = queries
        store_keys(at, parts, values, key_ref, vt_ref)
    lse_row = iota((8, SPAN), 0)

    def put(at, h, found, lse_tile):
        result, top, total = found
        out_ref[head_cols(h), pl.ds(at, SPAN)] = (result * (1.0 / total)).astype(BF)
        return jnp.where(lse_row == h, top + jnp.log2(total), lse_tile)

    def span(at, start, size, diagonal):
        query_label = row_ref[0:1, pl.ds(at, SPAN)]
        key_label = col_ref[pl.ds(start, size), :]
        lse_tile = jnp.zeros((8, SPAN), F32)
        for h in range(heads):
            found = attend(
                key_ref[pl.ds(start, size), head_cols(h, 2)],
                q_ref[pl.ds(at, SPAN), head_cols(h)],
                vt_ref[value_rows(h), pl.ds(start, size)],
                key_label, query_label, diagonal,
            )
            lse_tile = put(at, h, found, lse_tile)
        lse_ref[:, pl.ds(at, SPAN)] = lse_tile

    def flag(k):
        return (bits >> k) & 1

    @pl.when(flag(0) == 0)
    def _():
        span(0, 0, SPAN + TILE, 0)

    @pl.loop(1, SPANS - 1)
    def _(i):
        @pl.when(flag(i) == 0)
        def _():
            at = pl.multiple_of(i * SPAN, SPAN)
            span(at, pl.multiple_of(at - TILE, TILE), SPAN + 2 * TILE, TILE)

    @pl.when(flag(SPANS - 1) == 0)
    def _():
        span(BLOCK - SPAN, BLOCK - SPAN - TILE, SPAN + TILE, TILE)

    @pl.loop(0, SPANS)
    def _(i):
        at = pl.multiple_of(i * SPAN, SPAN)

        @pl.when((flag(i) != 0) & (flag(4 + i) == 0))
        def _():
            size = SPAN + 4 * TILE
            start = pl.multiple_of(jnp.clip(at - 2 * TILE, 0, BLOCK - size), TILE)
            span(at, start, size, at - start)

        @pl.when(flag(4 + i) != 0)
        def _():
            span(at, 0, BLOCK, at)

    @pl.loop(0, place_ref.shape[0] // STEP)
    def _(t):
        at = pl.multiple_of(t * STEP, STEP)
        place_ref[pl.ds(at, STEP), :] = place_columns(meta_ref[...], at, STEP)


def rest_kernel(
    xm_ref, xo_ref, wq_ref, wvt_ref, row_ref, col_ref, flag_ref,
    q_ref, own_ref, own_lse_ref, place_ref, send_ref,
    out_ref, lse_ref, sums_ref, key_ref, vt_ref, buf_ref, sem_ref,
):
    halo = xm_ref.shape[0]
    heads = q_ref.shape[1] // DH
    bits = flag_bits(flag_ref)
    lse_row = iota((8, TILE), 0)
    out_ref[...] = own_ref[...]
    lse_ref[...] = own_lse_ref[...]

    def merge(size):
        first = halo - size
        _, parts, values = project(xm_ref[first:, :], xo_ref[first:, :], wq_ref, wvt_ref)
        store_keys(first, parts, values, key_ref, vt_ref)

        @pl.loop(0, BLOCK // TILE)
        def _(i):
            @pl.when(((bits >> (8 + i)) & 1) != 0)
            def _():
                at = pl.multiple_of(i * TILE, TILE)
                lse_tile = lse_ref[:, pl.ds(at, TILE)]
                for h in range(heads):
                    result, top, total = attend(
                        key_ref[first:, head_cols(h, 2)],
                        q_ref[pl.ds(at, TILE), head_cols(h)],
                        vt_ref[value_rows(h), first:],
                        col_ref[BLOCK - size :, :], row_ref[0:1, pl.ds(at, TILE)], None,
                    )
                    here, there = lse_tile[h : h + 1, :], top + jnp.log2(total)
                    largest = jnp.maximum(here, there)
                    kept, added = jnp.exp2(here - largest), jnp.exp2(there - largest)
                    own = out_ref[head_cols(h), pl.ds(at, TILE)].astype(F32)
                    merged = (kept * own + result * (added / total)) * (1.0 / (kept + added))
                    out_ref[head_cols(h), pl.ds(at, TILE)] = merged.astype(BF)
                    new = largest + jnp.log2(kept + added)
                    lse_tile = jnp.where(lse_row == h, new, lse_tile)
                lse_ref[:, pl.ds(at, TILE)] = lse_tile

    size_class = bits >> 16

    @pl.when(size_class == 0)
    def _():
        merge(TILE)

    @pl.when(size_class == 1)
    def _():
        merge(3 * TILE)

    @pl.when(size_class > 1)
    def _():
        merge(halo)

    sums_ref[...] = sums_of(lse_ref[...], heads)
    steps = send_ref.shape[0] // STEP

    def sending(t):
        piece = pl.ds(pl.multiple_of(t * STEP, STEP), STEP)
        return pltpu.make_async_copy(buf_ref.at[piece], send_ref.at[piece], sem_ref.at[t])

    @pl.loop(0, steps)
    def _(t):
        at = pl.multiple_of(t * STEP, STEP)
        codes = place_ref[pl.ds(at, STEP), :]
        lane = (iota((STEP, 128), 1) + 32).astype(F32)
        pick = jnp.concatenate(
            [mask(codes == lane + float(c)) for c in range(0, BLOCK, 128)], axis=1
        )
        buf_ref[pl.ds(at, STEP), :] = packed_rows(pick, out_ref[...], sums_ref[...]).astype(BF)
        sending(t).start()

    @pl.loop(0, steps)
    def _(t):
        sending(t).wait()


def final_kernel(x_ref, slot_ref, w_ref, out_ref, *, owners):
    count = out_ref.shape[0]
    width = x_ref.shape[1]
    rows = owners * SLOTS
    lane = iota((count, 128), 1)
    picks, meta_picks, ranks = [], [], []
    for r in range(2):
        slot = slot_ref[r * count : (r + 1) * count, :].astype(I32)
        place = slot & (SLOTS - 1)
        at_meta = slot - place + META
        picks.append(
            jnp.concatenate([mask(slot == lane + c) for c in range(0, rows, 128)], axis=1)
        )
        meta_picks.append(
            jnp.concatenate([mask(at_meta == lane + c) for c in range(0, rows, 128)], axis=1)
        )
        ranks.append(place)
    v = iota((128, width), 0) & 7
    select = mask((v >> 1) == (iota((128, width), 1) >> 7))
    total = None
    for a in range(2):
        values, sums = [], []
        for r in range(2):
            at = (a * 2 + r) * rows
            values.append(mm(picks[r], x_ref[at : at + rows, :]))
            own = mm(meta_picks[r], x_ref[at : at + rows, 0:128])
            own = jnp.where((lane >> 3) == ranks[r], own, 0.0).astype(BF)
            sums.append(mm(own, select))
        largest = jnp.maximum(sums[0], sums[1])
        first, second = jnp.exp2(sums[0] - largest), jnp.exp2(sums[1] - largest)
        combined = ((first * values[0] + second * values[1]) / (first + second)).astype(BF)
        part = mm(combined, w_ref[a * width : (a + 1) * width, :])
        total = part if total is None else total + part
    out_ref[...] = total.astype(BF)


def shards(tokens, w_qk, w_v, w_out, positions, buckets):
    tok_dev, model_width = tokens.shape
    owners = lax.axis_size("seq")
    everyone = ("round", "head", "seq")
    total = 2 * 2 * owners
    width = model_width // 2
    heads = width // DH
    rows = total * SLOTS
    half = BLOCK // 2
    info = jnp.stack([lax.axis_index(axis) for axis in everyone]).astype(I32)
    params = pltpu.CompilerParams(vmem_limit_bytes=40 * 2**20)
    alone = pltpu.CompilerParams(vmem_limit_bytes=60 * 2**20)
    in_vmem = pl.BlockSpec(memory_space=pltpu.VMEM)
    in_smem = pl.BlockSpec(memory_space=pltpu.SMEM)
    in_hbm = pl.BlockSpec(memory_space=pltpu.HBM)

    def shape(*dims, dtype=BF):
        return jax.ShapeDtypeStruct(dims, dtype)

    def cost(flops, moved):
        return pl.CostEstimate(flops=flops, bytes_accessed=moved, transcendentals=0)

    def swap(x):
        return lax.ppermute(x, "round", [(0, 1), (1, 0)])

    def onward(x):
        return lax.ppermute(x, "seq", [(i, (i + 1) % owners) for i in range(owners)])

    def exchange(x):
        x = x.reshape(total, SLOTS, width)
        x = lax.all_to_all(x, everyone, split_axis=0, concat_axis=0, tiled=True)
        return x.reshape(rows, width)

    packed = pl.pallas_call(
        functools.partial(pack_kernel, owners=owners),
        out_shape=shape(rows, width),
        in_specs=[in_smem] + [in_vmem] * 3,
        out_specs=in_hbm,
        scratch_shapes=[pltpu.VMEM((rows, width), BF), pltpu.SemaphoreType.DMA((4,))],
        compiler_params=alone,
        name="pack",
    )(info, tokens, positions, buckets)
    arrived = exchange(packed)

    def weight(other):
        return pl.BlockSpec(
            (width, width), lambda i, s: (1 - s[0] if other else s[0], s[0])
        )

    weights = [weight(False), weight(True)] * 2
    wq, wvt, wout, slots = pl.pallas_call(
        functools.partial(prepare_kernel, owners=owners),
        out_shape=[
            shape(model_width, width),
            shape(width, model_width),
            shape(model_width, model_width),
            shape(2 * tok_dev, 128, dtype=F32),
        ],
        grid_spec=pltpu.PrefetchScalarGridSpec(
            num_scalar_prefetch=1,
            grid=(1,),
            in_specs=weights + [in_vmem] * 2,
            out_specs=[in_vmem] * 4,
        ),
        compiler_params=params,
        cost_estimate=cost(2**30, 8 * 2**20),
        name="prepare",
    )(info, w_qk, w_qk, w_v, w_v, w_out, positions)
    arrived, wq, wvt, wout, slots = lax.optimization_barrier((arrived, wq, wvt, wout, slots))

    high, meta, codes, wide = pl.pallas_call(
        sort_high_kernel,
        out_shape=[
            shape(half, width),
            shape(total, 128),
            shape(total // 8, 128, dtype=F32),
            shape(1, 1, dtype=F32),
        ],
        compiler_params=params,
        name="sort_high",
    )(arrived)
    halo_high = onward(high)
    high_other = swap(high)
    low, label_row, label_col, prior_col, flags = pl.pallas_call(
        functools.partial(sort_low_kernel, owners=owners),
        out_shape=[
            shape(half, width),
            shape(1, BLOCK, dtype=F32),
            shape(BLOCK, TILE, dtype=F32),
            shape(BLOCK, TILE, dtype=F32),
            shape(8, 128, dtype=F32),
        ],
        in_specs=[in_smem] + [in_vmem] * 2,
        out_specs=[in_vmem] * 5,
        compiler_params=params,
        cost_estimate=cost(2 * half * rows * width, 4 * 2**20),
        name="sort_low",
    )(info, arrived, codes)
    low_other = swap(low)

    queries, own_out, own_lse, places = pl.pallas_call(
        own_kernel,
        out_shape=[
            shape(BLOCK, width),
            shape(width, BLOCK),
            shape(8, BLOCK, dtype=F32),
            shape(rows, 128, dtype=F32),
        ],
        in_specs=[in_vmem] * 10,
        out_specs=[in_vmem] * 4,
        scratch_shapes=[
            pltpu.VMEM((BLOCK, 2 * width), BF),
            pltpu.VMEM((heads * (DH + 16), BLOCK), BF),
        ],
        compiler_params=params,
        cost_estimate=cost(8 * BLOCK * width * width, 8 * 2**20),
        name="own_block",
    )(low, high, low_other, high_other, wq, wvt, label_row, label_col, flags, meta)
    halo_high, own_lse = lax.optimization_barrier((halo_high, own_lse))

    def finish(halo_mine, halo_other):
        halo = halo_mine.shape[0]
        return pl.pallas_call(
            rest_kernel,
            out_shape=shape(rows, width),
            in_specs=[in_vmem] * 11,
            out_specs=in_hbm,
            scratch_shapes=[
                pltpu.VMEM((width, BLOCK), BF),
                pltpu.VMEM((8, BLOCK), F32),
                pltpu.VMEM((128, BLOCK), BF),
                pltpu.VMEM((halo, 2 * width), BF),
                pltpu.VMEM((heads * (DH + 16), halo), BF),
                pltpu.VMEM((rows, width), BF),
                pltpu.SemaphoreType.DMA((rows // STEP,)),
            ],
            compiler_params=params,
            name="prior_block",
        )(
            halo_mine, halo_other, wq, wvt, label_row, prior_col, flags,
            queries, own_out, own_lse, places,
        )

    halo_high_other = swap(halo_high)

    def whole_window():
        halo_low = onward(low)
        return finish(
            jnp.concatenate([halo_low, halo_high], axis=0),
            jnp.concatenate([swap(halo_low), halo_high_other], axis=0),
        )

    back = lax.cond(
        wide[0, 0] > 0.0, whole_window, lambda: finish(halo_high, halo_high_other)
    )
    returned = exchange(back)
    return pl.pallas_call(
        functools.partial(final_kernel, owners=owners),
        out_shape=shape(tok_dev, model_width),
        compiler_params=params,
        name="combine",
    )(returned, slots, wout)


def solution(mesh):
    in_specs = (
        P(("round", "head", "seq"), None),
        P(),
        P(),
        P(),
        P(None, ("round", "head", "seq")),
        P("round", "seq"),
    )
    out_specs = P(("round", "head", "seq"), None)
    return jax.shard_map(shards, mesh=mesh, in_specs=in_specs, out_specs=out_specs, check_vma=False)
```

time: 127 us -> 118 us (0.929)
  starting transfers between devices: 18.9 us -> 14 us
  Pallas kernels: 39 us -> 35.4 us
  local copies, waits for them, and re-layouts: 4.7 us -> 6.12 us
    ppermute x2 -> x0, waiting for transfers between devices: 24.7 us -> none  [to_round(): return lax.ppermute(x, everyone, route)]
    all_to_all x1, waiting for transfers between devices: 0.01 us -> 21.8 us  [exchange(): x = lax.all_to_all(x, everyone, split_axis=0, concat_axis=0, tiled=True)]
    ppermute x2 -> x0, starting transfers between devices: 6.44 us -> none  [to_round(): return lax.ppermute(x, everyone, route)]
    pallas_call x1, Pallas kernels: 16.4 us -> 11.8 us  [shards(): pl.pallas_call(own_kernel, out_shape=[shape(BLOCK, width), shape(width, B...]
    ppermute x1, waiting for transfers between devices: 0.01 us -> 3.72 us  [onward(): lax.ppermute(x, 'seq', [(i, (i + 1) % owners) for i in range(owners)])]
    pallas_call x1, Pallas kernels: 1.21 us -> 3.65 us  [shards(): pl.pallas_call(functools.partial(pack_kernel, owners=owners), out_shape=s...]
    unnamed x18 -> x16, local copies, waits for them, and re-layouts: 3.76 us -> 6.12 us
    pallas_call x2 -> x3, Pallas kernels: 16 us -> 14.7 us  [the longest x1 10.9 us: finish(): pl.pallas_call(rest_kernel, out_shape=shape(rows, width), in_specs=[in_vm...]
  transfers between devices with their start and end apart: 7 -> 5, of which waited for: 3 -> 5; matrix products, arithmetic and copies ran while one was open for 2% -> 0% of each run, Pallas kernels for 16% -> 12%
where the time goes in v3:
time: 118 us
  Pallas kernels  35.4 us (30%)
  blocking collectives  33.4 us (28%)
  waiting for transfers between devices  27.5 us (23%)
  starting transfers between devices  14 us (12%)
  local copies, waits for them, and re-layouts  6.12 us (5%)
    all_to_all x1, blocking collectives, exchange(): x = lax.all_to_all(x, everyone, split_axis=0, concat_axis=0, tiled=True)  33.4 us
    all_to_all x1, waiting for transfers between devices, exchange(): x = lax.all_to_all(x, everyone, split_axis=0, concat_axis=0, tiled=True)  21.8 us
    pallas_call x1, Pallas kernels, shards(): pl.pallas_call(own_kernel, out_shape=[shape(BLOCK, width), shape(width, B...  11.8 us
    all_to_all x1, starting transfers between devices, exchange(): x = lax.all_to_all(x, everyone, split_axis=0, concat_axis=0, tiled=True)  11.5 us
    pallas_call x1, Pallas kernels, finish(): pl.pallas_call(rest_kernel, out_shape=shape(rows, width), in_specs=[in_vm...  10.9 us
    unnamed x16, local copies, waits for them, and re-layouts  6.12 us
    ppermute x1, waiting for transfers between devices, onward(): lax.ppermute(x, 'seq', [(i, (i + 1) % owners) for i in range(owners)])  3.72 us
    pallas_call x1, Pallas kernels, shards(): pl.pallas_call(functools.partial(pack_kernel, owners=owners), out_shape=s...  3.65 us
  transfers between devices with their start and end apart: 5, of which 5 were waited for; matrix products, arithmetic and copies ran while one was open for 0% of the time, Pallas kernels for 12%

profile of v3, /device:TPU:1, one launch (start us, length us, event | category | flops | bytes accessed | tf_op | source)
XLA Modules:
  0.0 118.0 jit_solution(2352591502832567946)
XLA Ops:
  0.0 0.6 pad_add_fusion.info_ref
  0.6 3.7 %pack.1 = bf16[2048,512]{1,0:T(8,128)(2,1)} custom-call(s32[3]{0:T(128)} %pad_add_fusion.info_ref, bf16[256,1024]{1,0:T(8,128)(2,1)} %tok_ref.1, s32[2,256]{1,0:T(2,128)} %pos_ref.3, s32[1,1024]{1,0:T(1,128)} %label_ref.1), custom_call_target="tpu_custom_call" | custom-call | tf_op jit(solution)/shard_map/pack/pallas_call | solution.py:536
  4.3 0.0 copy-start.5
  4.3 0.0 copy-start.6
  4.3 11.5 %all-to-all-start = ((bf16[128,16,512]{2,1,0:T(8,128)(2,1)}), bf16[128,16,512]{2,1,0:T(8,128)(2,1)S(1)}, u32[]{:S(2)}, u32[]{:S(2)}) async-start(bf16[128,16,512]{2,1,0:T(8,128)(2,1)} %bitcast.12), calls=%async_computation | async-start | bytes 4194304 | tf_op jit(solution)/shard_map/all_to_all | solution.py:533
  15.8 0.0 copy-done.5
  15.8 0.0 copy-done.6
  15.8 0.0 copy-start
  15.8 1.6 %copy-done = bf16[1024,1024]{1,0:T(8,128)(2,1)S(1)} copy-done((bf16[1024,1024]{1,0:T(8,128)(2,1)S(1)}, bf16[1024,1024]{1,0:T(8,128)(2,1)}, u32[]{:S(2)}) %copy-start) | copy-done | bytes 2097176
  17.4 1.6 %copy-done.1 = bf16[1024,1024]{1,0:T(8,128)(2,1)S(1)} copy-done((bf16[1024,1024]{1,0:T(8,128)(2,1)S(1)}, bf16[1024,1024]{1,0:T(8,128)(2,1)}, u32[]{:S(2)}) %copy-start.1) | copy-done | bytes 2097176
  19.0 1.6 %copy-done.4 = bf16[1024,1024]{1,0:T(8,128)(2,1)S(1)} copy-done((bf16[1024,1024]{1,0:T(8,128)(2,1)S(1)}, bf16[1024,1024]{1,0:T(8,128)(2,1)}, u32[]{:S(2)}) %copy-start.4) | copy-done | bytes 2097176
  20.6 2.1 %prepare.1 = (bf16[1024,512]{1,0:T(8,128)(2,1)S(1)}, bf16[512,1024]{1,0:T(8,128)(2,1)}, bf16[1024,1024]{1,0:T(8,128)(2,1)S(1)}, f32[512,128]{1,0:T(8,128)S(1)}) custom-call(s32[3]{0:T(128)S(1)} %copy-done.6, bf16[1024,1024]{1,0:T(8,128)(2,1)S(1)} %copy-done, bf16[1024,1024]{1,0:T(8,128)(2,1)S(1)} %copy-done, bf16[1024,1024]{1,0:T(8,128)(2,1)S(1)} %copy-done.1, ...), custom_call_target="tpu_custom_call" | custom-call | flops 1073741824 | bytes 8388608 | tf_op jit(solution)/shard_map/prepare/pallas_call | solution.py:553
  22.7 1.3 %copy-done.2 = bf16[1024,1024]{1,0:T(8,128)(2,1)} copy-done((bf16[1024,1024]{1,0:T(8,128)(2,1)}, bf16[1024,1024]{1,0:T(8,128)(2,1)S(1)}, u32[]{:S(2)}) %copy-start.2) | copy-done | bytes 2097176
  24.0 21.8 %all-to-all-done = bf16[128,16,512]{2,1,0:T(8,128)(2,1)S(1)} async-done(((bf16[128,16,512]{2,1,0:T(8,128)(2,1)}), bf16[128,16,512]{2,1,0:T(8,128)(2,1)S(1)}, u32[]{:S(2)}, u32[]{:S(2)}) %all-to-all-start) | async-done | bytes 2097184 | tf_op jit(solution)/shard_map/all_to_all | solution.py:533
  45.8 2.0 %sort_high.1 = (bf16[512,512]{1,0:T(8,128)(2,1)S(1)}, bf16[128,128]{1,0:T(8,128)(2,1)S(1)}, f32[16,128]{1,0:T(8,128)S(1)}, f32[1,1]{1,0:T(1,128)}) custom-call(bf16[2048,512]{1,0:T(8,128)(2,1)S(1)} %bitcast.8), custom_call_target="tpu_custom_call" | custom-call | tf_op jit(solution)/shard_map/sort_high/pallas_call | solution.py:573
  47.7 1.8 %sort_low.1 = (bf16[512,512]{1,0:T(8,128)(2,1)S(1)}, f32[1,1024]{1,0:T(1,128)S(1)}, f32[1024,128]{1,0:T(8,128)S(1)}, f32[1024,128]{1,0:T(8,128)S(1)}, f32[8,128]{1,0:T(8,128)S(1)}) custom-call(s32[3]{0:T(128)S(1)} %copy-done.6, bf16[2048,512]{1,0:T(8,128)(2,1)S(1)} %bitcast.9, f32[16,128]{1,0:T(8,128)S(1)} %get-tuple-element.108.code_ref), custom_call_target="tpu_custom_call" | custom-call | flops 1073741824 | bytes 4194304 | tf_op jit(solution)/shard_map/sort_low/pallas_call | solution.py:586
  49.5 0.1 collective-permute-start.3
  49.6 0.5 collective-permute-start.4
  50.1 1.0 collective-permute-start.2
  51.1 0.4 collective-permute-done.3.lo_ref
  51.5 0.7 collective-permute-done.4.ho_ref
  52.3 0.0 copy-done.7
  52.3 11.8 %own_block.1 = (bf16[1024,512]{1,0:T(8,128)(2,1)S(1)}, bf16[512,1024]{1,0:T(8,128)(2,1)S(1)}, f32[8,1024]{1,0:T(8,128)S(1)}, f32[2048,128]{1,0:T(8,128)S(1)}) custom-call(bf16[512,512]{1,0:T(8,128)(2,1)S(1)} %get-tuple-element.109.lm_ref, bf16[512,512]{1,0:T(8,128)(2,1)S(1)} %get-tuple-element.107.hm_ref, ...), custom_call_target="tpu_custom_call" | custom-call | flops 2147483648 | bytes 8388608 | tf_op jit(solution)/shard_map/own_block/pallas_call | solution.py:603
  64.1 3.7 %collective-permute-done.2 = bf16[512,512]{1,0:T(8,128)(2,1)S(1)} collective-permute-done((bf16[512,512]{1,0:T(8,128)(2,1)S(1)}, bf16[512,512]{1,0:T(8,128)(2,1)S(1)}, u32[]{:S(2)}, u32[]{:S(2)}) %collective-permute-start.2) | collective-permute-done | bytes 524320 | tf_op jit(solution)/shard_map/ppermute | solution.py:529
  67.8 0.9 collective-permute-start.5
  69.3 0.9 collective-permute-done.5
  70.2 11.1 %conditional.1 = (bf16[2048,512]{1,0:T(8,128)(2,1)S(1)}) conditional(s32[]{:T(128)} %bitcast.5, (bf16[512,512]{1,0:T(8,128)(2,1)S(1)}, bf16[512,512]{1,0:T(8,128)(2,1)S(1)}, bf16[1024,512]{1,0:T(8,128)(2,1)S(1)}, bf16[512,1024]{1,0:T(8,128)(2,1)S(1)}, f32[1,1024]{1,0:T(1,128)S(1)}, /*index=5*/f32[1024,128]{1,0:T(8,128)S(1)}, f32[8,128]{1,0:T(8,128)S(1)}, ...), branch_computations={%region_0.0_spmd, %region_1.0_spmd} | conditional | flops 4194304 | bytes 12583056 | solution.py:655
  70.2 10.9 %prior_block.2 = bf16[2048,512]{1,0:T(8,128)(2,1)S(1)} custom-call(bf16[512,512]{1,0:T(8,128)(2,1)S(1)} %get-tuple-element.54.xm_ref, bf16[512,512]{1,0:T(8,128)(2,1)S(1)} %get-tuple-element.55.xo_ref, bf16[1024,512]{1,0:T(8,128)(2,1)S(1)} %get-tuple-element.56.wq_ref, bf16[512,1024]{1,0:T(8,128)(2,1)S(1)} %get-tuple-element.57.wvt_ref, ...), custom_call_target="tpu_custom_call" | custom-call | tf_op jit(solution)/shard_map/cond/branch_0_fun/prior_block/pallas_call | solution.py:625
  81.3 0.0 copy-start.3
  81.3 33.4 %all_to_all.10 = bf16[128,16,512]{2,1,0:T(8,128)(2,1)S(1)} all-to-all(bf16[128,16,512]{2,1,0:T(8,128)(2,1)S(1)} %bitcast.11), channel_id=1, replica_groups=mesh['round'=2,'head'=2,'seq'=32] {'round','head','seq'}, dimensions={0} | all-to-all | bytes 4194304 | tf_op jit(solution)/shard_map/all_to_all | solution.py:533
  114.7 0.0 copy-done.3
  114.7 3.3 %combine.1 = bf16[256,1024]{1,0:T(8,128)(2,1)} custom-call(bf16[2048,512]{1,0:T(8,128)(2,1)S(1)} %bitcast.10, f32[512,128]{1,0:T(8,128)S(1)} %get-tuple-element.123.slot_ref, bf16[1024,1024]{1,0:T(8,128)(2,1)S(1)} %copy-done.3), custom_call_target="tpu_custom_call" | custom-call | tf_op jit(solution)/shard_map/combine/pallas_call | solution.py:659
  (4 shorter events, 0.0 us)
Async XLA Ops:
  4.3 11.5 %copy-start.5 = (s32[2,256]{1,0:T(2,128)S(1)}, s32[2,256]{1,0:T(2,128)}, u32[]{:S(2)}) copy-start(s32[2,256]{1,0:T(2,128)} %pos_ref.3) | copy-start | bytes 6148
  4.3 11.5 %copy-start.6 = (s32[3]{0:T(128)S(1)}, s32[3]{0:T(128)}, u32[]{:S(2)}) copy-start(s32[3]{0:T(128)} %pad_add_fusion.info_ref) | copy-start | bytes 40
  4.3 41.5 %all-to-all-start = ((bf16[128,16,512]{2,1,0:T(8,128)(2,1)}), bf16[128,16,512]{2,1,0:T(8,128)(2,1)S(1)}, u32[]{:S(2)}, u32[]{:S(2)}) async-start(bf16[128,16,512]{2,1,0:T(8,128)(2,1)} %bitcast.12), calls=%async_computation | async-start | bytes 4194304 | tf_op jit(solution)/shard_map/all_to_all | solution.py:533
  15.8 1.6 %copy-start = (bf16[1024,1024]{1,0:T(8,128)(2,1)S(1)}, bf16[1024,1024]{1,0:T(8,128)(2,1)}, u32[]{:S(2)}) copy-start(bf16[1024,1024]{1,0:T(8,128)(2,1)} %wqo_ref.1) | copy-start | bytes 6291460
  17.4 1.6 %copy-start.1 = (bf16[1024,1024]{1,0:T(8,128)(2,1)S(1)}, bf16[1024,1024]{1,0:T(8,128)(2,1)}, u32[]{:S(2)}) copy-start(bf16[1024,1024]{1,0:T(8,128)(2,1)} %wvo_ref.1) | copy-start | bytes 6291460
  19.0 1.6 %copy-start.4 = (bf16[1024,1024]{1,0:T(8,128)(2,1)S(1)}, bf16[1024,1024]{1,0:T(8,128)(2,1)}, u32[]{:S(2)}) copy-start(bf16[1024,1024]{1,0:T(8,128)(2,1)} %wo_ref.1) | copy-start | bytes 6291460
  22.7 1.3 %copy-start.2 = (bf16[1024,1024]{1,0:T(8,128)(2,1)}, bf16[1024,1024]{1,0:T(8,128)(2,1)S(1)}, u32[]{:S(2)}) copy-start(bf16[1024,1024]{1,0:T(8,128)(2,1)S(1)} %get-tuple-element.124.w_ref) | copy-start | bytes 6291460
  47.7 4.5 %copy-start.7 = (bf16[512,1024]{1,0:T(8,128)(2,1)S(1)}, bf16[512,1024]{1,0:T(8,128)(2,1)}, u32[]{:S(2)}) copy-start(bf16[512,1024]{1,0:T(8,128)(2,1)} %get-tuple-element.111.wvt_ref) | copy-start | bytes 3145732
  49.5 2.0 %collective-permute-start.3 = (bf16[512,512]{1,0:T(8,128)(2,1)S(1)}, bf16[512,512]{1,0:T(8,128)(2,1)S(1)}, u32[]{:S(2)}, u32[]{:S(2)}) collective-permute-start(bf16[512,512]{1,0:T(8,128)(2,1)S(1)} %get-tuple-element.109.lm_ref), channel_id=1, source_target_pairs={{0,64},{64,0},{1,65},{65,1},{2,66},{66,2},{3,67},{67,3},{4,68},{68... | collective-permute-start | bytes 1572872 | tf_op jit(solution)/shard_map/ppermute | solution.py:526
  49.6 2.6 %collective-permute-start.4 = (bf16[512,512]{1,0:T(8,128)(2,1)S(1)}, bf16[512,512]{1,0:T(8,128)(2,1)S(1)}, u32[]{:S(2)}, u32[]{:S(2)}) collective-permute-start(bf16[512,512]{1,0:T(8,128)(2,1)S(1)} %get-tuple-element.107.hm_ref), channel_id=1, source_target_pairs={{0,64},{64,0},{1,65},{65,1},{2,66},{66,2},{3,67},{67,3},{4,68},{68... | collective-permute-start | bytes 1572872 | tf_op jit(solution)/shard_map/ppermute | solution.py:526
  50.1 17.7 %collective-permute-start.2 = (bf16[512,512]{1,0:T(8,128)(2,1)S(1)}, bf16[512,512]{1,0:T(8,128)(2,1)S(1)}, u32[]{:S(2)}, u32[]{:S(2)}) collective-permute-start(bf16[512,512]{1,0:T(8,128)(2,1)S(1)} %get-tuple-element.107.hm_ref), channel_id=1, source_target_pairs={{0,1},{1,2},{2,3},{3,4},{4,5},{5,6},{6,7},{7,8},{8,9},{9,10},{10,1... | collective-permute-start | bytes 1572872 | tf_op jit(solution)/shard_map/ppermute | solution.py:529
  67.8 2.4 %collective-permute-start.5 = (bf16[512,512]{1,0:T(8,128)(2,1)S(1)}, bf16[512,512]{1,0:T(8,128)(2,1)S(1)}, u32[]{:S(2)}, u32[]{:S(2)}) collective-permute-start(bf16[512,512]{1,0:T(8,128)(2,1)S(1)} %collective-permute-done.2), channel_id=1, source_target_pairs={{0,64},{64,0},{1,65},{65,1},{2,66},{66,2},{3,67},{67,3},{4,68},{68... | collective-permute-start | bytes 1572872 | tf_op jit(solution)/shard_map/ppermute | solution.py:526
  81.3 33.4 %copy-start.3 = (bf16[1024,1024]{1,0:T(8,128)(2,1)S(1)}, bf16[1024,1024]{1,0:T(8,128)(2,1)}, u32[]{:S(2)}) copy-start(bf16[1024,1024]{1,0:T(8,128)(2,1)} %copy-done.2) | copy-start | bytes 6291460

commit v4 on v3

--- a/solution.py
+++ b/solution.py
@@ -15,8 +15,9 @@
 SLOTS = 16
 META = 14
 LABELS = 15
+HALO = 3 * TILE
 SHIFT = 65536.0
-STEP = 256
+STEP = 1024
 
 LOG2E = 1.4426950408889634
 SELF_PENALTY = -100000.0 * LOG2E
@@ -27,6 +28,7 @@
 F32 = jnp.float32
 I32 = jnp.int32
 NT = (((1,), (1,)), ((), ()))
+AXES = ("round", "head", "seq")
 
 
 def iota(shape, dim):
@@ -49,9 +51,22 @@
     return slice(h * DH * wide, (h + 1) * DH * wide)
 
 
+def chip_of(block):
+    y = block >> 3
+    ring = (block & 7) ^ ((y & 1) * 7)
+    return (y << 3) | (ring & 4) | ((ring & 3) ^ ((ring >> 2) * 3))
+
+
+def block_of(chip):
+    y = chip >> 3
+    x = (chip >> 2) & 1
+    ring = (x << 2) | ((chip & 3) ^ (x * 3))
+    return (y << 3) | (ring ^ ((y & 1) * 7))
+
+
 def slots_of(pos, owners):
     count = pos.shape[1]
-    dest = pos >> 10
+    dest = chip_of(pos >> 10)
     hot = iota((owners, count), 0) == dest
     earlier = mask(iota((count, count), 0) < iota((count, count), 1))
     before = mm(mask(hot), earlier)
@@ -59,19 +74,22 @@
     return hot, dest * SLOTS + rank
 
 
-def pack_kernel(info_ref, tok_ref, pos_ref, label_ref, out_ref, buf_ref, sem_ref, *, owners):
+def pack_kernel(tok_ref, pos_ref, label_ref, out_ref, buf_ref, sem_ref, *, owners):
     count = tok_ref.shape[0]
     width = out_ref.shape[1]
     rows = owners * SLOTS
     tokens = tok_ref[...]
     half = BLOCK // 2
     first, last = label_ref[0:1, 0:1], label_ref[0:1, BLOCK - 1 : BLOCK]
-    middle = label_ref[0:1, half - 1 : half]
-    marked = jnp.where(last == 0, jnp.minimum(first, middle), jnp.abs(middle - last))
-    wide = jnp.where(jnp.broadcast_to(marked, (owners, 128)) == 0, 1.0, 0.0)
+    wide = []
+    for held in (HALO, half):
+        middle = label_ref[0:1, BLOCK - held - 1 : BLOCK - held]
+        marked = jnp.where(last == 0, jnp.minimum(first, middle), jnp.abs(middle - last))
+        wide.append(jnp.where(jnp.broadcast_to(marked, (owners, 128)) == 0, 1.0, 0.0))
     label = label_ref[...]
     label = ((128 + (label & 127)) << (label >> 7)).astype(F32)
-    label = jnp.where(info_ref[1] == 0, label[:, :half], label[:, half:])
+    core, head, seq = (lax.axis_index(axis) for axis in AXES)
+    label = jnp.where(head == 0, label[:, :half], label[:, half:])
     label = jnp.broadcast_to(label, (SLOTS, half))
     copies = []
     for r in range(2):
@@ -84,7 +102,9 @@
         code = jnp.where((value & 1) == 0, (within >> 5) + 1, within & 31)
         code = jnp.where((value >> 1) == rank, code, 0).astype(F32).astype(BF)
         places = mm_nt(mask(hot), code)
-        places = jnp.where(iota((owners, 128), 1) == 2 * SLOTS, wide, places).astype(BF)
+        lane = iota((owners, 128), 1)
+        places = jnp.where(lane == 2 * SLOTS, wide[0], places)
+        places = jnp.where(lane == 2 * SLOTS + 1, wide[1], places).astype(BF)
         at_meta = mask(iota((rows, owners), 0) == iota((rows, owners), 1) * SLOTS + META)
         extra = mm(at_meta, places)
         for a in range(2):
@@ -93,12 +113,12 @@
             buf_ref[at : at + rows, 0:128] = (body[:, 0:128] + extra).astype(BF)
             buf_ref[at : at + rows, 128:width] = body[:, 128:].astype(BF)
 
-        @pl.when(info_ref[0] == r)
+        @pl.when(core == r)
         def _():
             for a in range(2):
                 for ahead in range(2):
-                    block = (info_ref[2] + ahead) & (owners - 1)
-                    at = pl.multiple_of((a * 2 + r) * rows + block * SLOTS, SLOTS)
+                    chip = chip_of((seq + ahead) & (owners - 1))
+                    at = pl.multiple_of((a * 2 + r) * rows + chip * SLOTS, SLOTS)
                     old = buf_ref[pl.ds(at, SLOTS), :].astype(F32)
                     new = jnp.where(iota((SLOTS, half), 0) == LABELS, label, old)
                     buf_ref[pl.ds(at, SLOTS), :] = new.astype(BF)
@@ -115,21 +135,32 @@
 
 
 def prepare_kernel(
-    info_ref, wqm_ref, wqo_ref, wvm_ref, wvo_ref, wo_ref, pos_ref,
-    wq_ref, wvt_ref, wout_ref, slot_ref, *, owners,
+    wqk_ref, wv_ref, wo_ref, pos_ref, wq_ref, wvt_ref, wout_ref, slot_ref,
+    wv_buf_ref, sem_ref, *, owners,
 ):
-    width = wqm_ref.shape[0]
-    wq_ref[0:width, :] = wqm_ref[...]
-    wq_ref[width:, :] = wqo_ref[...]
-    wvt_ref[:, 0:width] = jnp.transpose(wvm_ref[...])
-    wvt_ref[:, width:] = jnp.transpose(wvo_ref[...])
-    wout_ref[...] = wo_ref[...]
+    width = wq_ref.shape[1]
+    core = lax.axis_index("round")
+    cols = pl.ds(pl.multiple_of(core * width, width), width)
+    copies = [pltpu.make_async_copy(wo_ref, wout_ref, sem_ref.at[4])]
+    for part in range(2):
+        source = core + part - 2 * part * core
+        rows = pl.ds(pl.multiple_of(source * width, width), width)
+        there = pl.ds(part * width, width)
+        copies += [
+            pltpu.make_async_copy(wqk_ref.at[rows, cols], wq_ref.at[there], sem_ref.at[part]),
+            pltpu.make_async_copy(wv_ref.at[rows, cols], wv_buf_ref.at[there], sem_ref.at[2 + part]),
+        ]
+    for copy in copies:
+        copy.start()
     count = pos_ref.shape[1]
     for r in range(2):
         slot = slots_of(pos_ref[r : r + 1, :], owners)[1].astype(F32)
         slot_ref[r * count : (r + 1) * count, :] = jnp.transpose(
             jnp.broadcast_to(slot, (128, count))
         )
+    for copy in copies:
+        copy.wait()
+    wvt_ref[...] = jnp.transpose(wv_buf_ref[...])
 
 
 def meta_of(x_ref):
@@ -150,54 +181,53 @@
     return jnp.sum(codes.reshape(count // 8, 8, 128), axis=1)
 
 
-def place_columns(meta, first, rows):
+def place_columns(meta):
     count = meta.shape[0]
-    slot = iota((rows, count), 0) + first
-    source = mask((slot >> 4) == iota((rows, count), 1))
-    values = mm(source, meta)
-    lane = iota((rows, 128), 1)
-    keep = (lane >> 1) == (iota((rows, 128), 0) & (SLOTS - 1))
-    values = jnp.where(keep, values, 0.0).astype(BF)
+    rows = count * SLOTS
+    values = jnp.broadcast_to(meta.astype(F32)[:, None, :], (count, SLOTS, 128))
+    keep = (iota((rows, 128), 1) >> 1) == (iota((rows, 128), 0) & (SLOTS - 1))
+    values = jnp.where(keep, values.reshape(rows, 128), 0.0).astype(BF)
     weight = jnp.where((iota((128, 128), 0) & 1) == 0, 32.0, 1.0).astype(BF)
     return mm(values, weight)
 
 
 def sorted_rows(x_ref, code_ref, out_ref, first):
-    step = 256
-    chunks = code_ref.shape[0]
-    for start in range(0, out_ref.shape[0], step):
-        position = (iota((step, 128), 0) + (first + start + 32)).astype(F32)
-        picks = [
-            mask(position == jnp.broadcast_to(code_ref[q : q + 1, :], (step, 128)))
-            for q in range(chunks)
-        ]
-        picks = jnp.concatenate(picks, axis=1)
-        out_ref[start : start + step, :] = mm(picks, x_ref[...]).astype(BF)
+    rows = out_ref.shape[0]
+    position = (iota((rows, 128), 0) + (first + 32)).astype(F32)
+    picks = [
+        mask(position == jnp.broadcast_to(code_ref[q : q + 1, :], (rows, 128)))
+        for q in range(code_ref.shape[0])
+    ]
+    out_ref[...] = mm(jnp.concatenate(picks, axis=1), x_ref[...]).astype(BF)
 
 
 def sort_high_kernel(x_ref, high_ref, meta_ref, code_ref, wide_ref):
     meta = meta_of(x_ref)
     meta_ref[...] = meta
-    flags = jnp.where(iota(meta.shape, 1) == 2 * SLOTS, meta.astype(F32), 0.0)
-    wide_ref[...] = jnp.max(jnp.max(flags, axis=1, keepdims=True), axis=0, keepdims=True)
+    lane = iota(meta.shape, 1)
+    flags = jnp.where((lane >> 1) == SLOTS, meta.astype(F32), 0.0)
+    flags = jnp.max(flags, axis=0, keepdims=True)
+    wide_ref[...] = jnp.sum(flags, axis=1, keepdims=True)
     code_ref[...] = place_rows(meta)
-    sorted_rows(x_ref, code_ref, high_ref, high_ref.shape[0])
+    sorted_rows(x_ref, code_ref, high_ref, BLOCK - high_ref.shape[0])
 
 
 def sort_low_kernel(
-    info_ref, x_ref, code_ref, low_ref, row_ref, col_ref, prior_col_ref, flag_ref, *, owners
+    x_ref, code_ref, low_ref, row_ref, col_ref, prior_col_ref, flag_ref, *, owners
 ):
+    my_round, me = lax.axis_index("head"), block_of(lax.axis_index("seq"))
+
     def labels(block):
         parts = []
         for half in range(2):
-            source = (info_ref[1] * 2 + half) * owners + block
+            source = (my_round * 2 + half) * owners + block
             rows = x_ref[pl.ds(pl.multiple_of(source * SLOTS, SLOTS), SLOTS), :].astype(F32)
             at_labels = iota(rows.shape, 0) == LABELS
             parts.append(jnp.sum(jnp.where(at_labels, rows, 0.0), axis=0, keepdims=True))
         return jnp.concatenate(parts, axis=1)
 
-    own = labels(info_ref[2])
-    prior = labels((info_ref[2] + owners - 1) & (owners - 1))
+    own = labels(me)
+    prior = labels((me + owners - 1) & (owners - 1))
     row_ref[...] = own
     col_ref[...] = jnp.transpose(jnp.broadcast_to(own, (TILE, BLOCK)))
     prior_col_ref[...] = jnp.transpose(jnp.broadcast_to(prior, (TILE, BLOCK)))
@@ -277,7 +307,7 @@
         vt_ref[first + DH : first + DH + 16, at : at + rows] = jnp.ones((16, rows), BF)
 
 
-def attend(keys, queries, values, key_label, query_label, diagonal):
+def score(keys, queries, key_label, query_label, diagonal):
     count, span = keys.shape[0], queries.shape[0]
     scores = mm_nt(keys, jnp.concatenate([queries, queries], axis=1))
     match = jnp.concatenate([key_label] * (span // TILE), axis=1) == query_label
@@ -291,9 +321,27 @@
     elif diagonal is not None:
         apart = iota((count, span), 0) - iota((count, span), 1)
         scores = jnp.where(apart == diagonal, SELF_PENALTY, scores)
+    return scores
+
+
+def weigh(scores, values):
     top = jnp.max(scores, axis=0, keepdims=True)
     result = mm(values, jnp.exp2(scores - top).astype(BF))
     return result[0:DH], top, result[DH : DH + 1]
+
+
+def ahead(work, first, second, depth):
+    pending = []
+    for item in work:
+        pending.append((item, first(item)))
+        if len(pending) > depth:
+            second(*pending.pop(0))
+    for entry in pending:
+        second(*entry)
+
+
+def late_span(bits, i):
+    return ((bits >> (8 + SPAN // TILE * i)) & (2 ** (SPAN // TILE) - 1)) != 0
 
 
 def sums_of(lse, heads):
@@ -319,53 +367,47 @@
 
 def own_kernel(
     lm_ref, hm_ref, lo_ref, ho_ref, wq_ref, wvt_ref, row_ref, col_ref, flag_ref, meta_ref,
-    q_ref, out_ref, lse_ref, place_ref, key_ref, vt_ref,
+    q_ref, out_ref, lse_ref, place_ref, early_ref, key_ref, vt_ref,
 ):
-    half = lm_ref.shape[0]
+    first_rows = lm_ref.shape[0]
     heads = q_ref.shape[1] // DH
     bits = flag_bits(flag_ref)
-    for m_part, o_part, at in ((hm_ref, ho_ref, half), (lm_ref, lo_ref, 0)):
+    for m_part, o_part, at in ((hm_ref, ho_ref, first_rows), (lm_ref, lo_ref, 0)):
         queries, parts, values = project(m_part[...], o_part[...], wq_ref, wvt_ref)
-        q_ref[at : at + half, :] = queries
+        q_ref[at : at + queries.shape[0], :] = queries
         store_keys(at, parts, values, key_ref, vt_ref)
+    place_ref[...] = place_columns(meta_ref[...])
     lse_row = iota((8, SPAN), 0)
 
-    def put(at, h, found, lse_tile):
-        result, top, total = found
-        out_ref[head_cols(h), pl.ds(at, SPAN)] = (result * (1.0 / total)).astype(BF)
-        return jnp.where(lse_row == h, top + jnp.log2(total), lse_tile)
-
-    def span(at, start, size, diagonal):
-        query_label = row_ref[0:1, pl.ds(at, SPAN)]
-        key_label = col_ref[pl.ds(start, size), :]
-        lse_tile = jnp.zeros((8, SPAN), F32)
-        for h in range(heads):
-            found = attend(
-                key_ref[pl.ds(start, size), head_cols(h, 2)],
-                q_ref[pl.ds(at, SPAN), head_cols(h)],
-                vt_ref[value_rows(h), pl.ds(start, size)],
-                key_label, query_label, diagonal,
+    def spans(work, depth):
+        tiles = {}
+
+        def first(item):
+            h, at, start, size, diagonal = item
+            return score(
+                key_ref[pl.ds(start, size), head_cols(h, 2)], q_ref[pl.ds(at, SPAN), head_cols(h)],
+                col_ref[pl.ds(start, size), :], row_ref[0:1, pl.ds(at, SPAN)], diagonal,
             )
-            lse_tile = put(at, h, found, lse_tile)
-        lse_ref[:, pl.ds(at, SPAN)] = lse_tile
+
+        def second(item, scores):
+            h, at, start, size, _ = item
+            result, top, total = weigh(scores, vt_ref[value_rows(h), pl.ds(start, size)])
+            out_ref[head_cols(h), pl.ds(at, SPAN)] = (result * (1.0 / total)).astype(BF)
+            tile = tiles.pop("lse") if h else jnp.zeros((8, SPAN), F32)
+            tiles["lse"] = jnp.where(lse_row == h, top + jnp.log2(total), tile)
+            if h == heads - 1:
+                lse_ref[:, pl.ds(at, SPAN)] = tiles.pop("lse")
+
+        ahead(work, first, second, depth)
+
+    work = []
+    for at in range(BLOCK - SPAN, -1, -SPAN):
+        start, stop = max(at - TILE, 0), min(at + SPAN + TILE, BLOCK)
+        work += [(h, at, start, stop - start, at - start) for h in range(heads)]
+    spans(work, 3)
 
     def flag(k):
         return (bits >> k) & 1
-
-    @pl.when(flag(0) == 0)
-    def _():
-        span(0, 0, SPAN + TILE, 0)
-
-    @pl.loop(1, SPANS - 1)
-    def _(i):
-        @pl.when(flag(i) == 0)
-        def _():
-            at = pl.multiple_of(i * SPAN, SPAN)
-            span(at, pl.multiple_of(at - TILE, TILE), SPAN + 2 * TILE, TILE)
-
-    @pl.when(flag(SPANS - 1) == 0)
-    def _():
-        span(BLOCK - SPAN, BLOCK - SPAN - TILE, SPAN + TILE, TILE)
 
     @pl.loop(0, SPANS)
     def _(i):
@@ -375,29 +417,39 @@
         def _():
             size = SPAN + 4 * TILE
             start = pl.multiple_of(jnp.clip(at - 2 * TILE, 0, BLOCK - size), TILE)
-            span(at, start, size, at - start)
+            spans([(h, at, start, size, at - start) for h in range(heads)], 2)
 
         @pl.when(flag(4 + i) != 0)
         def _():
-            span(at, 0, BLOCK, at)
-
-    @pl.loop(0, place_ref.shape[0] // STEP)
-    def _(t):
-        at = pl.multiple_of(t * STEP, STEP)
-        place_ref[pl.ds(at, STEP), :] = place_columns(meta_ref[...], at, STEP)
+            spans([(h, at, 0, BLOCK, at) for h in range(heads)], 0)
+
+    late = [jnp.where(late_span(bits, i), 4.0 * BLOCK, 0.0) for i in range(SPANS)]
+    sums = sums_of(lse_ref[...], heads)
+    for at in range(0, early_ref.shape[0], STEP):
+        codes = place_ref[at : at + STEP, :]
+        lane = (iota((STEP, 128), 1) + 32).astype(F32)
+        pick = jnp.concatenate(
+            [mask(codes == lane + (float(c) + late[c // SPAN])) for c in range(0, BLOCK, 128)],
+            axis=1,
+        )
+        early_ref[at : at + STEP, :] = packed_rows(pick, out_ref[...], sums).astype(BF)
 
 
 def rest_kernel(
     xm_ref, xo_ref, wq_ref, wvt_ref, row_ref, col_ref, flag_ref,
-    q_ref, own_ref, own_lse_ref, place_ref, send_ref,
-    out_ref, lse_ref, sums_ref, key_ref, vt_ref, buf_ref, sem_ref,
+    q_ref, own_ref, own_lse_ref, place_ref, early_ref, send_ref,
+    out_ref, lse_ref, key_ref, vt_ref, buf_ref, sem_ref,
 ):
     halo = xm_ref.shape[0]
     heads = q_ref.shape[1] // DH
     bits = flag_bits(flag_ref)
     lse_row = iota((8, TILE), 0)
-    out_ref[...] = own_ref[...]
     lse_ref[...] = own_lse_ref[...]
+    for i in range(SPANS):
+
+        @pl.when(late_span(bits, i))
+        def _():
+            out_ref[:, i * SPAN : (i + 1) * SPAN] = own_ref[:, i * SPAN : (i + 1) * SPAN]
 
     def merge(size):
         first = halo - size
@@ -409,59 +461,56 @@
             @pl.when(((bits >> (8 + i)) & 1) != 0)
             def _():
                 at = pl.multiple_of(i * TILE, TILE)
-                lse_tile = lse_ref[:, pl.ds(at, TILE)]
-                for h in range(heads):
-                    result, top, total = attend(
-                        key_ref[first:, head_cols(h, 2)],
-                        q_ref[pl.ds(at, TILE), head_cols(h)],
-                        vt_ref[value_rows(h), first:],
+                tiles = [lse_ref[:, pl.ds(at, TILE)]]
+
+                def first_step(h):
+                    return score(
+                        key_ref[first:, head_cols(h, 2)], q_ref[pl.ds(at, TILE), head_cols(h)],
                         col_ref[BLOCK - size :, :], row_ref[0:1, pl.ds(at, TILE)], None,
                     )
-                    here, there = lse_tile[h : h + 1, :], top + jnp.log2(total)
+
+                def second_step(h, scores):
+                    result, top, total = weigh(scores, vt_ref[value_rows(h), first:])
+                    here, there = tiles[0][h : h + 1, :], top + jnp.log2(total)
                     largest = jnp.maximum(here, there)
                     kept, added = jnp.exp2(here - largest), jnp.exp2(there - largest)
                     own = out_ref[head_cols(h), pl.ds(at, TILE)].astype(F32)
                     merged = (kept * own + result * (added / total)) * (1.0 / (kept + added))
                     out_ref[head_cols(h), pl.ds(at, TILE)] = merged.astype(BF)
                     new = largest + jnp.log2(kept + added)
-                    lse_tile = jnp.where(lse_row == h, new, lse_tile)
-                lse_ref[:, pl.ds(at, TILE)] = lse_tile
-
-    size_class = bits >> 16
-
-    @pl.when(size_class == 0)
-    def _():
-        merge(TILE)
-
-    @pl.when(size_class == 1)
-    def _():
-        merge(3 * TILE)
-
-    @pl.when(size_class > 1)
-    def _():
+                    tiles[0] = jnp.where(lse_row == h, new, tiles[0])
+
+                ahead(range(heads), first_step, second_step, 3)
+                lse_ref[:, pl.ds(at, TILE)] = tiles[0]
+
+    if halo > HALO:
         merge(halo)
-
-    sums_ref[...] = sums_of(lse_ref[...], heads)
-    steps = send_ref.shape[0] // STEP
-
-    def sending(t):
-        piece = pl.ds(pl.multiple_of(t * STEP, STEP), STEP)
-        return pltpu.make_async_copy(buf_ref.at[piece], send_ref.at[piece], sem_ref.at[t])
-
-    @pl.loop(0, steps)
-    def _(t):
-        at = pl.multiple_of(t * STEP, STEP)
-        codes = place_ref[pl.ds(at, STEP), :]
-        lane = (iota((STEP, 128), 1) + 32).astype(F32)
-        pick = jnp.concatenate(
-            [mask(codes == lane + float(c)) for c in range(0, BLOCK, 128)], axis=1
-        )
-        buf_ref[pl.ds(at, STEP), :] = packed_rows(pick, out_ref[...], sums_ref[...]).astype(BF)
-        sending(t).start()
-
-    @pl.loop(0, steps)
-    def _(t):
-        sending(t).wait()
+    else:
+        pl.when(bits >> 16 == 0)(lambda: merge(TILE))
+        pl.when(bits >> 16 != 0)(lambda: merge(halo))
+
+    copies = []
+    for t in range(send_ref.shape[0] // STEP):
+        piece = pl.ds(t * STEP, STEP)
+        buf_ref[piece, :] = early_ref[piece, :]
+
+        @pl.loop(0, SPANS)
+        def _(i):
+            @pl.when(late_span(bits, i))
+            def _():
+                cols = pl.ds(pl.multiple_of(i * SPAN, SPAN), SPAN)
+                codes = place_ref[piece, :]
+                lane = (iota((STEP, 128), 1) + (32 + i * SPAN)).astype(F32)
+                pick = jnp.concatenate(
+                    [mask(codes == lane + float(c)) for c in range(0, SPAN, 128)], axis=1
+                )
+                rows = packed_rows(pick, out_ref[:, cols], sums_of(lse_ref[:, cols], heads))
+                buf_ref[piece, :] = (buf_ref[piece, :].astype(F32) + rows).astype(BF)
+
+        copies.append(pltpu.make_async_copy(buf_ref.at[piece], send_ref.at[piece], sem_ref.at[t]))
+        copies[-1].start()
+    for copy in copies:
+        copy.wait()
 
 
 def final_kernel(x_ref, slot_ref, w_ref, out_ref, *, owners):
@@ -503,17 +552,13 @@
 def shards(tokens, w_qk, w_v, w_out, positions, buckets):
     tok_dev, model_width = tokens.shape
     owners = lax.axis_size("seq")
-    everyone = ("round", "head", "seq")
     total = 2 * 2 * owners
     width = model_width // 2
     heads = width // DH
     rows = total * SLOTS
-    half = BLOCK // 2
-    info = jnp.stack([lax.axis_index(axis) for axis in everyone]).astype(I32)
     params = pltpu.CompilerParams(vmem_limit_bytes=40 * 2**20)
     alone = pltpu.CompilerParams(vmem_limit_bytes=60 * 2**20)
     in_vmem = pl.BlockSpec(memory_space=pltpu.VMEM)
-    in_smem = pl.BlockSpec(memory_space=pltpu.SMEM)
     in_hbm = pl.BlockSpec(memory_space=pltpu.HBM)
 
     def shape(*dims, dtype=BF):
@@ -526,30 +571,24 @@
         return lax.ppermute(x, "round", [(0, 1), (1, 0)])
 
     def onward(x):
-        return lax.ppermute(x, "seq", [(i, (i + 1) % owners) for i in range(owners)])
+        route = [(chip_of(i), chip_of((i + 1) % owners)) for i in range(owners)]
+        return lax.ppermute(x, "seq", route)
 
     def exchange(x):
         x = x.reshape(total, SLOTS, width)
-        x = lax.all_to_all(x, everyone, split_axis=0, concat_axis=0, tiled=True)
+        x = lax.all_to_all(x, AXES, split_axis=0, concat_axis=0, tiled=True)
         return x.reshape(rows, width)
 
     packed = pl.pallas_call(
         functools.partial(pack_kernel, owners=owners),
         out_shape=shape(rows, width),
-        in_specs=[in_smem] + [in_vmem] * 3,
         out_specs=in_hbm,
         scratch_shapes=[pltpu.VMEM((rows, width), BF), pltpu.SemaphoreType.DMA((4,))],
         compiler_params=alone,
         name="pack",
-    )(info, tokens, positions, buckets)
+    )(tokens, positions, buckets)
     arrived = exchange(packed)
 
-    def weight(other):
-        return pl.BlockSpec(
-            (width, width), lambda i, s: (1 - s[0] if other else s[0], s[0])
-        )
-
-    weights = [weight(False), weight(True)] * 2
     wq, wvt, wout, slots = pl.pallas_call(
         functools.partial(prepare_kernel, owners=owners),
         out_shape=[
@@ -558,22 +597,19 @@
             shape(model_width, model_width),
             shape(2 * tok_dev, 128, dtype=F32),
         ],
-        grid_spec=pltpu.PrefetchScalarGridSpec(
-            num_scalar_prefetch=1,
-            grid=(1,),
-            in_specs=weights + [in_vmem] * 2,
-            out_specs=[in_vmem] * 4,
-        ),
+        in_specs=[in_hbm] * 3 + [in_vmem],
+        out_specs=[in_vmem] * 4,
+        scratch_shapes=[pltpu.VMEM((model_width, width), BF), pltpu.SemaphoreType.DMA((5,))],
         compiler_params=params,
         cost_estimate=cost(2**30, 8 * 2**20),
         name="prepare",
-    )(info, w_qk, w_qk, w_v, w_v, w_out, positions)
+    )(w_qk, w_v, w_out, positions)
     arrived, wq, wvt, wout, slots = lax.optimization_barrier((arrived, wq, wvt, wout, slots))
 
     high, meta, codes, wide = pl.pallas_call(
         sort_high_kernel,
         out_shape=[
-            shape(half, width),
+            shape(HALO, width),
             shape(total, 128),
             shape(total // 8, 128, dtype=F32),
             shape(1, 1, dtype=F32),
@@ -581,58 +617,56 @@
         compiler_params=params,
         name="sort_high",
     )(arrived)
-    halo_high = onward(high)
+    halo = onward(high)
     high_other = swap(high)
     low, label_row, label_col, prior_col, flags = pl.pallas_call(
         functools.partial(sort_low_kernel, owners=owners),
         out_shape=[
-            shape(half, width),
+            shape(BLOCK - HALO, width),
             shape(1, BLOCK, dtype=F32),
             shape(BLOCK, TILE, dtype=F32),
             shape(BLOCK, TILE, dtype=F32),
             shape(8, 128, dtype=F32),
         ],
-        in_specs=[in_smem] + [in_vmem] * 2,
-        out_specs=[in_vmem] * 5,
         compiler_params=params,
-        cost_estimate=cost(2 * half * rows * width, 4 * 2**20),
+        cost_estimate=cost(4 * BLOCK * rows * width, 4 * 2**20),
         name="sort_low",
-    )(info, arrived, codes)
+    )(arrived, codes)
     low_other = swap(low)
 
-    queries, own_out, own_lse, places = pl.pallas_call(
+    queries, own_out, own_lse, places, early = pl.pallas_call(
         own_kernel,
         out_shape=[
             shape(BLOCK, width),
             shape(width, BLOCK),
             shape(8, BLOCK, dtype=F32),
             shape(rows, 128, dtype=F32),
+            shape(rows, width),
         ],
         in_specs=[in_vmem] * 10,
-        out_specs=[in_vmem] * 4,
+        out_specs=[in_vmem] * 5,
         scratch_shapes=[
             pltpu.VMEM((BLOCK, 2 * width), BF),
             pltpu.VMEM((heads * (DH + 16), BLOCK), BF),
         ],
         compiler_params=params,
-        cost_estimate=cost(8 * BLOCK * width * width, 8 * 2**20),
+        cost_estimate=cost(2**20, 2**20),
         name="own_block",
     )(low, high, low_other, high_other, wq, wvt, label_row, label_col, flags, meta)
-    halo_high, own_lse = lax.optimization_barrier((halo_high, own_lse))
+    halo, own_lse = lax.optimization_barrier((halo, own_lse))
 
     def finish(halo_mine, halo_other):
-        halo = halo_mine.shape[0]
+        size = halo_mine.shape[0]
         return pl.pallas_call(
             rest_kernel,
             out_shape=shape(rows, width),
-            in_specs=[in_vmem] * 11,
+            in_specs=[in_vmem] * 12,
             out_specs=in_hbm,
             scratch_shapes=[
                 pltpu.VMEM((width, BLOCK), BF),
                 pltpu.VMEM((8, BLOCK), F32),
-                pltpu.VMEM((128, BLOCK), BF),
-                pltpu.VMEM((halo, 2 * width), BF),
-                pltpu.VMEM((heads * (DH + 16), halo), BF),
+                pltpu.VMEM((size, 2 * width), BF),
+                pltpu.VMEM((heads * (DH + 16), size), BF),
                 pltpu.VMEM((rows, width), BF),
                 pltpu.SemaphoreType.DMA((rows // STEP,)),
             ],
@@ -640,21 +674,19 @@
             name="prior_block",
         )(
             halo_mine, halo_other, wq, wvt, label_row, prior_col, flags,
-            queries, own_out, own_lse, places,
+            queries, own_out, own_lse, places, early,
         )
 
-    halo_high_other = swap(halo_high)
-
-    def whole_window():
-        halo_low = onward(low)
+    halo_other = swap(halo)
+
+    def more(rows):
+        rest = onward(rows)
         return finish(
-            jnp.concatenate([halo_low, halo_high], axis=0),
-            jnp.concatenate([swap(halo_low), halo_high_other], axis=0),
+            jnp.concatenate([rest, halo], axis=0),
+            jnp.concatenate([swap(rest), halo_other], axis=0),
         )
 
-    back = lax.cond(
-        wide[0, 0] > 0.0, whole_window, lambda: finish(halo_high, halo_high_other)
-    )
+    back = lax.cond(wide[0, 0] > 0.0, lambda: more(low), lambda: finish(halo, halo_other))
     returned = exchange(back)
     return pl.pallas_call(
         functools.partial(final_kernel, owners=owners),

time: 118 us -> 107 us (0.907)
  Pallas kernels: 35.4 us -> 29.7 us
  waiting for transfers between devices: 27.5 us -> 23.8 us
    pallas_call x1, Pallas kernels: 10.9 us -> 6.67 us  [finish(): pl.pallas_call(rest_kernel, out_shape=shape(rows, width), in_specs=[in_vm...]
    ppermute x1, waiting for transfers between devices: 3.72 us -> 0.01 us  [onward(): return lax.ppermute(x, 'seq', route)]
    unnamed x16 -> x14, local copies, waits for them, and re-layouts: 6.12 us -> 6.12 us
  transfers between devices with their start and end apart: 5 -> 5, of which waited for: 5 -> 3; matrix products, arithmetic and copies ran while one was open for 0% -> 0% of each run, Pallas kernels for 12% -> 12%
where the time goes in v4:
time: 107 us
  blocking collectives  33.2 us (31%)
  Pallas kernels  29.7 us (28%)
  waiting for transfers between devices  23.8 us (22%)
  starting transfers between devices  13.3 us (12%)
  local copies, waits for them, and re-layouts  6.12 us (6%)
    all_to_all x1, blocking collectives, exchange(): x = lax.all_to_all(x, AXES, split_axis=0, concat_axis=0, tiled=True)  33.2 us
    all_to_all x1, waiting for transfers between devices, exchange(): x = lax.all_to_all(x, AXES, split_axis=0, concat_axis=0, tiled=True)  21.7 us
    all_to_all x1, starting transfers between devices, exchange(): x = lax.all_to_all(x, AXES, split_axis=0, concat_axis=0, tiled=True)  11.5 us
    pallas_call x1, Pallas kernels, shards(): pl.pallas_call(own_kernel, out_shape=[shape(BLOCK, width), shape(width, B...  11 us
    pallas_call x1, Pallas kernels, finish(): pl.pallas_call(rest_kernel, out_shape=shape(rows, width), in_specs=[in_vm...  6.67 us
    unnamed x14, local copies, waits for them, and re-layouts  6.12 us
    pallas_call x1, Pallas kernels, shards(): pl.pallas_call(functools.partial(pack_kernel, owners=owners), out_shape=s...  3.67 us
    pallas_call x1, Pallas kernels, shards(): pl.pallas_call(functools.partial(final_kernel, owners=owners), out_shape=...  3.32 us
  transfers between devices with their start and end apart: 5, of which 3 were waited for; matrix products, arithmetic and copies ran while one was open for 0% of the time, Pallas kernels for 12%

profile of v4, /device:TPU:1, one launch (start us, length us, event | category | flops | bytes accessed | tf_op | source)
XLA Modules:
  0.0 107.0 jit_solution(10087507318691663560)
XLA Ops:
  0.0 3.7 %pack.1 = bf16[2048,512]{1,0:T(8,128)(2,1)} custom-call(bf16[256,1024]{1,0:T(8,128)(2,1)} %tok_ref.1, s32[2,256]{1,0:T(2,128)} %pos_ref.3, s32[1,1024]{1,0:T(1,128)} %label_ref.1), custom_call_target="tpu_custom_call" | custom-call | tf_op jit(solution)/shard_map/pack/pallas_call | solution.py:582
  3.7 0.0 copy-start.5
  3.7 11.5 %all-to-all-start = ((bf16[128,16,512]{2,1,0:T(8,128)(2,1)}), bf16[128,16,512]{2,1,0:T(8,128)(2,1)S(1)}, u32[]{:S(2)}, u32[]{:S(2)}) async-start(bf16[128,16,512]{2,1,0:T(8,128)(2,1)} %bitcast.8), calls=%async_computation | async-start | bytes 4194304 | tf_op jit(solution)/shard_map/all_to_all | solution.py:579
  15.2 0.0 copy-done.5
  15.2 0.0 copy-start
  15.2 1.6 %copy-done = bf16[1024,1024]{1,0:T(8,128)(2,1)S(1)} copy-done((bf16[1024,1024]{1,0:T(8,128)(2,1)S(1)}, bf16[1024,1024]{1,0:T(8,128)(2,1)}, u32[]{:S(2)}) %copy-start) | copy-done | bytes 2097176
  16.8 0.0 copy-start.1
  16.8 1.6 %copy-done.1 = bf16[1024,1024]{1,0:T(8,128)(2,1)S(1)} copy-done((bf16[1024,1024]{1,0:T(8,128)(2,1)S(1)}, bf16[1024,1024]{1,0:T(8,128)(2,1)}, u32[]{:S(2)}) %copy-start.1) | copy-done | bytes 2097176
  18.4 1.6 %copy-done.2 = bf16[1024,1024]{1,0:T(8,128)(2,1)S(1)} copy-done((bf16[1024,1024]{1,0:T(8,128)(2,1)S(1)}, bf16[1024,1024]{1,0:T(8,128)(2,1)}, u32[]{:S(2)}) %copy-start.2) | copy-done | bytes 2097176
  20.0 2.1 %prepare.1 = (bf16[1024,512]{1,0:T(8,128)(2,1)S(1)}, bf16[512,1024]{1,0:T(8,128)(2,1)}, bf16[1024,1024]{1,0:T(8,128)(2,1)S(1)}, f32[512,128]{1,0:T(8,128)S(1)}) custom-call(bf16[1024,1024]{1,0:T(8,128)(2,1)S(1)} %copy-done, bf16[1024,1024]{1,0:T(8,128)(2,1)S(1)} %copy-done.1, bf16[1024,1024]{1,0:T(8,128)(2,1)S(1)} %copy-done.2, s32[2,256]{1,0:T(2,128)S(1)} %copy-done.5), custom_call_target="tpu_custom_call" | custom-call | flops 1073741824 | bytes 8388608 | tf_op jit(solution)/shard_map/prepare/pallas_call | solution.py:592
  22.1 0.0 copy-start.3
  22.1 1.3 %copy-done.3 = bf16[1024,1024]{1,0:T(8,128)(2,1)} copy-done((bf16[1024,1024]{1,0:T(8,128)(2,1)}, bf16[1024,1024]{1,0:T(8,128)(2,1)S(1)}, u32[]{:S(2)}) %copy-start.3) | copy-done | bytes 2097176
  23.5 21.7 %all-to-all-done = bf16[128,16,512]{2,1,0:T(8,128)(2,1)S(1)} async-done(((bf16[128,16,512]{2,1,0:T(8,128)(2,1)}), bf16[128,16,512]{2,1,0:T(8,128)(2,1)S(1)}, u32[]{:S(2)}, u32[]{:S(2)}) %all-to-all-start) | async-done | bytes 2097184 | tf_op jit(solution)/shard_map/all_to_all | solution.py:579
  45.2 1.4 %sort_high.1 = (bf16[384,512]{1,0:T(8,128)(2,1)S(1)}, bf16[128,128]{1,0:T(8,128)(2,1)S(1)}, f32[16,128]{1,0:T(8,128)S(1)}, f32[1,1]{1,0:T(1,128)}) custom-call(bf16[2048,512]{1,0:T(8,128)(2,1)S(1)} %bitcast.5), custom_call_target="tpu_custom_call" | custom-call | tf_op jit(solution)/shard_map/sort_high/pallas_call | solution.py:609
  46.5 0.0 copy-start.6
  46.6 1.5 %sort_low.1 = (bf16[640,512]{1,0:T(8,128)(2,1)S(1)}, f32[1,1024]{1,0:T(1,128)S(1)}, f32[1024,128]{1,0:T(8,128)S(1)}, f32[1024,128]{1,0:T(8,128)S(1)}, f32[8,128]{1,0:T(8,128)S(1)}) custom-call(bf16[2048,512]{1,0:T(8,128)(2,1)S(1)} %bitcast.6, f32[16,128]{1,0:T(8,128)S(1)} %get-tuple-element.115.code_ref), custom_call_target="tpu_custom_call" | custom-call | flops 4294967296 | bytes 4194304 | tf_op jit(solution)/shard_map/sort_low/pallas_call | solution.py:622
  48.1 0.1 collective-permute-start.3
  48.2 0.5 collective-permute-start.4
  48.7 1.0 collective-permute-start.2
  49.7 1.1 %collective-permute-done.4.ho_ref = bf16[384,512]{1,0:T(8,128)(2,1)S(1)} collective-permute-done((bf16[384,512]{1,0:T(8,128)(2,1)S(1)}, bf16[384,512]{1,0:T(8,128)(2,1)S(1)}, u32[]{:S(2)}, u32[]{:S(2)}) %collective-permute-start.4) | collective-permute-done | bytes 393248 | tf_op jit(solution)/shard_map/ppermute | solution.py:571
  50.8 0.0 collective-permute-done.3.lo_ref
  50.8 0.0 copy-done.6
  50.8 11.0 %own_block.1 = (bf16[1024,512]{1,0:T(8,128)(2,1)S(1)}, bf16[512,1024]{1,0:T(8,128)(2,1)S(1)}, f32[8,1024]{1,0:T(8,128)S(1)}, f32[2048,128]{1,0:T(8,128)S(1)}, bf16[2048,512]{1,0:T(8,128)(2,1)S(1)}) custom-call(bf16[640,512]{1,0:T(8,128)(2,1)S(1)} %get-tuple-element.116.lm_ref, bf16[384,512]{1,0:T(8,128)(2,1)S(1)} %get-tuple-element.114.hm_ref, ...), custom_call_target="tpu_custom_call" | custom-call | flops 1048576 | bytes 1048576 | tf_op jit(solution)/shard_map/own_block/pallas_call | solution.py:637
  61.8 0.0 collective-permute-done.2
  61.8 0.2 collective-permute-start.5
  62.7 0.9 collective-permute-done.5
  63.6 6.9 %conditional.1 = (bf16[2048,512]{1,0:T(8,128)(2,1)S(1)}) conditional(s32[]{:T(128)} %bitcast.2, (bf16[384,512]{1,0:T(8,128)(2,1)S(1)}, bf16[384,512]{1,0:T(8,128)(2,1)S(1)}, bf16[1024,512]{1,0:T(8,128)(2,1)S(1)}, bf16[512,1024]{1,0:T(8,128)(2,1)S(1)}, f32[1,1024]{1,0:T(1,128)S(1)}, /*index=5*/f32[1024,128]{1,0:T(8,128)S(1)}, f32[8,128]{1,0:T(8,128)S(1)}, ...), branch_computations={%region_0.0_spmd, %region_1.0_spmd} | conditional | flops 4194304 | bytes 33554716 | solution.py:689
  63.6 6.7 %prior_block.2 = bf16[2048,512]{1,0:T(8,128)(2,1)S(1)} custom-call(bf16[384,512]{1,0:T(8,128)(2,1)S(1)} %get-tuple-element.58.xm_ref, bf16[384,512]{1,0:T(8,128)(2,1)S(1)} %get-tuple-element.59.xo_ref, bf16[1024,512]{1,0:T(8,128)(2,1)S(1)} %get-tuple-element.60.wq_ref, bf16[512,1024]{1,0:T(8,128)(2,1)S(1)} %get-tuple-element.61.wvt_ref, ...), custom_call_target="tpu_custom_call" | custom-call | tf_op jit(solution)/shard_map/cond/branch_0_fun/prior_block/pallas_call | solution.py:660
  70.5 0.0 copy-start.4
  70.5 33.2 %all_to_all.10 = bf16[128,16,512]{2,1,0:T(8,128)(2,1)S(1)} all-to-all(bf16[128,16,512]{2,1,0:T(8,128)(2,1)S(1)} %bitcast.9), channel_id=1, replica_groups=mesh['round'=2,'head'=2,'seq'=32] {'round','head','seq'}, dimensions={0} | all-to-all | bytes 4194304 | tf_op jit(solution)/shard_map/all_to_all | solution.py:579
  103.7 0.0 copy-done.4
  103.7 3.3 %combine.1 = bf16[256,1024]{1,0:T(8,128)(2,1)} custom-call(bf16[2048,512]{1,0:T(8,128)(2,1)S(1)} %bitcast.7, f32[512,128]{1,0:T(8,128)S(1)} %get-tuple-element.131.slot_ref, bf16[1024,1024]{1,0:T(8,128)(2,1)S(1)} %copy-done.4), custom_call_target="tpu_custom_call" | custom-call | tf_op jit(solution)/shard_map/combine/pallas_call | solution.py:691
  (1 shorter events, 0.0 us)
Async XLA Ops:
  3.7 11.5 %copy-start.5 = (s32[2,256]{1,0:T(2,128)S(1)}, s32[2,256]{1,0:T(2,128)}, u32[]{:S(2)}) copy-start(s32[2,256]{1,0:T(2,128)} %pos_ref.3) | copy-start | bytes 6148
  3.7 41.5 %all-to-all-start = ((bf16[128,16,512]{2,1,0:T(8,128)(2,1)}), bf16[128,16,512]{2,1,0:T(8,128)(2,1)S(1)}, u32[]{:S(2)}, u32[]{:S(2)}) async-start(bf16[128,16,512]{2,1,0:T(8,128)(2,1)} %bitcast.8), calls=%async_computation | async-start | bytes 4194304 | tf_op jit(solution)/shard_map/all_to_all | solution.py:579
  15.2 1.6 %copy-start = (bf16[1024,1024]{1,0:T(8,128)(2,1)S(1)}, bf16[1024,1024]{1,0:T(8,128)(2,1)}, u32[]{:S(2)}) copy-start(bf16[1024,1024]{1,0:T(8,128)(2,1)} %wqk_ref.1) | copy-start | bytes 6291460
  16.8 1.6 %copy-start.1 = (bf16[1024,1024]{1,0:T(8,128)(2,1)S(1)}, bf16[1024,1024]{1,0:T(8,128)(2,1)}, u32[]{:S(2)}) copy-start(bf16[1024,1024]{1,0:T(8,128)(2,1)} %wv_ref.1) | copy-start | bytes 6291460
  18.4 1.6 %copy-start.2 = (bf16[1024,1024]{1,0:T(8,128)(2,1)S(1)}, bf16[1024,1024]{1,0:T(8,128)(2,1)}, u32[]{:S(2)}) copy-start(bf16[1024,1024]{1,0:T(8,128)(2,1)} %wo_ref.1) | copy-start | bytes 6291460
  22.1 1.3 %copy-start.3 = (bf16[1024,1024]{1,0:T(8,128)(2,1)}, bf16[1024,1024]{1,0:T(8,128)(2,1)S(1)}, u32[]{:S(2)}) copy-start(bf16[1024,1024]{1,0:T(8,128)(2,1)S(1)} %get-tuple-element.132.w_ref) | copy-start | bytes 6291460
  46.5 4.3 %copy-start.6 = (bf16[512,1024]{1,0:T(8,128)(2,1)S(1)}, bf16[512,1024]{1,0:T(8,128)(2,1)}, u32[]{:S(2)}) copy-start(bf16[512,1024]{1,0:T(8,128)(2,1)} %get-tuple-element.118.wvt_ref) | copy-start | bytes 3145732
  48.1 2.7 %collective-permute-start.3 = (bf16[640,512]{1,0:T(8,128)(2,1)S(1)}, bf16[640,512]{1,0:T(8,128)(2,1)S(1)}, u32[]{:S(2)}, u32[]{:S(2)}) collective-permute-start(bf16[640,512]{1,0:T(8,128)(2,1)S(1)} %get-tuple-element.116.lm_ref), channel_id=1, source_target_pairs={{0,64},{64,0},{1,65},{65,1},{2,66},{66,2},{3,67},{67,3},{4,68},{68... | collective-permute-start | bytes 1966088 | tf_op jit(solution)/shard_map/ppermute | solution.py:571
  48.2 2.6 %collective-permute-start.4 = (bf16[384,512]{1,0:T(8,128)(2,1)S(1)}, bf16[384,512]{1,0:T(8,128)(2,1)S(1)}, u32[]{:S(2)}, u32[]{:S(2)}) collective-permute-start(bf16[384,512]{1,0:T(8,128)(2,1)S(1)} %get-tuple-element.114.hm_ref), channel_id=1, source_target_pairs={{0,64},{64,0},{1,65},{65,1},{2,66},{66,2},{3,67},{67,3},{4,68},{68... | collective-permute-start | bytes 1179656 | tf_op jit(solution)/shard_map/ppermute | solution.py:571
  48.7 13.2 %collective-permute-start.2 = (bf16[384,512]{1,0:T(8,128)(2,1)S(1)}, bf16[384,512]{1,0:T(8,128)(2,1)S(1)}, u32[]{:S(2)}, u32[]{:S(2)}) collective-permute-start(bf16[384,512]{1,0:T(8,128)(2,1)S(1)} %get-tuple-element.114.hm_ref), channel_id=1, source_target_pairs={{0,1},{1,2},{2,3},{3,7},{7,6},{6,5},{5,4},{4,12},{12,13},{13,14},{... | collective-permute-start | bytes 1179656 | tf_op jit(solution)/shard_map/ppermute | solution.py:575
  61.8 1.8 %collective-permute-start.5 = (bf16[384,512]{1,0:T(8,128)(2,1)S(1)}, bf16[384,512]{1,0:T(8,128)(2,1)S(1)}, u32[]{:S(2)}, u32[]{:S(2)}) collective-permute-start(bf16[384,512]{1,0:T(8,128)(2,1)S(1)} %collective-permute-done.2), channel_id=1, source_target_pairs={{0,64},{64,0},{1,65},{65,1},{2,66},{66,2},{3,67},{67,3},{4,68},{68... | collective-permute-start | bytes 1179656 | tf_op jit(solution)/shard_map/ppermute | solution.py:571
  70.5 33.2 %copy-start.4 = (bf16[1024,1024]{1,0:T(8,128)(2,1)S(1)}, bf16[1024,1024]{1,0:T(8,128)(2,1)}, u32[]{:S(2)}) copy-start(bf16[1024,1024]{1,0:T(8,128)(2,1)} %copy-done.3) | copy-start | bytes 6291460

commit v5 on v4

--- a/solution.py
+++ b/solution.py
@@ -18,6 +18,7 @@
 HALO = 3 * TILE
 SHIFT = 65536.0
 STEP = 1024
+PIECE = 512
 
 LOG2E = 1.4426950408889634
 SELF_PENALTY = -100000.0 * LOG2E
@@ -74,12 +75,20 @@
     return hot, dest * SLOTS + rank
 
 
-def pack_kernel(tok_ref, pos_ref, label_ref, out_ref, buf_ref, sem_ref, *, owners):
+def pack_kernel(
+    tok_hbm_ref, pos_ref, label_ref, out_ref, tok_ref, buf_ref, in_sem, sem_ref, *, owners
+):
     count = tok_ref.shape[0]
     width = out_ref.shape[1]
     rows = owners * SLOTS
-    tokens = tok_ref[...]
     half = BLOCK // 2
+    loads = []
+    for a in range(2):
+        cols = pl.ds(a * width, width)
+        loads.append(
+            pltpu.make_async_copy(tok_hbm_ref.at[:, cols], tok_ref.at[:, cols], in_sem.at[a])
+        )
+        loads[-1].start()
     first, last = label_ref[0:1, 0:1], label_ref[0:1, BLOCK - 1 : BLOCK]
     wide = []
     for held in (HALO, half):
@@ -91,13 +100,13 @@
     core, head, seq = (lax.axis_index(axis) for axis in AXES)
     label = jnp.where(head == 0, label[:, :half], label[:, half:])
     label = jnp.broadcast_to(label, (SLOTS, half))
-    copies = []
+    picks, extras = [], []
     for r in range(2):
         pos = pos_ref[r : r + 1, :]
         hot, slot = slots_of(pos, owners)
         rank = slot & (SLOTS - 1)
         within = pos & (BLOCK - 1)
-        pick = mask(iota((rows, count), 0) == slot)
+        picks.append(mask(iota((rows, count), 0) == slot))
         value = iota((128, count), 0)
         code = jnp.where((value & 1) == 0, (within >> 5) + 1, within & 31)
         code = jnp.where((value >> 1) == rank, code, 0).astype(F32).astype(BF)
@@ -106,25 +115,26 @@
         places = jnp.where(lane == 2 * SLOTS, wide[0], places)
         places = jnp.where(lane == 2 * SLOTS + 1, wide[1], places).astype(BF)
         at_meta = mask(iota((rows, owners), 0) == iota((rows, owners), 1) * SLOTS + META)
-        extra = mm(at_meta, places)
-        for a in range(2):
+        extras.append(mm(at_meta, places))
+    copies = []
+    for a in range(2):
+        loads[a].wait()
+        for r in range(2):
             at = (a * 2 + r) * rows
-            body = mm(pick, tokens[:, a * width : (a + 1) * width])
-            buf_ref[at : at + rows, 0:128] = (body[:, 0:128] + extra).astype(BF)
+            body = mm(picks[r], tok_ref[:, a * width : (a + 1) * width])
+            buf_ref[at : at + rows, 0:128] = (body[:, 0:128] + extras[r]).astype(BF)
             buf_ref[at : at + rows, 128:width] = body[:, 128:].astype(BF)
 
-        @pl.when(core == r)
-        def _():
-            for a in range(2):
-                for ahead in range(2):
-                    chip = chip_of((seq + ahead) & (owners - 1))
-                    at = pl.multiple_of((a * 2 + r) * rows + chip * SLOTS, SLOTS)
-                    old = buf_ref[pl.ds(at, SLOTS), :].astype(F32)
+            @pl.when(core == r)
+            def _():
+                for step in range(2):
+                    chip = chip_of((seq + step) & (owners - 1))
+                    tile = pl.ds(pl.multiple_of(at + chip * SLOTS, SLOTS), SLOTS)
+                    old = buf_ref[tile, :].astype(F32)
                     new = jnp.where(iota((SLOTS, half), 0) == LABELS, label, old)
-                    buf_ref[pl.ds(at, SLOTS), :] = new.astype(BF)
-
-        for a in range(2):
-            piece = pl.ds((a * 2 + r) * rows, rows)
+                    buf_ref[tile, :] = new.astype(BF)
+
+            piece = pl.ds(at, rows)
             copy = pltpu.make_async_copy(
                 buf_ref.at[piece], out_ref.at[piece], sem_ref.at[a * 2 + r]
             )
@@ -191,14 +201,18 @@
     return mm(values, weight)
 
 
-def sorted_rows(x_ref, code_ref, out_ref, first):
-    rows = out_ref.shape[0]
+def sorted_rows(x_ref, code_ref, out_refs, first):
+    rows = sum(out_ref.shape[0] for out_ref in out_refs)
     position = (iota((rows, 128), 0) + (first + 32)).astype(F32)
     picks = [
         mask(position == jnp.broadcast_to(code_ref[q : q + 1, :], (rows, 128)))
         for q in range(code_ref.shape[0])
     ]
-    out_ref[...] = mm(jnp.concatenate(picks, axis=1), x_ref[...]).astype(BF)
+    result = mm(jnp.concatenate(picks, axis=1), x_ref[...]).astype(BF)
+    at = 0
+    for out_ref in out_refs:
+        out_ref[...] = result[at : at + out_ref.shape[0]]
+        at += out_ref.shape[0]
 
 
 def sort_high_kernel(x_ref, high_ref, meta_ref, code_ref, wide_ref):
@@ -209,11 +223,11 @@
     flags = jnp.max(flags, axis=0, keepdims=True)
     wide_ref[...] = jnp.sum(flags, axis=1, keepdims=True)
     code_ref[...] = place_rows(meta)
-    sorted_rows(x_ref, code_ref, high_ref, BLOCK - high_ref.shape[0])
+    sorted_rows(x_ref, code_ref, (high_ref,), BLOCK - high_ref.shape[0])
 
 
 def sort_low_kernel(
-    x_ref, code_ref, low_ref, row_ref, col_ref, prior_col_ref, flag_ref, *, owners
+    x_ref, code_ref, low_ref, low_next_ref, row_ref, col_ref, prior_col_ref, flag_ref, *, owners
 ):
     my_round, me = lax.axis_index("head"), block_of(lax.axis_index("seq"))
 
@@ -231,8 +245,12 @@
     row_ref[...] = own
     col_ref[...] = jnp.transpose(jnp.broadcast_to(own, (TILE, BLOCK)))
     prior_col_ref[...] = jnp.transpose(jnp.broadcast_to(prior, (TILE, BLOCK)))
-    flag_ref[...] = jnp.broadcast_to(plan(own, prior), flag_ref.shape)
-    sorted_rows(x_ref, code_ref, low_ref, 0)
+    flag_ref[...] = plan(own, prior)
+    sorted_rows(x_ref, code_ref, (low_ref, low_next_ref), 0)
+
+
+def window(i):
+    return max(i * SPAN - TILE, 0), min((i + 1) * SPAN + TILE, BLOCK)
 
 
 def plan(own, prior):
@@ -248,32 +266,35 @@
     low, high = ends(own)
     prior_low, prior_high = ends(prior)
     tile = iota(low.shape, 0)
-    bits = jnp.zeros((1, TILE), F32)
-
-    def add(bits, flag, found):
-        found = jnp.max(jnp.where(found, 1.0, 0.0), axis=0, keepdims=True)
-        return bits + float(2**flag) * found
-
+    weight = (1 << tile).astype(F32)
     per, tiles = SPAN // TILE, BLOCK // TILE
+
+    def bits(found):
+        return jnp.sum(jnp.where(found, weight, 0.0), axis=0, keepdims=True)
+
+    words = []
     for i in range(SPANS):
         at = i * per
         span_low = jnp.min(low[at : at + per], axis=0, keepdims=True)
         span_high = jnp.max(high[at : at + per], axis=0, keepdims=True)
-        meets = (low <= span_high) & (high >= span_low)
-        bits = add(bits, i, meets & ((tile < at - 1) | (tile > at + per)))
-        start = min(max(at - 2, 0), tiles - per - 4)
-        bits = add(bits, 4 + i, meets & ((tile < start) | (tile >= start + per + 4)))
+        begin, end = window(i)
+        outside = (tile < begin // TILE) | (tile >= end // TILE)
+        words.append(bits((low <= span_high) & (high >= span_low) & outside))
     some = jnp.zeros(low.shape, F32)
+    late = jnp.zeros((1, TILE), F32)
     for i in range(tiles):
         meets = (prior_low <= high[i : i + 1]) & (prior_high >= low[i : i + 1])
-        some = jnp.maximum(some, jnp.where(meets, 1.0, 0.0))
-        bits = add(bits, 8 + i, meets)
-    bits = add(bits, 16, (some > 0.0) & (tile < tiles - 1))
-    return add(bits, 17, (some > 0.0) & (tile < tiles - 3))
-
-
-def flag_bits(flag_ref):
-    return jnp.max(flag_ref[...]).astype(I32)
+        meets = jnp.where(meets, 1.0, 0.0)
+        some = jnp.maximum(some, meets)
+        late = late + float(2**i) * jnp.max(meets, axis=0, keepdims=True)
+    some = jnp.where(tile < tiles - 1, some, 0.0)
+    late = late + 256.0 * jnp.max(some, axis=0, keepdims=True)
+    rows = [late, words[0] + 256.0 * words[1], words[2] + 256.0 * words[3]]
+    return jnp.concatenate(rows + [jnp.zeros((5, TILE), F32)], axis=0)
+
+
+def flag_bits(flag_ref, row):
+    return jnp.max(flag_ref[row : row + 1, :]).astype(I32)
 
 
 def project(mine, other, wq_ref, wvt_ref):
@@ -330,6 +351,29 @@
     return result[0:DH], top, result[DH : DH + 1]
 
 
+def merge_heads(keys, queries, values, key_label, query_label, at, out_ref, lse_ref):
+    span = query_label.shape[1]
+    lse_row = iota((8, span), 0)
+    tiles = [lse_ref[:, pl.ds(at, span)]]
+
+    def first(h):
+        return score(keys(h), queries(h), key_label, query_label, None)
+
+    def second(h, scores):
+        result, top, total = weigh(scores, values(h))
+        here, there = tiles[0][h : h + 1, :], top + jnp.log2(total)
+        largest = jnp.maximum(here, there)
+        kept, added = jnp.exp2(here - largest), jnp.exp2(there - largest)
+        own = out_ref[head_cols(h), pl.ds(at, span)].astype(F32)
+        merged = (kept * own + result * (added / total)) * (1.0 / (kept + added))
+        out_ref[head_cols(h), pl.ds(at, span)] = merged.astype(BF)
+        new = largest + jnp.log2(kept + added)
+        tiles[0] = jnp.where(lse_row == h, new, tiles[0])
+
+    ahead(range(out_ref.shape[0] // DH), first, second, 3)
+    lse_ref[:, pl.ds(at, span)] = tiles[0]
+
+
 def ahead(work, first, second, depth):
     pending = []
     for item in work:
@@ -341,7 +385,7 @@
 
 
 def late_span(bits, i):
-    return ((bits >> (8 + SPAN // TILE * i)) & (2 ** (SPAN // TILE) - 1)) != 0
+    return ((bits >> (SPAN // TILE * i)) & (2 ** (SPAN // TILE) - 1)) != 0
 
 
 def sums_of(lse, heads):
@@ -354,29 +398,54 @@
     return jnp.concatenate([sums] * SLOTS, axis=0).astype(BF)
 
 
-def packed_rows(pick, out, sums):
-    body = mm_nt(pick, out)
-    sums = mm_nt(pick, sums)
-    row = iota((STEP, 128), 0) & (SLOTS - 1)
-    sums = jnp.where(row == (iota((STEP, 128), 1) >> 3), sums, 0.0)
-    sums = jnp.sum(sums.reshape(STEP // SLOTS, SLOTS, 128), axis=1, keepdims=True)
-    sums = jnp.broadcast_to(sums, (STEP // SLOTS, SLOTS, 128)).reshape(STEP, 128)
-    extra = jnp.where(row == META, sums, 0.0)
+def in_meta_row(sums):
+    rows = sums.shape[0]
+    row = iota((rows, 128), 0) & (SLOTS - 1)
+    sums = jnp.where(row == (iota((rows, 128), 1) >> 3), sums, 0.0)
+    sums = jnp.sum(sums.reshape(rows // SLOTS, SLOTS, 128), axis=1, keepdims=True)
+    sums = jnp.broadcast_to(sums, (rows // SLOTS, SLOTS, 128)).reshape(rows, 128)
+    return jnp.where(row == META, sums, 0.0)
+
+
+def pick_of(codes, start, stop):
+    lane = (iota(codes.shape, 1) + 32).astype(F32)
+    return jnp.concatenate([mask(codes == lane + float(c)) for c in range(start, stop, 128)], 1)
+
+
+def packed_rows(codes, out, sums):
+    half = BLOCK // 2
+    body = mm_nt(pick_of(codes, 0, BLOCK), out)
+    upper = codes >= float(half + 32)
+    both = jnp.concatenate([sums[:, :half], sums[:, half:]], axis=0)
+    found = mm_nt(pick_of(jnp.where(upper, codes - half, codes), 0, half), both)
+    extra = in_meta_row(jnp.where(upper, found[:, 128:], found[:, :128]))
     return jnp.concatenate([body[:, 0:128] + extra, body[:, 128:]], axis=1)
 
 
+def first_kernel(hm_ref, ho_ref, wq_ref, wvt_ref, meta_ref, q_ref, key_ref, vt_ref, place_ref):
+    queries, parts, values = project(hm_ref[...], ho_ref[...], wq_ref, wvt_ref)
+    q_ref[...] = queries
+    store_keys(0, parts, values, key_ref, vt_ref)
+    place_ref[...] = place_columns(meta_ref[...])
+
+
 def own_kernel(
-    lm_ref, hm_ref, lo_ref, ho_ref, wq_ref, wvt_ref, row_ref, col_ref, flag_ref, meta_ref,
-    q_ref, out_ref, lse_ref, place_ref, early_ref, key_ref, vt_ref,
+    lm_ref, nm_ref, lo_ref, no_ref, q_high_ref, key_high_ref, vt_high_ref, wq_ref, wvt_ref,
+    row_ref, col_ref, flag_ref, place_ref,
+    q_ref, out_ref, lse_ref, early_ref, key_ref, vt_ref,
 ):
-    first_rows = lm_ref.shape[0]
+    low_rows = 2 * lm_ref.shape[0]
     heads = q_ref.shape[1] // DH
-    bits = flag_bits(flag_ref)
-    for m_part, o_part, at in ((hm_ref, ho_ref, first_rows), (lm_ref, lo_ref, 0)):
-        queries, parts, values = project(m_part[...], o_part[...], wq_ref, wvt_ref)
-        q_ref[at : at + queries.shape[0], :] = queries
-        store_keys(at, parts, values, key_ref, vt_ref)
-    place_ref[...] = place_columns(meta_ref[...])
+    late_bits = flag_bits(flag_ref, 0)
+    far_bits = [flag_bits(flag_ref, 1), flag_bits(flag_ref, 2)]
+    q_ref[low_rows:, :] = q_high_ref[...]
+    key_ref[low_rows:, :] = key_high_ref[...]
+    vt_ref[:, low_rows:] = vt_high_ref[...]
+    mine = jnp.concatenate([lm_ref[...], nm_ref[...]], axis=0)
+    other = jnp.concatenate([lo_ref[...], no_ref[...]], axis=0)
+    queries, parts, values = project(mine, other, wq_ref, wvt_ref)
+    q_ref[0:low_rows, :] = queries
+    store_keys(0, parts, values, key_ref, vt_ref)
     lse_row = iota((8, SPAN), 0)
 
     def spans(work, depth):
@@ -402,37 +471,34 @@
 
     work = []
     for at in range(BLOCK - SPAN, -1, -SPAN):
-        start, stop = max(at - TILE, 0), min(at + SPAN + TILE, BLOCK)
+        start, stop = window(at // SPAN)
         work += [(h, at, start, stop - start, at - start) for h in range(heads)]
     spans(work, 3)
 
-    def flag(k):
-        return (bits >> k) & 1
-
-    @pl.loop(0, SPANS)
-    def _(i):
-        at = pl.multiple_of(i * SPAN, SPAN)
-
-        @pl.when((flag(i) != 0) & (flag(4 + i) == 0))
+    for pair in range(2):
+
+        @pl.when(far_bits[pair] != 0)
         def _():
-            size = SPAN + 4 * TILE
-            start = pl.multiple_of(jnp.clip(at - 2 * TILE, 0, BLOCK - size), TILE)
-            spans([(h, at, start, size, at - start) for h in range(heads)], 2)
-
-        @pl.when(flag(4 + i) != 0)
-        def _():
-            spans([(h, at, 0, BLOCK, at) for h in range(heads)], 0)
-
-    late = [jnp.where(late_span(bits, i), 4.0 * BLOCK, 0.0) for i in range(SPANS)]
+            @pl.loop(0, 2 * BLOCK // TILE)
+            def _(k):
+                @pl.when(((far_bits[pair] >> k) & 1) != 0)
+                def _():
+                    at = pl.multiple_of((2 * pair + (k >> 3)) * SPAN, SPAN)
+                    rows = pl.ds(pl.multiple_of((k & 7) * TILE, TILE), TILE)
+                    merge_heads(
+                        lambda h: key_ref[rows, head_cols(h, 2)],
+                        lambda h: q_ref[pl.ds(at, SPAN), head_cols(h)],
+                        lambda h: vt_ref[value_rows(h), rows],
+                        col_ref[rows, :], row_ref[0:1, pl.ds(at, SPAN)], at, out_ref, lse_ref,
+                    )
+
     sums = sums_of(lse_ref[...], heads)
     for at in range(0, early_ref.shape[0], STEP):
         codes = place_ref[at : at + STEP, :]
-        lane = (iota((STEP, 128), 1) + 32).astype(F32)
-        pick = jnp.concatenate(
-            [mask(codes == lane + (float(c) + late[c // SPAN])) for c in range(0, BLOCK, 128)],
-            axis=1,
-        )
-        early_ref[at : at + STEP, :] = packed_rows(pick, out_ref[...], sums).astype(BF)
+        for i in range(SPANS):
+            late = jnp.where(late_span(late_bits, i), float(32 + i * SPAN), 4.0 * BLOCK)
+            codes = jnp.where((codes >= late) & (codes < late + SPAN), 0.0, codes)
+        early_ref[at : at + STEP, :] = packed_rows(codes, out_ref[...], sums).astype(BF)
 
 
 def rest_kernel(
@@ -442,75 +508,99 @@
 ):
     halo = xm_ref.shape[0]
     heads = q_ref.shape[1] // DH
-    bits = flag_bits(flag_ref)
-    lse_row = iota((8, TILE), 0)
+    bits = flag_bits(flag_ref, 0)
     lse_ref[...] = own_lse_ref[...]
     for i in range(SPANS):
+        cols = slice(i * SPAN, (i + 1) * SPAN)
 
         @pl.when(late_span(bits, i))
         def _():
-            out_ref[:, i * SPAN : (i + 1) * SPAN] = own_ref[:, i * SPAN : (i + 1) * SPAN]
+            out_ref[:, cols] = own_ref[:, cols]
+
+        @pl.when(jnp.logical_not(late_span(bits, i)))
+        def _():
+            out_ref[:, cols] = jnp.zeros((heads * DH, SPAN), BF)
+            lse_ref[:, cols] = jnp.zeros((8, SPAN), F32)
+
+    def at_once(at, first, span):
+        merge_heads(
+            lambda h: key_ref[first:, head_cols(h, 2)],
+            lambda h: q_ref[pl.ds(at, span), head_cols(h)],
+            lambda h: vt_ref[value_rows(h), first:],
+            col_ref[BLOCK - halo + first :, :], row_ref[0:1, pl.ds(at, span)], at, out_ref, lse_ref,
+        )
 
     def merge(size):
         first = halo - size
         _, parts, values = project(xm_ref[first:, :], xo_ref[first:, :], wq_ref, wvt_ref)
         store_keys(first, parts, values, key_ref, vt_ref)
-
-        @pl.loop(0, BLOCK // TILE)
-        def _(i):
-            @pl.when(((bits >> (8 + i)) & 1) != 0)
-            def _():
-                at = pl.multiple_of(i * TILE, TILE)
-                tiles = [lse_ref[:, pl.ds(at, TILE)]]
-
-                def first_step(h):
-                    return score(
-                        key_ref[first:, head_cols(h, 2)], q_ref[pl.ds(at, TILE), head_cols(h)],
-                        col_ref[BLOCK - size :, :], row_ref[0:1, pl.ds(at, TILE)], None,
-                    )
-
-                def second_step(h, scores):
-                    result, top, total = weigh(scores, vt_ref[value_rows(h), first:])
-                    here, there = tiles[0][h : h + 1, :], top + jnp.log2(total)
-                    largest = jnp.maximum(here, there)
-                    kept, added = jnp.exp2(here - largest), jnp.exp2(there - largest)
-                    own = out_ref[head_cols(h), pl.ds(at, TILE)].astype(F32)
-                    merged = (kept * own + result * (added / total)) * (1.0 / (kept + added))
-                    out_ref[head_cols(h), pl.ds(at, TILE)] = merged.astype(BF)
-                    new = largest + jnp.log2(kept + added)
-                    tiles[0] = jnp.where(lse_row == h, new, tiles[0])
-
-                ahead(range(heads), first_step, second_step, 3)
-                lse_ref[:, pl.ds(at, TILE)] = tiles[0]
+        many = 3 * TILE if size == 3 * TILE else TILE
+        few = (bits & 255) < 2 ** (many // TILE)
+
+        @pl.when(few & (bits != 0))
+        def _():
+            at_once(0, first, many)
+
+        @pl.when(jnp.logical_not(few))
+        def _():
+            @pl.loop(0, BLOCK // TILE)
+            def _(i):
+                @pl.when(((bits >> i) & 1) != 0)
+                def _():
+                    at_once(pl.multiple_of(i * TILE, TILE), first, TILE)
 
     if halo > HALO:
         merge(halo)
     else:
-        pl.when(bits >> 16 == 0)(lambda: merge(TILE))
-        pl.when(bits >> 16 != 0)(lambda: merge(halo))
-
-    copies = []
-    for t in range(send_ref.shape[0] // STEP):
-        piece = pl.ds(t * STEP, STEP)
-        buf_ref[piece, :] = early_ref[piece, :]
-
-        @pl.loop(0, SPANS)
-        def _(i):
-            @pl.when(late_span(bits, i))
-            def _():
-                cols = pl.ds(pl.multiple_of(i * SPAN, SPAN), SPAN)
-                codes = place_ref[piece, :]
-                lane = (iota((STEP, 128), 1) + (32 + i * SPAN)).astype(F32)
-                pick = jnp.concatenate(
-                    [mask(codes == lane + float(c)) for c in range(0, SPAN, 128)], axis=1
-                )
-                rows = packed_rows(pick, out_ref[:, cols], sums_of(lse_ref[:, cols], heads))
-                buf_ref[piece, :] = (buf_ref[piece, :].astype(F32) + rows).astype(BF)
-
-        copies.append(pltpu.make_async_copy(buf_ref.at[piece], send_ref.at[piece], sem_ref.at[t]))
-        copies[-1].start()
-    for copy in copies:
-        copy.wait()
+        pl.when(bits < 256)(lambda: merge(TILE))
+        pl.when(bits >= 256)(lambda: merge(halo))
+
+    pieces = send_ref.shape[0] // PIECE
+
+    def sending(t):
+        piece = pl.ds(pl.multiple_of(t * PIECE, PIECE), PIECE)
+        return pltpu.make_async_copy(buf_ref.at[piece], send_ref.at[piece], sem_ref.at[t])
+
+    def complete(piece, codes, rows_ref, cols):
+        pick = pick_of(codes, 0, cols.size)
+        body = mm_nt(pick, out_ref[:, cols])
+        extra = in_meta_row(mm_nt(pick, sums_of(lse_ref[:, cols], heads)))
+        rows = jnp.concatenate([body[:, 0:128] + extra, body[:, 128:]], axis=1)
+        buf_ref[piece, :] = (rows_ref[piece, :].astype(F32) + rows).astype(BF)
+
+    def finish(span):
+        @pl.loop(0, pieces)
+        def _(t):
+            piece = pl.ds(pl.multiple_of(t * PIECE, PIECE), PIECE)
+            complete(piece, place_ref[piece, :], early_ref, pl.ds(0, span))
+            sending(t).start()
+
+    needed = bits & 255
+    pl.when(needed < 2 ** (SPAN // TILE))(lambda: finish(SPAN))
+    pl.when((needed >= 2 ** (SPAN // TILE)) & (needed < 2 ** (2 * SPAN // TILE)))(
+        lambda: finish(2 * SPAN)
+    )
+
+    @pl.when(needed >= 2 ** (2 * SPAN // TILE))
+    def _():
+        @pl.loop(0, pieces)
+        def _(t):
+            piece = pl.ds(pl.multiple_of(t * PIECE, PIECE), PIECE)
+            buf_ref[piece, :] = early_ref[piece, :]
+
+            @pl.loop(0, SPANS)
+            def _(i):
+                @pl.when(late_span(bits, i))
+                def _():
+                    codes = place_ref[piece, :] - (i * SPAN).astype(F32)
+                    cols = pl.ds(pl.multiple_of(i * SPAN, SPAN), SPAN)
+                    complete(piece, codes, buf_ref, cols)
+
+            sending(t).start()
+
+    @pl.loop(0, pieces)
+    def _(t):
+        sending(t).wait()
 
 
 def final_kernel(x_ref, slot_ref, w_ref, out_ref, *, owners):
@@ -530,20 +620,26 @@
             jnp.concatenate([mask(at_meta == lane + c) for c in range(0, rows, 128)], axis=1)
         )
         ranks.append(place)
-    v = iota((128, width), 0) & 7
-    select = mask((v >> 1) == (iota((128, width), 1) >> 7))
+    sums = []
+    for r in range(2):
+        there = [x_ref[(a * 2 + r) * rows : (a * 2 + r + 1) * rows, 0:128] for a in range(2)]
+        own = mm(meta_picks[r], jnp.concatenate(there, axis=1))
+        keep = (lane >> 3) == ranks[r]
+        sums.append([jnp.where(keep, own[:, a * 128 : (a + 1) * 128], 0.0) for a in range(2)])
+    v = iota((256, width), 0)
+    select = jnp.where(((v & 7) >> 1) == (iota((256, width), 1) >> 7), 1.0, 0.0)
+    select = jnp.where(v < 128, -select, select).astype(BF)
     total = None
     for a in range(2):
-        values, sums = [], []
-        for r in range(2):
-            at = (a * 2 + r) * rows
-            values.append(mm(picks[r], x_ref[at : at + rows, :]))
-            own = mm(meta_picks[r], x_ref[at : at + rows, 0:128])
-            own = jnp.where((lane >> 3) == ranks[r], own, 0.0).astype(BF)
-            sums.append(mm(own, select))
-        largest = jnp.maximum(sums[0], sums[1])
-        first, second = jnp.exp2(sums[0] - largest), jnp.exp2(sums[1] - largest)
-        combined = ((first * values[0] + second * values[1]) / (first + second)).astype(BF)
+        values = [
+            mm(picks[r], x_ref[(a * 2 + r) * rows : (a * 2 + r + 1) * rows, :]) for r in range(2)
+        ]
+        apart = mm(jnp.concatenate([sums[0][a], sums[1][a]], axis=1).astype(BF), select)
+        small = jnp.exp2(-jnp.abs(apart))
+        large = 1.0 / (1.0 + small)
+        second = jnp.where(apart < 0.0, small * large, large)
+        first = jnp.where(apart < 0.0, large, small * large)
+        combined = (first * values[0] + second * values[1]).astype(BF)
         part = mm(combined, w_ref[a * width : (a + 1) * width, :])
         total = part if total is None else total + part
     out_ref[...] = total.astype(BF)
@@ -556,7 +652,7 @@
     width = model_width // 2
     heads = width // DH
     rows = total * SLOTS
-    params = pltpu.CompilerParams(vmem_limit_bytes=40 * 2**20)
+    params = pltpu.CompilerParams(vmem_limit_bytes=24 * 2**20)
     alone = pltpu.CompilerParams(vmem_limit_bytes=60 * 2**20)
     in_vmem = pl.BlockSpec(memory_space=pltpu.VMEM)
     in_hbm = pl.BlockSpec(memory_space=pltpu.HBM)
@@ -582,8 +678,14 @@
     packed = pl.pallas_call(
         functools.partial(pack_kernel, owners=owners),
         out_shape=shape(rows, width),
+        in_specs=[in_hbm, in_vmem, in_vmem],
         out_specs=in_hbm,
-        scratch_shapes=[pltpu.VMEM((rows, width), BF), pltpu.SemaphoreType.DMA((4,))],
+        scratch_shapes=[
+            pltpu.VMEM((tok_dev, model_width), BF),
+            pltpu.VMEM((rows, width), BF),
+            pltpu.SemaphoreType.DMA((2,)),
+            pltpu.SemaphoreType.DMA((4,)),
+        ],
         compiler_params=alone,
         name="pack",
     )(tokens, positions, buckets)
@@ -619,10 +721,11 @@
     )(arrived)
     halo = onward(high)
     high_other = swap(high)
-    low, label_row, label_col, prior_col, flags = pl.pallas_call(
+    low, low_next, label_row, label_col, prior_col, flags = pl.pallas_call(
         functools.partial(sort_low_kernel, owners=owners),
         out_shape=[
-            shape(BLOCK - HALO, width),
+            shape((BLOCK - HALO) // 2, width),
+            shape((BLOCK - HALO) // 2, width),
             shape(1, BLOCK, dtype=F32),
             shape(BLOCK, TILE, dtype=F32),
             shape(BLOCK, TILE, dtype=F32),
@@ -632,27 +735,37 @@
         cost_estimate=cost(4 * BLOCK * rows * width, 4 * 2**20),
         name="sort_low",
     )(arrived, codes)
-    low_other = swap(low)
-
-    queries, own_out, own_lse, places, early = pl.pallas_call(
+    low_other, low_next_other = swap(low), swap(low_next)
+
+    values_shape = (heads * (DH + 16), BLOCK)
+    q_high, key_high, vt_high, places = pl.pallas_call(
+        first_kernel,
+        out_shape=[
+            shape(HALO, width),
+            shape(HALO, 2 * width),
+            shape(values_shape[0], HALO),
+            shape(rows, 128, dtype=F32),
+        ],
+        compiler_params=params,
+        cost_estimate=cost(4 * HALO * model_width * width, 2**20),
+        name="own_rows",
+    )(high, high_other, wq, wvt, meta)
+    queries, own_out, own_lse, early = pl.pallas_call(
         own_kernel,
         out_shape=[
             shape(BLOCK, width),
             shape(width, BLOCK),
             shape(8, BLOCK, dtype=F32),
-            shape(rows, 128, dtype=F32),
             shape(rows, width),
         ],
-        in_specs=[in_vmem] * 10,
-        out_specs=[in_vmem] * 5,
-        scratch_shapes=[
-            pltpu.VMEM((BLOCK, 2 * width), BF),
-            pltpu.VMEM((heads * (DH + 16), BLOCK), BF),
-        ],
+        scratch_shapes=[pltpu.VMEM((BLOCK, 2 * width), BF), pltpu.VMEM(values_shape, BF)],
         compiler_params=params,
         cost_estimate=cost(2**20, 2**20),
         name="own_block",
-    )(low, high, low_other, high_other, wq, wvt, label_row, label_col, flags, meta)
+    )(
+        low, low_next, low_other, low_next_other, q_high, key_high, vt_high, wq, wvt,
+        label_row, label_col, flags, places,
+    )
     halo, own_lse = lax.optimization_barrier((halo, own_lse))
 
     def finish(halo_mine, halo_other):
@@ -668,7 +781,7 @@
                 pltpu.VMEM((size, 2 * width), BF),
                 pltpu.VMEM((heads * (DH + 16), size), BF),
                 pltpu.VMEM((rows, width), BF),
-                pltpu.SemaphoreType.DMA((rows // STEP,)),
+                pltpu.SemaphoreType.DMA((rows // PIECE,)),
             ],
             compiler_params=params,
             name="prior_block",
@@ -686,7 +799,7 @@
             jnp.concatenate([swap(rest), halo_other], axis=0),
         )
 
-    back = lax.cond(wide[0, 0] > 0.0, lambda: more(low), lambda: finish(halo, halo_other))
+    back = lax.cond(wide[0, 0] > 0.0, lambda: more(jnp.concatenate([low, low_next], axis=0)), lambda: finish(halo, halo_other))
     returned = exchange(back)
     return pl.pallas_call(
         functools.partial(final_kernel, owners=owners),

time: 107 us -> 106 us (level)
  Pallas kernels: 29.7 us -> 27.9 us
  waiting for transfers between devices: 23.8 us -> 22.5 us
  blocking collectives: 33.2 us -> 34.3 us
    pallas_call x1, Pallas kernels: 11 us -> 8.9 us  [shards(): pl.pallas_call(own_kernel, out_shape=[shape(BLOCK, width), shape(width, B...]
    pallas_call x0 -> x1, Pallas kernels: none -> 1.5 us  [shards(): pl.pallas_call(first_kernel, out_shape=[shape(HALO, width), shape(HALO, 2...]
    ppermute x3 -> x4, waiting for transfers between devices: 2.05 us -> 0.82 us  [swap(): return lax.ppermute(x, 'round', [(0, 1), (1, 0)])]
    all_to_all x1, blocking collectives: 33.2 us -> 34.3 us  [exchange(): x = lax.all_to_all(x, AXES, split_axis=0, concat_axis=0, tiled=True)]
  transfers between devices with their start and end apart: 5 -> 6, of which waited for: 3 -> 3; matrix products, arithmetic and copies ran while one was open for 0% -> 0% of each run, Pallas kernels for 12% -> 13%
where the time goes in v5:
time: 106 us
  blocking collectives  34.3 us (32%)
  Pallas kernels  27.9 us (26%)
  waiting for transfers between devices  22.5 us (21%)
  starting transfers between devices  14 us (13%)
  local copies, waits for them, and re-layouts  6.1 us (6%)
    all_to_all x1, blocking collectives, exchange(): x = lax.all_to_all(x, AXES, split_axis=0, concat_axis=0, tiled=True)  34.3 us
    all_to_all x1, waiting for transfers between devices, exchange(): x = lax.all_to_all(x, AXES, split_axis=0, concat_axis=0, tiled=True)  21.7 us
    all_to_all x1, starting transfers between devices, exchange(): x = lax.all_to_all(x, AXES, split_axis=0, concat_axis=0, tiled=True)  11.5 us
    pallas_call x1, Pallas kernels, shards(): pl.pallas_call(own_kernel, out_shape=[shape(BLOCK, width), shape(width, B...  8.9 us
    unnamed x14, local copies, waits for them, and re-layouts  6.1 us
    pallas_call x1, Pallas kernels, finish(): pl.pallas_call(rest_kernel, out_shape=shape(rows, width), in_specs=[in_vm...  6.04 us
    pallas_call x1, Pallas kernels, shards(): pl.pallas_call(functools.partial(pack_kernel, owners=owners), out_shape=s...  3.73 us
    pallas_call x1, Pallas kernels, shards(): pl.pallas_call(functools.partial(final_kernel, owners=owners), out_shape=...  2.7 us
  transfers between devices with their start and end apart: 6, of which 3 were waited for; matrix products, arithmetic and copies ran while one was open for 0% of the time, Pallas kernels for 13%

profile of v5, /device:TPU:1, one launch (start us, length us, event | category | flops | bytes accessed | tf_op | source)
XLA Modules:
  0.0 105.6 jit_solution(5733700003756129622)
XLA Ops:
  0.0 3.7 %pack.1 = bf16[2048,512]{1,0:T(8,128)(2,1)} custom-call(bf16[256,1024]{1,0:T(8,128)(2,1)} %tok_hbm_ref.1, s32[2,256]{1,0:T(2,128)} %pos_ref.3, s32[1,1024]{1,0:T(1,128)} %label_ref.1), custom_call_target="tpu_custom_call" | custom-call | tf_op jit(solution)/shard_map/pack/pallas_call | solution.py:678
  3.7 0.0 copy-start.5
  3.7 11.5 %all-to-all-start = ((bf16[128,16,512]{2,1,0:T(8,128)(2,1)}), bf16[128,16,512]{2,1,0:T(8,128)(2,1)S(1)}, u32[]{:S(2)}, u32[]{:S(2)}) async-start(bf16[128,16,512]{2,1,0:T(8,128)(2,1)} %bitcast.8), calls=%async_computation | async-start | bytes 4194304 | tf_op jit(solution)/shard_map/all_to_all | solution.py:675
  15.3 0.0 copy-done.5
  15.3 0.0 copy-start
  15.3 1.6 %copy-done = bf16[1024,1024]{1,0:T(8,128)(2,1)S(1)} copy-done((bf16[1024,1024]{1,0:T(8,128)(2,1)S(1)}, bf16[1024,1024]{1,0:T(8,128)(2,1)}, u32[]{:S(2)}) %copy-start) | copy-done | bytes 2097176
  16.9 1.6 %copy-done.1 = bf16[1024,1024]{1,0:T(8,128)(2,1)S(1)} copy-done((bf16[1024,1024]{1,0:T(8,128)(2,1)S(1)}, bf16[1024,1024]{1,0:T(8,128)(2,1)}, u32[]{:S(2)}) %copy-start.1) | copy-done | bytes 2097176
  18.5 1.6 %copy-done.2 = bf16[1024,1024]{1,0:T(8,128)(2,1)S(1)} copy-done((bf16[1024,1024]{1,0:T(8,128)(2,1)S(1)}, bf16[1024,1024]{1,0:T(8,128)(2,1)}, u32[]{:S(2)}) %copy-start.2) | copy-done | bytes 2097176
  20.0 2.1 %prepare.1 = (bf16[1024,512]{1,0:T(8,128)(2,1)S(1)}, bf16[512,1024]{1,0:T(8,128)(2,1)}, bf16[1024,1024]{1,0:T(8,128)(2,1)S(1)}, f32[512,128]{1,0:T(8,128)S(1)}) custom-call(bf16[1024,1024]{1,0:T(8,128)(2,1)S(1)} %copy-done, bf16[1024,1024]{1,0:T(8,128)(2,1)S(1)} %copy-done.1, bf16[1024,1024]{1,0:T(8,128)(2,1)S(1)} %copy-done.2, s32[2,256]{1,0:T(2,128)S(1)} %copy-done.5), custom_call_target="tpu_custom_call" | custom-call | flops 1073741824 | bytes 8388608 | tf_op jit(solution)/shard_map/prepare/pallas_call | solution.py:694
  22.2 0.0 copy-start.3
  22.2 1.3 %copy-done.3 = bf16[1024,1024]{1,0:T(8,128)(2,1)} copy-done((bf16[1024,1024]{1,0:T(8,128)(2,1)}, bf16[1024,1024]{1,0:T(8,128)(2,1)S(1)}, u32[]{:S(2)}) %copy-start.3) | copy-done | bytes 2097176
  23.5 21.7 %all-to-all-done = bf16[128,16,512]{2,1,0:T(8,128)(2,1)S(1)} async-done(((bf16[128,16,512]{2,1,0:T(8,128)(2,1)}), bf16[128,16,512]{2,1,0:T(8,128)(2,1)S(1)}, u32[]{:S(2)}, u32[]{:S(2)}) %all-to-all-start) | async-done | bytes 2097184 | tf_op jit(solution)/shard_map/all_to_all | solution.py:675
  45.2 1.4 %sort_high.1 = (bf16[384,512]{1,0:T(8,128)(2,1)S(1)}, bf16[128,128]{1,0:T(8,128)(2,1)S(1)}, f32[16,128]{1,0:T(8,128)S(1)}, f32[1,1]{1,0:T(1,128)}) custom-call(bf16[2048,512]{1,0:T(8,128)(2,1)S(1)} %bitcast.5), custom_call_target="tpu_custom_call" | custom-call | tf_op jit(solution)/shard_map/sort_high/pallas_call | solution.py:711
  46.6 0.1 collective-permute-start.5
  46.7 1.1 %collective-permute-start.2 = (bf16[384,512]{1,0:T(8,128)(2,1)S(1)}, bf16[384,512]{1,0:T(8,128)(2,1)S(1)}, u32[]{:S(2)}, u32[]{:S(2)}) collective-permute-start(bf16[384,512]{1,0:T(8,128)(2,1)S(1)} %get-tuple-element.121.hm_ref), channel_id=1, source_target_pairs={{0,1},{1,2},{2,3},{3,7},{7,6},{6,5},{5,4},{4,12},{12,13},{13,14},{... | collective-permute-start | bytes 1179656 | tf_op jit(solution)/shard_map/ppermute | solution.py:671
  47.8 1.5 %sort_low.1 = (bf16[320,512]{1,0:T(8,128)(2,1)S(1)}, bf16[320,512]{1,0:T(8,128)(2,1)S(1)}, f32[1,1024]{1,0:T(1,128)S(1)}, f32[1024,128]{1,0:T(8,128)S(1)}, f32[1...) custom-call(bf16[2048,512]{1,0:T(8,128)(2,1)S(1)} %bitcast.6, f32[16,128]{1,0:T(8,128)S(1)} %get-tuple-element.122.code_ref), custom_call_target="tpu_custom_call" | custom-call | flops 4294967296 | bytes 4194304 | tf_op jit(solution)/shard_map/sort_low/pallas_call | solution.py:724
  49.3 0.8 collective-permute-start.3
  50.1 0.1 collective-permute-start.4
  50.2 0.0 collective-permute-done.5.ho_ref
  50.2 0.0 copy-done.6
  50.2 1.5 %own_rows.1 = (bf16[384,512]{1,0:T(8,128)(2,1)S(1)}, bf16[384,1024]{1,0:T(8,128)(2,1)S(1)}, bf16[576,384]{1,0:T(8,128)(2,1)S(1)}, f32[2048,128]{1,0:T(8,128)S(1)}) custom-call(bf16[384,512]{1,0:T(8,128)(2,1)S(1)} %get-tuple-element.121.hm_ref, bf16[384,512]{1,0:T(8,128)(2,1)S(1)} %collective-permute-done.5.ho_ref, ...), custom_call_target="tpu_custom_call" | custom-call | flops 805306368 | bytes 1048576 | tf_op jit(solution)/shard_map/own_rows/pallas_call | solution.py:741
  51.7 0.0 collective-permute-done.3.lo_ref
  51.7 0.1 collective-permute-done.4.no_ref
  51.8 8.9 %own_block.1 = (bf16[1024,512]{1,0:T(8,128)(2,1)S(1)}, bf16[512,1024]{1,0:T(8,128)(2,1)S(1)}, f32[8,1024]{1,0:T(8,128)S(1)}, bf16[2048,512]{1,0:T(8,128)(2,1)S(1)}) custom-call(bf16[320,512]{1,0:T(8,128)(2,1)S(1)} %get-tuple-element.123.lm_ref, bf16[320,512]{1,0:T(8,128)(2,1)S(1)} %get-tuple-element.124.nm_ref, ...), custom_call_target="tpu_custom_call" | custom-call | flops 1048576 | bytes 1048576 | tf_op jit(solution)/shard_map/own_block/pallas_call | solution.py:753
  60.7 0.0 collective-permute-done.2
  60.7 0.4 collective-permute-start.6
  61.8 0.7 collective-permute-done.6
  62.5 6.0 %conditional.1 = (bf16[2048,512]{1,0:T(8,128)(2,1)}) conditional(s32[]{:T(128)} %bitcast.2, (bf16[384,512]{1,0:T(8,128)(2,1)S(1)}, bf16[384,512]{1,0:T(8,128)(2,1)S(1)}, bf16[1024,512]{1,0:T(8,128)(2,1)S(1)}, bf16[512,1024]{1,0:T(8,128)(2,1)S(1)}, f32[1,1024]{1,0:T(1,128)S(1)}, /*index=5*/f32[1024,128]{1,0:T(8,128)S(1)}, f32[8,128]{1,0:T(8,128)S(1)}, ...), branch_computations={%region_0.0_spmd, %region_1.0_spmd} | conditional | flops 5505024 | bytes 15466668 | solution.py:802
  62.5 6.0 %prior_block.2 = bf16[2048,512]{1,0:T(8,128)(2,1)} custom-call(bf16[384,512]{1,0:T(8,128)(2,1)S(1)} %get-tuple-element.60.xm_ref, bf16[384,512]{1,0:T(8,128)(2,1)S(1)} %get-tuple-element.61.xo_ref, bf16[1024,512]{1,0:T(8,128)(2,1)S(1)} %get-tuple-element.62.wq_ref, bf16[512,1024]{1,0:T(8,128)(2,1)S(1)} %get-tuple-element.63.wvt_ref, ...), custom_call_target="tpu_custom_call" | custom-call | tf_op jit(solution)/shard_map/cond/branch_0_fun/prior_block/pallas_call | solution.py:773
  68.6 0.0 copy-start.4
  68.6 34.3 %all_to_all.10 = bf16[128,16,512]{2,1,0:T(8,128)(2,1)S(1)} all-to-all(bf16[128,16,512]{2,1,0:T(8,128)(2,1)} %bitcast.9), channel_id=1, replica_groups=mesh['round'=2,'head'=2,'seq'=32] {'round','head','seq'}, dimensions={0} | all-to-all | bytes 4194304 | tf_op jit(solution)/shard_map/all_to_all | solution.py:675
  102.9 2.7 %combine.1 = bf16[256,1024]{1,0:T(8,128)(2,1)} custom-call(bf16[2048,512]{1,0:T(8,128)(2,1)S(1)} %bitcast.7, f32[512,128]{1,0:T(8,128)S(1)} %get-tuple-element.142.slot_ref, bf16[1024,1024]{1,0:T(8,128)(2,1)S(1)} %copy-done.4), custom_call_target="tpu_custom_call" | custom-call | tf_op jit(solution)/shard_map/combine/pallas_call | solution.py:804
  (4 shorter events, 0.0 us)
Async XLA Ops:
  3.7 11.5 %copy-start.5 = (s32[2,256]{1,0:T(2,128)S(1)}, s32[2,256]{1,0:T(2,128)}, u32[]{:S(2)}) copy-start(s32[2,256]{1,0:T(2,128)} %pos_ref.3) | copy-start | bytes 6148
  3.7 41.5 %all-to-all-start = ((bf16[128,16,512]{2,1,0:T(8,128)(2,1)}), bf16[128,16,512]{2,1,0:T(8,128)(2,1)S(1)}, u32[]{:S(2)}, u32[]{:S(2)}) async-start(bf16[128,16,512]{2,1,0:T(8,128)(2,1)} %bitcast.8), calls=%async_computation | async-start | bytes 4194304 | tf_op jit(solution)/shard_map/all_to_all | solution.py:675
  15.3 1.6 %copy-start = (bf16[1024,1024]{1,0:T(8,128)(2,1)S(1)}, bf16[1024,1024]{1,0:T(8,128)(2,1)}, u32[]{:S(2)}) copy-start(bf16[1024,1024]{1,0:T(8,128)(2,1)} %wqk_ref.1) | copy-start | bytes 6291460
  16.9 1.6 %copy-start.1 = (bf16[1024,1024]{1,0:T(8,128)(2,1)S(1)}, bf16[1024,1024]{1,0:T(8,128)(2,1)}, u32[]{:S(2)}) copy-start(bf16[1024,1024]{1,0:T(8,128)(2,1)} %wv_ref.1) | copy-start | bytes 6291460
  18.5 1.6 %copy-start.2 = (bf16[1024,1024]{1,0:T(8,128)(2,1)S(1)}, bf16[1024,1024]{1,0:T(8,128)(2,1)}, u32[]{:S(2)}) copy-start(bf16[1024,1024]{1,0:T(8,128)(2,1)} %wo_ref.1) | copy-start | bytes 6291460
  22.2 1.3 %copy-start.3 = (bf16[1024,1024]{1,0:T(8,128)(2,1)}, bf16[1024,1024]{1,0:T(8,128)(2,1)S(1)}, u32[]{:S(2)}) copy-start(bf16[1024,1024]{1,0:T(8,128)(2,1)S(1)} %get-tuple-element.143.w_ref) | copy-start | bytes 6291460
  46.6 3.6 %collective-permute-start.5 = (bf16[384,512]{1,0:T(8,128)(2,1)S(1)}, bf16[384,512]{1,0:T(8,128)(2,1)S(1)}, u32[]{:S(2)}, u32[]{:S(2)}) collective-permute-start(bf16[384,512]{1,0:T(8,128)(2,1)S(1)} %get-tuple-element.121.hm_ref), channel_id=1, source_target_pairs={{0,64},{64,0},{1,65},{65,1},{2,66},{66,2},{3,67},{67,3},{4,68},{68... | collective-permute-start | bytes 1179656 | tf_op jit(solution)/shard_map/ppermute | solution.py:667
  46.7 14.0 %collective-permute-start.2 = (bf16[384,512]{1,0:T(8,128)(2,1)S(1)}, bf16[384,512]{1,0:T(8,128)(2,1)S(1)}, u32[]{:S(2)}, u32[]{:S(2)}) collective-permute-start(bf16[384,512]{1,0:T(8,128)(2,1)S(1)} %get-tuple-element.121.hm_ref), channel_id=1, source_target_pairs={{0,1},{1,2},{2,3},{3,7},{7,6},{6,5},{5,4},{4,12},{12,13},{13,14},{... | collective-permute-start | bytes 1179656 | tf_op jit(solution)/shard_map/ppermute | solution.py:671
  47.8 2.4 %copy-start.6 = (bf16[512,1024]{1,0:T(8,128)(2,1)S(1)}, bf16[512,1024]{1,0:T(8,128)(2,1)}, u32[]{:S(2)}) copy-start(bf16[512,1024]{1,0:T(8,128)(2,1)} %get-tuple-element.126.wvt_ref) | copy-start | bytes 3145732
  49.3 2.4 %collective-permute-start.3 = (bf16[320,512]{1,0:T(8,128)(2,1)S(1)}, bf16[320,512]{1,0:T(8,128)(2,1)S(1)}, u32[]{:S(2)}, u32[]{:S(2)}) collective-permute-start(bf16[320,512]{1,0:T(8,128)(2,1)S(1)} %get-tuple-element.123.lm_ref), channel_id=1, source_target_pairs={{0,64},{64,0},{1,65},{65,1},{2,66},{66,2},{3,67},{67,3},{4,68},{68... | collective-permute-start | bytes 983048 | tf_op jit(solution)/shard_map/ppermute | solution.py:667
  50.1 1.7 %collective-permute-start.4 = (bf16[320,512]{1,0:T(8,128)(2,1)S(1)}, bf16[320,512]{1,0:T(8,128)(2,1)S(1)}, u32[]{:S(2)}, u32[]{:S(2)}) collective-permute-start(bf16[320,512]{1,0:T(8,128)(2,1)S(1)} %get-tuple-element.124.nm_ref), channel_id=1, source_target_pairs={{0,64},{64,0},{1,65},{65,1},{2,66},{66,2},{3,67},{67,3},{4,68},{68... | collective-permute-start | bytes 983048 | tf_op jit(solution)/shard_map/ppermute | solution.py:667
  60.7 1.8 %collective-permute-start.6 = (bf16[384,512]{1,0:T(8,128)(2,1)S(1)}, bf16[384,512]{1,0:T(8,128)(2,1)S(1)}, u32[]{:S(2)}, u32[]{:S(2)}) collective-permute-start(bf16[384,512]{1,0:T(8,128)(2,1)S(1)} %collective-permute-done.2), channel_id=1, source_target_pairs={{0,64},{64,0},{1,65},{65,1},{2,66},{66,2},{3,67},{67,3},{4,68},{68... | collective-permute-start | bytes 1179656 | tf_op jit(solution)/shard_map/ppermute | solution.py:667
  68.6 34.3 %copy-start.4 = (bf16[1024,1024]{1,0:T(8,128)(2,1)S(1)}, bf16[1024,1024]{1,0:T(8,128)(2,1)}, u32[]{:S(2)}) copy-start(bf16[1024,1024]{1,0:T(8,128)(2,1)} %copy-done.3) | copy-start | bytes 6291460

commit v6 on v5

--- a/solution.py
+++ b/solution.py
@@ -76,19 +76,27 @@
 
 
 def pack_kernel(
-    tok_hbm_ref, pos_ref, label_ref, out_ref, tok_ref, buf_ref, in_sem, sem_ref, *, owners
+    tok_hbm_ref, pos_hbm_ref, label_hbm_ref, out_ref,
+    tok_ref, pos_ref, label_ref, buf_ref, in_sem, sem_ref, *, owners,
 ):
     count = tok_ref.shape[0]
     width = out_ref.shape[1]
     rows = owners * SLOTS
     half = BLOCK // 2
+    small = [
+        pltpu.make_async_copy(pos_hbm_ref, pos_ref, in_sem.at[2]),
+        pltpu.make_async_copy(label_hbm_ref, label_ref, in_sem.at[3]),
+    ]
     loads = []
     for a in range(2):
         cols = pl.ds(a * width, width)
         loads.append(
             pltpu.make_async_copy(tok_hbm_ref.at[:, cols], tok_ref.at[:, cols], in_sem.at[a])
         )
-        loads[-1].start()
+    for load in small + loads:
+        load.start()
+    for load in small:
+        load.wait()
     first, last = label_ref[0:1, 0:1], label_ref[0:1, BLOCK - 1 : BLOCK]
     wide = []
     for held in (HALO, half):
@@ -100,13 +108,13 @@
     core, head, seq = (lax.axis_index(axis) for axis in AXES)
     label = jnp.where(head == 0, label[:, :half], label[:, half:])
     label = jnp.broadcast_to(label, (SLOTS, half))
-    picks, extras = [], []
+    copies = []
     for r in range(2):
         pos = pos_ref[r : r + 1, :]
         hot, slot = slots_of(pos, owners)
         rank = slot & (SLOTS - 1)
         within = pos & (BLOCK - 1)
-        picks.append(mask(iota((rows, count), 0) == slot))
+        pick = mask(iota((rows, count), 0) == slot)
         value = iota((128, count), 0)
         code = jnp.where((value & 1) == 0, (within >> 5) + 1, within & 31)
         code = jnp.where((value >> 1) == rank, code, 0).astype(F32).astype(BF)
@@ -115,14 +123,13 @@
         places = jnp.where(lane == 2 * SLOTS, wide[0], places)
         places = jnp.where(lane == 2 * SLOTS + 1, wide[1], places).astype(BF)
         at_meta = mask(iota((rows, owners), 0) == iota((rows, owners), 1) * SLOTS + META)
-        extras.append(mm(at_meta, places))
-    copies = []
-    for a in range(2):
-        loads[a].wait()
-        for r in range(2):
+        extra = mm(at_meta, places)
+        for a in range(2):
+            if r == 0:
+                loads[a].wait()
             at = (a * 2 + r) * rows
-            body = mm(picks[r], tok_ref[:, a * width : (a + 1) * width])
-            buf_ref[at : at + rows, 0:128] = (body[:, 0:128] + extras[r]).astype(BF)
+            body = mm(pick, tok_ref[:, a * width : (a + 1) * width])
+            buf_ref[at : at + rows, 0:128] = (body[:, 0:128] + extra).astype(BF)
             buf_ref[at : at + rows, 128:width] = body[:, 128:].astype(BF)
 
             @pl.when(core == r)
@@ -250,7 +257,9 @@
 
 
 def window(i):
-    return max(i * SPAN - TILE, 0), min((i + 1) * SPAN + TILE, BLOCK)
+    start = i * SPAN - TILE * (1 + (i == 1))
+    stop = (i + 1) * SPAN + TILE * (1 + (i == SPANS - 2))
+    return max(start, 0), min(stop, BLOCK)
 
 
 def plan(own, prior):
@@ -603,7 +612,7 @@
         sending(t).wait()
 
 
-def final_kernel(x_ref, slot_ref, w_ref, out_ref, *, owners):
+def final_kernel(x_ref, slot_ref, w_ref, out_ref, buf_ref, sem_ref, *, owners):
     count = out_ref.shape[0]
     width = x_ref.shape[1]
     rows = owners * SLOTS
@@ -629,7 +638,7 @@
     v = iota((256, width), 0)
     select = jnp.where(((v & 7) >> 1) == (iota((256, width), 1) >> 7), 1.0, 0.0)
     select = jnp.where(v < 128, -select, select).astype(BF)
-    total = None
+    combined = []
     for a in range(2):
         values = [
             mm(picks[r], x_ref[(a * 2 + r) * rows : (a * 2 + r + 1) * rows, :]) for r in range(2)
@@ -639,10 +648,18 @@
         large = 1.0 / (1.0 + small)
         second = jnp.where(apart < 0.0, small * large, large)
         first = jnp.where(apart < 0.0, large, small * large)
-        combined = (first * values[0] + second * values[1]).astype(BF)
-        part = mm(combined, w_ref[a * width : (a + 1) * width, :])
-        total = part if total is None else total + part
-    out_ref[...] = total.astype(BF)
+        combined.append((first * values[0] + second * values[1]).astype(BF))
+    combined = jnp.concatenate(combined, axis=1)
+    copies = []
+    for part in range(2):
+        cols = pl.ds(part * width, width)
+        buf_ref[:, cols] = mm(combined, w_ref[:, cols]).astype(BF)
+        copies.append(
+            pltpu.make_async_copy(buf_ref.at[:, cols], out_ref.at[:, cols], sem_ref.at[part])
+        )
+        copies[-1].start()
+    for copy in copies:
+        copy.wait()
 
 
 def shards(tokens, w_qk, w_v, w_out, positions, buckets):
@@ -678,12 +695,14 @@
     packed = pl.pallas_call(
         functools.partial(pack_kernel, owners=owners),
         out_shape=shape(rows, width),
-        in_specs=[in_hbm, in_vmem, in_vmem],
+        in_specs=[in_hbm] * 3,
         out_specs=in_hbm,
         scratch_shapes=[
             pltpu.VMEM((tok_dev, model_width), BF),
+            pltpu.VMEM(positions.shape, I32),
+            pltpu.VMEM(buckets.shape, I32),
             pltpu.VMEM((rows, width), BF),
-            pltpu.SemaphoreType.DMA((2,)),
+            pltpu.SemaphoreType.DMA((4,)),
             pltpu.SemaphoreType.DMA((4,)),
         ],
         compiler_params=alone,
@@ -804,6 +823,11 @@
     return pl.pallas_call(
         functools.partial(final_kernel, owners=owners),
         out_shape=shape(tok_dev, model_width),
+        out_specs=in_hbm,
+        scratch_shapes=[
+            pltpu.VMEM((tok_dev, model_width), BF),
+            pltpu.SemaphoreType.DMA((2,)),
+        ],
         compiler_params=params,
         name="combine",
     )(returned, slots, wout)

time: 106 us -> 106 us (level)
  no operation moved by 1% of the time
where the time goes in v6:
time: 106 us; the launch traced here: 105 us
  blocking collectives  34.5 us (33%)
  Pallas kernels  27.2 us (26%)
  waiting for transfers between devices  22.5 us (21%)
  starting transfers between devices  14 us (13%)
  local copies, waits for them, and re-layouts  6.1 us (6%)
    all_to_all x1, blocking collectives, exchange(): x = lax.all_to_all(x, AXES, split_axis=0, concat_axis=0, tiled=True)  34.5 us
    all_to_all x1, waiting for transfers between devices, exchange(): x = lax.all_to_all(x, AXES, split_axis=0, concat_axis=0, tiled=True)  21.7 us
    all_to_all x1, starting transfers between devices, exchange(): x = lax.all_to_all(x, AXES, split_axis=0, concat_axis=0, tiled=True)  11.5 us
    pallas_call x1, Pallas kernels, shards(): pl.pallas_call(own_kernel, out_shape=[shape(BLOCK, width), shape(width, B...  8.41 us
    unnamed x14, local copies, waits for them, and re-layouts  6.1 us
    pallas_call x1, Pallas kernels, finish(): pl.pallas_call(rest_kernel, out_shape=shape(rows, width), in_specs=[in_vm...  6.04 us
    pallas_call x1, Pallas kernels, shards(): pl.pallas_call(functools.partial(pack_kernel, owners=owners), out_shape=s...  3.67 us
    pallas_call x1, Pallas kernels, shards(): pl.pallas_call(functools.partial(final_kernel, owners=owners), out_shape=...  2.55 us
  transfers between devices with their start and end apart: 6, of which 3 were waited for; matrix products, arithmetic and copies ran while one was open for 0% of the time, Pallas kernels for 13%

profile of v6, /device:TPU:1, one launch (start us, length us, event | category | flops | bytes accessed | tf_op | source)
XLA Modules:
  0.0 105.2 jit_solution(9707203531543012238)
XLA Ops:
  0.0 3.7 %pack.1 = bf16[2048,512]{1,0:T(8,128)(2,1)} custom-call(bf16[256,1024]{1,0:T(8,128)(2,1)} %tok_hbm_ref.1, s32[2,256]{1,0:T(2,128)} %pos_ref.1, s32[1,1024]{1,0:T(1,128)} %label_hbm_ref.1), custom_call_target="tpu_custom_call" | custom-call | tf_op jit(solution)/shard_map/pack/pallas_call | solution.py:695
  3.7 0.0 copy-start.5
  3.7 11.5 %all-to-all-start = ((bf16[128,16,512]{2,1,0:T(8,128)(2,1)}), bf16[128,16,512]{2,1,0:T(8,128)(2,1)S(1)}, u32[]{:S(2)}, u32[]{:S(2)}) async-start(bf16[128,16,512]{2,1,0:T(8,128)(2,1)} %bitcast.8), calls=%async_computation | async-start | bytes 4194304 | tf_op jit(solution)/shard_map/all_to_all | solution.py:692
  15.2 0.0 copy-done.5
  15.2 0.0 copy-start
  15.2 1.6 %copy-done = bf16[1024,1024]{1,0:T(8,128)(2,1)S(1)} copy-done((bf16[1024,1024]{1,0:T(8,128)(2,1)S(1)}, bf16[1024,1024]{1,0:T(8,128)(2,1)}, u32[]{:S(2)}) %copy-start) | copy-done | bytes 2097176
  16.8 1.6 %copy-done.1 = bf16[1024,1024]{1,0:T(8,128)(2,1)S(1)} copy-done((bf16[1024,1024]{1,0:T(8,128)(2,1)S(1)}, bf16[1024,1024]{1,0:T(8,128)(2,1)}, u32[]{:S(2)}) %copy-start.1) | copy-done | bytes 2097176
  18.4 1.6 %copy-done.2 = bf16[1024,1024]{1,0:T(8,128)(2,1)S(1)} copy-done((bf16[1024,1024]{1,0:T(8,128)(2,1)S(1)}, bf16[1024,1024]{1,0:T(8,128)(2,1)}, u32[]{:S(2)}) %copy-start.2) | copy-done | bytes 2097176
  20.0 2.1 %prepare.1 = (bf16[1024,512]{1,0:T(8,128)(2,1)S(1)}, bf16[512,1024]{1,0:T(8,128)(2,1)}, bf16[1024,1024]{1,0:T(8,128)(2,1)S(1)}, f32[512,128]{1,0:T(8,128)S(1)}) custom-call(bf16[1024,1024]{1,0:T(8,128)(2,1)S(1)} %copy-done, bf16[1024,1024]{1,0:T(8,128)(2,1)S(1)} %copy-done.1, bf16[1024,1024]{1,0:T(8,128)(2,1)S(1)} %copy-done.2, s32[2,256]{1,0:T(2,128)S(1)} %copy-done.5), custom_call_target="tpu_custom_call" | custom-call | flops 1073741824 | bytes 8388608 | tf_op jit(solution)/shard_map/prepare/pallas_call | solution.py:713
  22.1 0.0 copy-start.3
  22.1 1.3 %copy-done.3 = bf16[1024,1024]{1,0:T(8,128)(2,1)} copy-done((bf16[1024,1024]{1,0:T(8,128)(2,1)}, bf16[1024,1024]{1,0:T(8,128)(2,1)S(1)}, u32[]{:S(2)}) %copy-start.3) | copy-done | bytes 2097176
  23.4 21.7 %all-to-all-done = bf16[128,16,512]{2,1,0:T(8,128)(2,1)S(1)} async-done(((bf16[128,16,512]{2,1,0:T(8,128)(2,1)}), bf16[128,16,512]{2,1,0:T(8,128)(2,1)S(1)}, u32[]{:S(2)}, u32[]{:S(2)}) %all-to-all-start) | async-done | bytes 2097184 | tf_op jit(solution)/shard_map/all_to_all | solution.py:692
  45.2 1.4 %sort_high.1 = (bf16[384,512]{1,0:T(8,128)(2,1)S(1)}, bf16[128,128]{1,0:T(8,128)(2,1)S(1)}, f32[16,128]{1,0:T(8,128)S(1)}, f32[1,1]{1,0:T(1,128)}) custom-call(bf16[2048,512]{1,0:T(8,128)(2,1)S(1)} %bitcast.5), custom_call_target="tpu_custom_call" | custom-call | tf_op jit(solution)/shard_map/sort_high/pallas_call | solution.py:730
  46.5 0.1 collective-permute-start.5
  46.6 1.1 %collective-permute-start.2 = (bf16[384,512]{1,0:T(8,128)(2,1)S(1)}, bf16[384,512]{1,0:T(8,128)(2,1)S(1)}, u32[]{:S(2)}, u32[]{:S(2)}) collective-permute-start(bf16[384,512]{1,0:T(8,128)(2,1)S(1)} %get-tuple-element.121.hm_ref), channel_id=1, source_target_pairs={{0,1},{1,2},{2,3},{3,7},{7,6},{6,5},{5,4},{4,12},{12,13},{13,14},{... | collective-permute-start | bytes 1179656 | tf_op jit(solution)/shard_map/ppermute | solution.py:688
  47.7 1.5 %sort_low.1 = (bf16[320,512]{1,0:T(8,128)(2,1)S(1)}, bf16[320,512]{1,0:T(8,128)(2,1)S(1)}, f32[1,1024]{1,0:T(1,128)S(1)}, f32[1024,128]{1,0:T(8,128)S(1)}, f32[1...) custom-call(bf16[2048,512]{1,0:T(8,128)(2,1)S(1)} %bitcast.6, f32[16,128]{1,0:T(8,128)S(1)} %get-tuple-element.122.code_ref), custom_call_target="tpu_custom_call" | custom-call | flops 4294967296 | bytes 4194304 | tf_op jit(solution)/shard_map/sort_low/pallas_call | solution.py:743
  49.2 0.8 collective-permute-start.3
  50.0 0.1 collective-permute-start.4
  50.1 0.0 collective-permute-done.5.ho_ref
  50.1 0.0 copy-done.6
  50.1 1.5 %own_rows.1 = (bf16[384,512]{1,0:T(8,128)(2,1)S(1)}, bf16[384,1024]{1,0:T(8,128)(2,1)S(1)}, bf16[576,384]{1,0:T(8,128)(2,1)S(1)}, f32[2048,128]{1,0:T(8,128)S(1)}) custom-call(bf16[384,512]{1,0:T(8,128)(2,1)S(1)} %get-tuple-element.121.hm_ref, bf16[384,512]{1,0:T(8,128)(2,1)S(1)} %collective-permute-done.5.ho_ref, ...), custom_call_target="tpu_custom_call" | custom-call | flops 805306368 | bytes 1048576 | tf_op jit(solution)/shard_map/own_rows/pallas_call | solution.py:760
  51.6 0.0 collective-permute-done.3.lo_ref
  51.6 0.1 collective-permute-done.4.no_ref
  51.7 8.4 %own_block.1 = (bf16[1024,512]{1,0:T(8,128)(2,1)S(1)}, bf16[512,1024]{1,0:T(8,128)(2,1)S(1)}, f32[8,1024]{1,0:T(8,128)S(1)}, bf16[2048,512]{1,0:T(8,128)(2,1)S(1)}) custom-call(bf16[320,512]{1,0:T(8,128)(2,1)S(1)} %get-tuple-element.123.lm_ref, bf16[320,512]{1,0:T(8,128)(2,1)S(1)} %get-tuple-element.124.nm_ref, ...), custom_call_target="tpu_custom_call" | custom-call | flops 1048576 | bytes 1048576 | tf_op jit(solution)/shard_map/own_block/pallas_call | solution.py:772
  60.2 0.0 collective-permute-done.2
  60.2 0.5 collective-permute-start.6
  61.3 0.7 collective-permute-done.6
  62.0 6.0 %conditional.1 = (bf16[2048,512]{1,0:T(8,128)(2,1)}) conditional(s32[]{:T(128)} %bitcast.2, (bf16[384,512]{1,0:T(8,128)(2,1)S(1)}, bf16[384,512]{1,0:T(8,128)(2,1)S(1)}, bf16[1024,512]{1,0:T(8,128)(2,1)S(1)}, bf16[512,1024]{1,0:T(8,128)(2,1)S(1)}, f32[1,1024]{1,0:T(1,128)S(1)}, /*index=5*/f32[1024,128]{1,0:T(8,128)S(1)}, f32[8,128]{1,0:T(8,128)S(1)}, ...), branch_computations={%region_0.0_spmd, %region_1.0_spmd} | conditional | flops 5505024 | bytes 15466668 | solution.py:821
  62.0 6.0 %prior_block.2 = bf16[2048,512]{1,0:T(8,128)(2,1)} custom-call(bf16[384,512]{1,0:T(8,128)(2,1)S(1)} %get-tuple-element.60.xm_ref, bf16[384,512]{1,0:T(8,128)(2,1)S(1)} %get-tuple-element.61.xo_ref, bf16[1024,512]{1,0:T(8,128)(2,1)S(1)} %get-tuple-element.62.wq_ref, bf16[512,1024]{1,0:T(8,128)(2,1)S(1)} %get-tuple-element.63.wvt_ref, ...), custom_call_target="tpu_custom_call" | custom-call | tf_op jit(solution)/shard_map/cond/branch_0_fun/prior_block/pallas_call | solution.py:792
  68.0 0.0 copy-start.4
  68.0 34.5 %all_to_all.10 = bf16[128,16,512]{2,1,0:T(8,128)(2,1)S(1)} all-to-all(bf16[128,16,512]{2,1,0:T(8,128)(2,1)} %bitcast.9), channel_id=1, replica_groups=mesh['round'=2,'head'=2,'seq'=32] {'round','head','seq'}, dimensions={0} | all-to-all | bytes 4194304 | tf_op jit(solution)/shard_map/all_to_all | solution.py:692
  102.5 2.5 %combine.1 = bf16[256,1024]{1,0:T(8,128)(2,1)} custom-call(bf16[2048,512]{1,0:T(8,128)(2,1)S(1)} %bitcast.7, f32[512,128]{1,0:T(8,128)S(1)} %get-tuple-element.142.slot_ref, bf16[1024,1024]{1,0:T(8,128)(2,1)S(1)} %copy-done.4), custom_call_target="tpu_custom_call" | custom-call | tf_op jit(solution)/shard_map/combine/pallas_call | solution.py:823
  (4 shorter events, 0.0 us)
Async XLA Ops:
  3.7 11.5 %copy-start.5 = (s32[2,256]{1,0:T(2,128)S(1)}, s32[2,256]{1,0:T(2,128)}, u32[]{:S(2)}) copy-start(s32[2,256]{1,0:T(2,128)} %pos_ref.1) | copy-start | bytes 6148
  3.7 41.5 %all-to-all-start = ((bf16[128,16,512]{2,1,0:T(8,128)(2,1)}), bf16[128,16,512]{2,1,0:T(8,128)(2,1)S(1)}, u32[]{:S(2)}, u32[]{:S(2)}) async-start(bf16[128,16,512]{2,1,0:T(8,128)(2,1)} %bitcast.8), calls=%async_computation | async-start | bytes 4194304 | tf_op jit(solution)/shard_map/all_to_all | solution.py:692
  15.2 1.6 %copy-start = (bf16[1024,1024]{1,0:T(8,128)(2,1)S(1)}, bf16[1024,1024]{1,0:T(8,128)(2,1)}, u32[]{:S(2)}) copy-start(bf16[1024,1024]{1,0:T(8,128)(2,1)} %wqk_ref.1) | copy-start | bytes 6291460
  16.8 1.6 %copy-start.1 = (bf16[1024,1024]{1,0:T(8,128)(2,1)S(1)}, bf16[1024,1024]{1,0:T(8,128)(2,1)}, u32[]{:S(2)}) copy-start(bf16[1024,1024]{1,0:T(8,128)(2,1)} %wv_ref.1) | copy-start | bytes 6291460
  18.4 1.6 %copy-start.2 = (bf16[1024,1024]{1,0:T(8,128)(2,1)S(1)}, bf16[1024,1024]{1,0:T(8,128)(2,1)}, u32[]{:S(2)}) copy-start(bf16[1024,1024]{1,0:T(8,128)(2,1)} %wo_ref.1) | copy-start | bytes 6291460
  22.1 1.3 %copy-start.3 = (bf16[1024,1024]{1,0:T(8,128)(2,1)}, bf16[1024,1024]{1,0:T(8,128)(2,1)S(1)}, u32[]{:S(2)}) copy-start(bf16[1024,1024]{1,0:T(8,128)(2,1)S(1)} %get-tuple-element.143.w_ref) | copy-start | bytes 6291460
  46.5 3.6 %collective-permute-start.5 = (bf16[384,512]{1,0:T(8,128)(2,1)S(1)}, bf16[384,512]{1,0:T(8,128)(2,1)S(1)}, u32[]{:S(2)}, u32[]{:S(2)}) collective-permute-start(bf16[384,512]{1,0:T(8,128)(2,1)S(1)} %get-tuple-element.121.hm_ref), channel_id=1, source_target_pairs={{0,64},{64,0},{1,65},{65,1},{2,66},{66,2},{3,67},{67,3},{4,68},{68... | collective-permute-start | bytes 1179656 | tf_op jit(solution)/shard_map/ppermute | solution.py:684
  46.6 13.5 %collective-permute-start.2 = (bf16[384,512]{1,0:T(8,128)(2,1)S(1)}, bf16[384,512]{1,0:T(8,128)(2,1)S(1)}, u32[]{:S(2)}, u32[]{:S(2)}) collective-permute-start(bf16[384,512]{1,0:T(8,128)(2,1)S(1)} %get-tuple-element.121.hm_ref), channel_id=1, source_target_pairs={{0,1},{1,2},{2,3},{3,7},{7,6},{6,5},{5,4},{4,12},{12,13},{13,14},{... | collective-permute-start | bytes 1179656 | tf_op jit(solution)/shard_map/ppermute | solution.py:688
  47.7 2.4 %copy-start.6 = (bf16[512,1024]{1,0:T(8,128)(2,1)S(1)}, bf16[512,1024]{1,0:T(8,128)(2,1)}, u32[]{:S(2)}) copy-start(bf16[512,1024]{1,0:T(8,128)(2,1)} %get-tuple-element.126.wvt_ref) | copy-start | bytes 3145732
  49.2 2.4 %collective-permute-start.3 = (bf16[320,512]{1,0:T(8,128)(2,1)S(1)}, bf16[320,512]{1,0:T(8,128)(2,1)S(1)}, u32[]{:S(2)}, u32[]{:S(2)}) collective-permute-start(bf16[320,512]{1,0:T(8,128)(2,1)S(1)} %get-tuple-element.123.lm_ref), channel_id=1, source_target_pairs={{0,64},{64,0},{1,65},{65,1},{2,66},{66,2},{3,67},{67,3},{4,68},{68... | collective-permute-start | bytes 983048 | tf_op jit(solution)/shard_map/ppermute | solution.py:684
  50.0 1.7 %collective-permute-start.4 = (bf16[320,512]{1,0:T(8,128)(2,1)S(1)}, bf16[320,512]{1,0:T(8,128)(2,1)S(1)}, u32[]{:S(2)}, u32[]{:S(2)}) collective-permute-start(bf16[320,512]{1,0:T(8,128)(2,1)S(1)} %get-tuple-element.124.nm_ref), channel_id=1, source_target_pairs={{0,64},{64,0},{1,65},{65,1},{2,66},{66,2},{3,67},{67,3},{4,68},{68... | collective-permute-start | bytes 983048 | tf_op jit(solution)/shard_map/ppermute | solution.py:684
  60.2 1.8 %collective-permute-start.6 = (bf16[384,512]{1,0:T(8,128)(2,1)S(1)}, bf16[384,512]{1,0:T(8,128)(2,1)S(1)}, u32[]{:S(2)}, u32[]{:S(2)}) collective-permute-start(bf16[384,512]{1,0:T(8,128)(2,1)S(1)} %collective-permute-done.2), channel_id=1, source_target_pairs={{0,64},{64,0},{1,65},{65,1},{2,66},{66,2},{3,67},{67,3},{4,68},{68... | collective-permute-start | bytes 1179656 | tf_op jit(solution)/shard_map/ppermute | solution.py:684
  68.0 34.5 %copy-start.4 = (bf16[1024,1024]{1,0:T(8,128)(2,1)S(1)}, bf16[1024,1024]{1,0:T(8,128)(2,1)}, u32[]{:S(2)}) copy-start(bf16[1024,1024]{1,0:T(8,128)(2,1)} %copy-done.3) | copy-start | bytes 6291460
